TPU v7x, 32 devices: a whole 2x2x4 slice. The times are simulated.
32 devices in a mesh: seq: 16 (over z, y, x), opt: 2 (over core).
Axes of the slice: x: 2, y: 2, z: 4, core: 2. Of those that a mesh axis runs over, the one named last changes fastest.
Arguments:
- features: bfloat16 [2, 2048, 1536], P('opt', 'seq'), may hold values from -6 to 6
- tile_mask: int32 [2, 2048], P('opt', 'seq'), may hold values from 0 to 1, as said below
- lengths: int32 [2, 4], replicated, may hold values from 1 to 1024, 2048 in all within a row
- owners: int32 [768], replicated, may hold values from 0 to 767, each once
- layer_blocks: float32 [768, 96, 96], P(('seq', 'opt')), may hold values from -0.21875 to 0.21875
- stat_left: float32 [768, 96, 96], P(('seq', 'opt')), as said below
- stat_right: float32 [768, 96, 96], P(('seq', 'opt')), as said below
- io_weights: float32 [1536, 2, 768], P(('seq', 'opt')), may hold values from -0.21875 to 0.21875
- io_first: float32 [1536, 2, 768], P(('seq', 'opt')), may hold values from -0.00048828125 to 0.00048828125
- io_second: float32 [1536, 2, 768], P(('seq', 'opt')), may hold values from 5.5650915e-09 to 2.2218046e-08
- vectors: float32 [19, 768], replicated, may hold values from -3 to 3, as said below
- vec_first: float32 [19, 768], replicated, may hold values from -0.0017089844 to 0.0017089844
- vec_second: float32 [19, 768], replicated, may hold values from 5.2900113e-08 to 2.1160045e-07
Outputs:
- grad_norm: float32 [], replicated
- error_sum: float32 [], replicated
- masked_count: float32 [], replicated
- block_grads: float32 [768, 96, 96], P(('seq', 'opt'))
- left_new: float32 [768, 96, 96], P(('seq', 'opt'))
- right_new: float32 [768, 96, 96], P(('seq', 'opt'))
- blocks_new: float32 [768, 96, 96], P(('seq', 'opt'))
- io_first_new: float32 [1536, 2, 768], P(('seq', 'opt'))
- io_second_new: float32 [1536, 2, 768], P(('seq', 'opt'))
- io_new: float32 [1536, 2, 768], P(('seq', 'opt'))
- vec_first_new: float32 [19, 768], replicated
- vec_second_new: float32 [19, 768], replicated
- vec_new: float32 [19, 768], replicated
Inputs may be any that keep to these rules, and one draw needn't show every extreme that they name: `tile_mask`: 1 marks a masked tile. `lengths`: the 4 slides of a micro-batch in order fill all 2048 tiles; the longest has half of 2048 tiles. `owners`: each natural block in exactly one slot. `stat_left`: symmetric positive definite. `stat_right`: symmetric positive definite. `vectors`: gains positive.
All inputs are finite; a program needn't handle non-finite values.
Results may differ from a plain program's by a relative error of at most 0.0006.
The roundings to bfloat16 on the way count: a program that leaves them out, or rounds other values in their place, can miss the bound.
Values may be sent and summed in bfloat16 or wider, within the bound.
No kernel may reach another device: no remote copies, remote signals or barrier semaphores. Data moves between devices by JAX's collectives and lax.ppermute only.
A program may use at most 256 MiB of HBM per device.

v0:
```python
from functools import partial
import math

import jax
import jax.numpy as jnp
import numpy as np
from jax import lax
from jax.experimental import pallas as pl
from jax.experimental.pallas import tpu as pltpu
from jax.sharding import PartitionSpec as P

D = 768
HEADS = 16
HEAD_DIM = 48
FF = 3072
FEAT = 1536
LAYERS = 1
BRANCHES = 5
SEG0 = 1024
BLOCK = 96
SLIDES = 4
NEWTON = 6
STEP = 10


norm_eps = 1e-05
clip_limit = 1.0
beta_one = 0.9
beta_two = 0.95
adam_eps = 1e-08
rate_adam = 0.01
rate_vector = 0.2
weight_decay = 0.05
beta_stat = 0.95
rate_shampoo = 0.05
root_eps = 1e-12
masked_score = -1e30
highest = lax.Precision.HIGHEST


def from_partner(value, axis, stride):
    mask = 2**stride
    pairs = [(source, source ^ mask) for source in range(lax.axis_size(axis))]
    return lax.ppermute(value, axis, pairs)


def for_sending(shard):

    def short(part):
        return part.astype(jnp.bfloat16) if part.dtype == jnp.float32 else part

    return jax.tree.map(short, shard)


def layer_norm(values, gain, shift):
    centred = values - jnp.mean(values, axis=-1, keepdims=True)
    spread = jnp.mean(centred * centred, axis=-1, keepdims=True)
    return centred * lax.rsqrt(spread + norm_eps) * gain + shift


def sine_places(places):
    half_width = D // 2
    freq_rates = jnp.exp(
        jnp.arange(half_width, dtype=jnp.float32) * (-math.log(10000.0) / half_width)
    )
    angles = (places.astype(jnp.float32) / 64.0)[:, None] * freq_rates[None, :]
    return jnp.concatenate([jnp.sin(angles), jnp.cos(angles)], axis=1)


def slide_ids(lengths_row, places):
    slide_ends = jnp.cumsum(lengths_row)
    return jnp.sum((places[..., None] >= slide_ends[:-1]).astype(jnp.int32), axis=-1)


def slide_offsets(lengths_row, places):
    slide_ends = jnp.cumsum(lengths_row)
    slide_starts = slide_ends - lengths_row
    owner_ids = slide_ids(lengths_row, places)
    match_rows = owner_ids[:, None] == jnp.arange(SLIDES, dtype=jnp.int32)[None, :]
    picked = jnp.sum(jnp.where(match_rows, slide_starts[None, :], 0), axis=1)
    return places - picked


def head_offsets(dilation):
    return np.arange(HEADS) % dilation


def pick_rows(values, dilation):
    row_count = values.shape[0] // dilation
    shaped = values.reshape((row_count, dilation) + values.shape[1:])
    return shaped[:, head_offsets(dilation), np.arange(HEADS)]


def spread_rows(values, dilation, filler):
    row_count = values.shape[0]
    hit_mask = np.arange(dilation)[:, None] == head_offsets(dilation)[None, :]
    hit_mask = hit_mask.reshape((1, dilation, HEADS) + (1,) * (values.ndim - 2))
    spread_out = jnp.where(hit_mask, values[:, None], filler)
    return spread_out.reshape((row_count * dilation,) + values.shape[1:])


def branch_geom(branch, tok_dev, seq_len):
    dilation = 2**branch
    segment = min(SEG0 * dilation, seq_len)
    return (dilation, segment, max(1, segment // tok_dev))


def branch_docs(lengths_row, first_place, row_count, dilation):
    places = (
        first_place
        + jnp.asarray(head_offsets(dilation), jnp.int32)[None, :]
        + dilation * jnp.arange(row_count, dtype=jnp.int32)[:, None]
    )
    return slide_ids(lengths_row, places)


def contract_rows(left, right):
    return lax.dot_general(
        left, right, (((0,), (0,)), ((), ())), preferred_element_type=jnp.float32
    )


def contract_cols(left, right):
    return lax.dot_general(
        left, right, (((1,), (1,)), ((), ())), preferred_element_type=jnp.float32
    )


def assemble(natural):
    per_layer = natural.reshape(LAYERS, -1, BLOCK, BLOCK)
    col_count = (4 * D + FF) // BLOCK
    wide_count = D // BLOCK * col_count
    upper_mats = per_layer[:, :wide_count].reshape(LAYERS, D // BLOCK, col_count, BLOCK, BLOCK)
    upper_mats = upper_mats.transpose(0, 1, 3, 2, 4).reshape(LAYERS, D, 4 * D + FF)
    lower_mats = per_layer[:, wide_count:].reshape(LAYERS, FF // BLOCK, D // BLOCK, BLOCK, BLOCK)
    lower_mats = lower_mats.transpose(0, 1, 3, 2, 4).reshape(LAYERS, FF, D)
    return (upper_mats, lower_mats)


def disassemble(upper_mats, lower_mats):
    col_count = (4 * D + FF) // BLOCK
    top_part = upper_mats.reshape(LAYERS, D // BLOCK, BLOCK, col_count, BLOCK).transpose(
        0, 1, 3, 2, 4
    )
    top_part = top_part.reshape(LAYERS, -1, BLOCK, BLOCK)
    bottom_part = lower_mats.reshape(LAYERS, FF // BLOCK, BLOCK, D // BLOCK, BLOCK).transpose(
        0, 1, 3, 2, 4
    )
    bottom_part = bottom_part.reshape(LAYERS, -1, BLOCK, BLOCK)
    return jnp.concatenate([top_part, bottom_part], axis=1).reshape(-1, BLOCK, BLOCK)


def unpack(vector_set):
    per_layer = 8 + FF // D
    return (
        vector_set[: LAYERS * per_layer].reshape(LAYERS, per_layer, D),
        vector_set[LAYERS * per_layer :],
    )


def collect_pairs(pieces, bit_counts, seq_index):
    pieces = list(pieces)
    for bit_id in range(max(bit_counts + [0])):
        active_ids = [branch for branch in range(len(pieces)) if bit_counts[branch] > bit_id]
        outgoing = jnp.concatenate([pieces[branch] for branch in active_ids], axis=0)
        partner = from_partner(outgoing, "seq", bit_id)
        lower_side = seq_index // 2**bit_id % 2 == 0
        offset_at = 0
        for branch in active_ids:
            my_part = pieces[branch]
            part_size = my_part.shape[0]
            their_part = partner[offset_at : offset_at + part_size]
            offset_at = offset_at + part_size
            pieces[branch] = jnp.where(
                lower_side,
                jnp.concatenate([my_part, their_part], 0),
                jnp.concatenate([their_part, my_part], 0),
            )
    return pieces


def return_pairs(pieces, bit_counts, seq_index):
    pieces = list(pieces)
    for bit_id in reversed(range(max(bit_counts + [0]))):
        active_ids = [branch for branch in range(len(pieces)) if bit_counts[branch] > bit_id]
        lower_side = seq_index // 2**bit_id % 2 == 0
        kept_parts, sent_parts = ([], [])
        for branch in active_ids:
            half_size = pieces[branch].shape[0] // 2
            first_part = pieces[branch][:half_size]
            second_part = pieces[branch][half_size:]
            kept_parts.append(jnp.where(lower_side, first_part, second_part))
            sent_parts.append(jnp.where(lower_side, second_part, first_part))
        partner = from_partner(for_sending(jnp.concatenate(sent_parts, axis=0)), "seq", bit_id)
        offset_at = 0
        for branch, kept_part in zip(active_ids, kept_parts):
            part_size = kept_part.shape[0]
            pieces[branch] = kept_part + partner[offset_at : offset_at + part_size]
            offset_at = offset_at + part_size
    return pieces


def score_block(query_rows, key_rows, query_docs, key_docs):
    raw_scores = jnp.einsum(
        "sqhd,skhd->shqk", query_rows, key_rows, preferred_element_type=jnp.float32
    ) * HEAD_DIM ** (-0.5)
    same_slide = (
        jnp.transpose(query_docs, (0, 2, 1))[..., None]
        == jnp.transpose(key_docs, (0, 2, 1))[:, :, None, :]
    )
    return jnp.where(same_slide, raw_scores, masked_score)


def attend_forward(packed, lengths_row, seq_len, seq_index):
    tok_dev = packed.shape[0]
    triple = packed.reshape(tok_dev, 3, HEADS, HEAD_DIM)
    queries, key_all, value_all = (triple[:, 0], triple[:, 1], triple[:, 2])
    geoms = [branch_geom(branch, tok_dev, seq_len) for branch in range(BRANCHES)]
    local_pairs = [
        jnp.stack([pick_rows(key_all, geom[0]), pick_rows(value_all, geom[0])], axis=1).reshape(
            -1, 2 * D
        )
        for geom in geoms
    ]
    bit_counts = [geom[2].bit_length() - 1 for geom in geoms]
    joined = collect_pairs(local_pairs, bit_counts, seq_index)
    kept_state, outputs, totals_all = ([], [], [])
    for branch in range(BRANCHES):
        dilation, segment, group_size = geoms[branch]
        sections = max(1, tok_dev // segment)
        query_rows = pick_rows(queries, dilation).reshape(sections, -1, HEADS, HEAD_DIM)
        pair_rows = joined[branch].reshape(sections, -1, 2, HEADS, HEAD_DIM)
        key_rows = pair_rows[:, :, 0]
        value_rows = pair_rows[:, :, 1]
        query_docs = branch_docs(
            lengths_row, seq_index * tok_dev, tok_dev // dilation, dilation
        ).reshape(sections, -1, HEADS)
        group_first = seq_index // group_size * group_size * tok_dev
        key_docs = branch_docs(lengths_row, group_first, joined[branch].shape[0], dilation).reshape(
            sections, -1, HEADS
        )
        scores = score_block(query_rows, key_rows, query_docs, key_docs)
        totals = jax.nn.logsumexp(scores, axis=-1)
        softmax_rows = jnp.exp(scores - totals[..., None]).astype(jnp.bfloat16)
        output = jnp.einsum(
            "shqk,skhd->sqhd", softmax_rows, value_rows, preferred_element_type=jnp.float32
        ).reshape(-1, HEADS, HEAD_DIM)
        totals_rows = jnp.transpose(totals, (0, 2, 1)).reshape(-1, HEADS)
        kept_state.append(
            (query_rows, key_rows, value_rows, query_docs, key_docs, output, totals_rows)
        )
        outputs.append(spread_rows(output, dilation, 0.0))
        totals_all.append(spread_rows(totals_rows, dilation, masked_score))
    stacked = jnp.stack(totals_all)
    grand_total = jax.nn.logsumexp(stacked, axis=0)
    mixed_out = jnp.zeros_like(outputs[0])
    for branch in range(BRANCHES):
        mixed_out = mixed_out + jnp.exp(stacked[branch] - grand_total)[..., None] * outputs[branch]
    return (mixed_out, (mixed_out, grand_total, kept_state))


def attend_backward(grad_mixed, attention_state, seq_len, seq_index):
    mixed_out, grand_total, kept_state = attention_state
    tok_dev = grad_mixed.shape[0]
    score_scale = HEAD_DIM ** (-0.5)
    grad_query = jnp.zeros(grad_mixed.shape, jnp.float32)
    key_terms, bit_counts, dilations = ([], [], [])
    for branch in range(BRANCHES):
        dilation, segment, group_size = branch_geom(branch, tok_dev, seq_len)
        query_rows, key_rows, value_rows, query_docs, key_docs, output, totals_rows = kept_state[
            branch
        ]
        sections = query_rows.shape[0]
        weight = jnp.exp(totals_rows - pick_rows(grand_total, dilation))
        grad_picked = pick_rows(grad_mixed, dilation)
        grad_output = (
            (weight[..., None] * grad_picked)
            .astype(jnp.bfloat16)
            .reshape(sections, -1, HEADS, HEAD_DIM)
        )
        grad_totals = weight * jnp.sum(
            grad_picked * (output - pick_rows(mixed_out, dilation)), axis=-1
        )
        grad_totals = jnp.transpose(grad_totals.reshape(sections, -1, HEADS), (0, 2, 1))
        totals = jnp.transpose(totals_rows.reshape(sections, -1, HEADS), (0, 2, 1))
        softmax_rows = jnp.exp(
            score_block(query_rows, key_rows, query_docs, key_docs) - totals[..., None]
        )
        grad_value = jnp.einsum(
            "shqk,sqhd->skhd",
            softmax_rows.astype(jnp.bfloat16),
            grad_output,
            preferred_element_type=jnp.float32,
        )
        grad_probs = jnp.einsum(
            "sqhd,skhd->shqk", grad_output, value_rows, preferred_element_type=jnp.float32
        )
        inner_sum = jnp.sum(softmax_rows * grad_probs, axis=-1, keepdims=True)
        grad_scores = (softmax_rows * (grad_probs - inner_sum + grad_totals[..., None])).astype(
            jnp.bfloat16
        )
        grad_q = (
            jnp.einsum("shqk,skhd->sqhd", grad_scores, key_rows, preferred_element_type=jnp.float32)
            * score_scale
        )
        grad_k = (
            jnp.einsum(
                "shqk,sqhd->skhd", grad_scores, query_rows, preferred_element_type=jnp.float32
            )
            * score_scale
        )
        grad_query = grad_query + spread_rows(grad_q.reshape(-1, HEADS, HEAD_DIM), dilation, 0.0)
        key_terms.append(
            jnp.stack(
                [grad_k.reshape(-1, HEADS, HEAD_DIM), grad_value.reshape(-1, HEADS, HEAD_DIM)],
                axis=1,
            ).reshape(-1, 2 * D)
        )
        bit_counts.append(group_size.bit_length() - 1)
        dilations.append(dilation)
    own_terms = return_pairs(key_terms, bit_counts, seq_index)
    grad_key = jnp.zeros(grad_mixed.shape, jnp.float32)
    grad_val = jnp.zeros(grad_mixed.shape, jnp.float32)
    for branch in range(BRANCHES):
        pair_rows = own_terms[branch].reshape(-1, 2, HEADS, HEAD_DIM)
        grad_key = grad_key + spread_rows(pair_rows[:, 0], dilations[branch], 0.0)
        grad_val = grad_val + spread_rows(pair_rows[:, 1], dilations[branch], 0.0)
    return jnp.stack([grad_query, grad_key, grad_val], axis=1).reshape(tok_dev, 3 * D)


def layer_forward(hidden, upper_mat, lower_mat, row_set, lengths_row, seq_len, seq_index):
    normed = layer_norm(hidden, row_set[0], row_set[1]).astype(jnp.bfloat16)
    biases = jnp.concatenate([row_set[2], jnp.zeros_like(row_set[2]), row_set[3]])
    packed = (
        jnp.dot(normed, upper_mat[:, : 3 * D], preferred_element_type=jnp.float32) + biases[None, :]
    ).astype(jnp.bfloat16)
    mixed_out, attention_state = attend_forward(packed, lengths_row, seq_len, seq_index)
    mixed_low = mixed_out.reshape(-1, D).astype(jnp.bfloat16)
    middle = (
        hidden
        + jnp.dot(mixed_low, upper_mat[:, 3 * D : 4 * D], preferred_element_type=jnp.float32)
        + row_set[4][None, :]
    )
    second = layer_norm(middle, row_set[5], row_set[6]).astype(jnp.bfloat16)
    before = (
        jnp.dot(second, upper_mat[:, 4 * D :], preferred_element_type=jnp.float32)
        + row_set[8:].reshape(-1)[None, :]
    )
    active = jax.nn.gelu(before, approximate=True).astype(jnp.bfloat16)
    result = (
        middle
        + jnp.dot(active, lower_mat, preferred_element_type=jnp.float32)
        + row_set[7][None, :]
    )
    return (result, (hidden, normed, mixed_low, middle, second, before, active, attention_state))


def layer_backward(grad_result, upper_mat, lower_mat, row_set, layer_state, seq_len, seq_index):
    hidden, normed, mixed_low, middle, second, before, active, attention_state = layer_state
    grad_out = grad_result.astype(jnp.bfloat16)
    grad_lower = contract_rows(active, grad_out)
    grad_fc2_bias = jnp.sum(grad_out, axis=0, dtype=jnp.float32)
    grad_active = contract_cols(grad_out, lower_mat)
    gelu_value, gelu_back = jax.vjp(partial(jax.nn.gelu, approximate=True), before)
    grad_before = gelu_back(grad_active)[0].astype(jnp.bfloat16)
    grad_fc1 = contract_rows(second, grad_before)
    grad_fc1_bias = jnp.sum(grad_before, axis=0, dtype=jnp.float32)
    grad_second = contract_cols(grad_before, upper_mat[:, 4 * D :])
    norm_value, norm_back = jax.vjp(layer_norm, middle, row_set[5], row_set[6])
    grad_middle, grad_gain_two, grad_shift_two = norm_back(grad_second)
    grad_middle = grad_middle + grad_result
    grad_branch = grad_middle.astype(jnp.bfloat16)
    grad_proj = contract_rows(mixed_low, grad_branch)
    grad_proj_bias = jnp.sum(grad_branch, axis=0, dtype=jnp.float32)
    grad_mixed = contract_cols(grad_branch, upper_mat[:, 3 * D : 4 * D]).reshape(
        -1, HEADS, HEAD_DIM
    )
    grad_packed = attend_backward(grad_mixed, attention_state, seq_len, seq_index).astype(
        jnp.bfloat16
    )
    grad_qkv = contract_rows(normed, grad_packed)
    packed_sums = jnp.sum(grad_packed, axis=0, dtype=jnp.float32)
    grad_normed = contract_cols(grad_packed, upper_mat[:, : 3 * D])
    first_value, first_back = jax.vjp(layer_norm, hidden, row_set[0], row_set[1])
    grad_hidden, grad_gain_one, grad_shift_one = first_back(grad_normed)
    grad_hidden = grad_hidden + grad_middle
    grad_upper = jnp.concatenate([grad_qkv, grad_proj, grad_fc1], axis=1)
    small_rows = jnp.stack(
        [
            grad_gain_one,
            grad_shift_one,
            packed_sums[:D],
            packed_sums[2 * D :],
            grad_proj_bias,
            grad_gain_two,
            grad_shift_two,
            grad_fc2_bias,
        ]
    )
    grad_rows = jnp.concatenate([small_rows, grad_fc1_bias.reshape(-1, D)], axis=0)
    return (grad_hidden, (grad_upper, grad_lower, grad_rows))


def inverse_root(matrix):
    identity = jnp.eye(matrix.shape[-1], dtype=jnp.float32)
    regular = matrix + root_eps * identity
    frob_norm = jnp.sqrt(jnp.sum(regular * regular, axis=(1, 2), keepdims=True))
    scaled = 2.5 / frob_norm
    root_mat = identity * jnp.sqrt(jnp.sqrt(scaled))
    moving = regular * scaled
    for sweep_id in range(NEWTON):
        factor = (5.0 * identity - moving) * 0.25
        root_mat = jnp.einsum("kij,kjl->kil", root_mat, factor, precision=highest)
        square = jnp.einsum("kij,kjl->kil", factor, factor, precision=highest)
        fourth = jnp.einsum("kij,kjl->kil", square, square, precision=highest)
        moving = jnp.einsum("kij,kjl->kil", fourth, moving, precision=highest)
    return root_mat


def adam_update(weight, first_mom, second_mom, grad, rate, decay):
    first_new = beta_one * first_mom + (1.0 - beta_one) * grad
    second_new = beta_two * second_mom + (1.0 - beta_two) * grad * grad
    first_hat = first_new / (1.0 - beta_one**STEP)
    second_hat = second_new / (1.0 - beta_two**STEP)
    return (
        first_new,
        second_new,
        weight - rate * (first_hat / (jnp.sqrt(second_hat) + adam_eps) + decay * weight),
    )


def per_device(
    features,
    tile_mask,
    lengths,
    owners,
    layer_blocks,
    stat_left,
    stat_right,
    io_weights,
    io_first,
    io_second,
    vectors,
    vec_first,
    vec_second,
):
    tok_dev = features.shape[1]
    seq_size = lax.axis_size("seq")
    seq_len = tok_dev * seq_size
    seq_index = lax.axis_index("seq")
    core_index = lax.axis_index("opt")
    targets = features[0].astype(jnp.float32)
    chosen = tile_mask[0][:, None] > 0
    lengths_row = lax.dynamic_index_in_dim(lengths, core_index, 0, keepdims=False)
    places = seq_index * tok_dev + jnp.arange(tok_dev, dtype=jnp.int32)
    all_blocks, all_io = (
        lax.all_gather(layer_blocks.astype(jnp.bfloat16), ("seq", "opt"), axis=0, tiled=True),
        lax.all_gather(io_weights.astype(jnp.bfloat16), ("seq", "opt"), axis=0, tiled=True),
    )
    natural = jnp.zeros_like(all_blocks).at[owners].set(all_blocks)
    upper_mats, lower_mats = assemble(natural)
    tile_count = lax.psum(jnp.sum(tile_mask.astype(jnp.float32)), ("seq", "opt"))
    layer_rows, tail_rows = unpack(vectors)
    token_vec = tail_rows[3 + FEAT // D :].reshape(FEAT)
    head_bias = tail_rows[3 : 3 + FEAT // D].reshape(FEAT)
    inputs = jnp.where(chosen, token_vec[None, :], targets).astype(jnp.bfloat16)
    in_weight = all_io[:, 0]
    head_weight = all_io[:, 1]
    hidden = jnp.dot(inputs, in_weight, preferred_element_type=jnp.float32) + tail_rows[2][None, :]
    hidden = hidden + sine_places(slide_offsets(lengths_row, places))
    layer_id = 0
    hidden, layer_state = layer_forward(
        hidden,
        upper_mats[layer_id],
        lower_mats[layer_id],
        layer_rows[layer_id],
        lengths_row,
        seq_len,
        seq_index,
    )
    layer_states = [layer_state]
    final, final_back = jax.vjp(layer_norm, hidden, tail_rows[0], tail_rows[1])
    final_low = final.astype(jnp.bfloat16)
    predict = contract_cols(final_low, head_weight) + head_bias[None, :]
    difference = predict - targets
    error_local = jnp.sum(jnp.where(chosen, difference * difference, 0.0))
    grad_pred = jnp.where(chosen, 2.0 * difference / tile_count, 0.0).astype(jnp.bfloat16)
    grad_head = contract_rows(grad_pred, final_low)
    grad_head_bias = jnp.sum(grad_pred, axis=0, dtype=jnp.float32)
    grad_final = jnp.dot(grad_pred, head_weight, preferred_element_type=jnp.float32)
    grad_hidden, grad_gain_last, grad_shift_last = final_back(grad_final)
    layer_grads = [None] * LAYERS
    for layer_id in reversed(range(LAYERS)):
        grad_hidden, layer_grads[layer_id] = layer_backward(
            grad_hidden,
            upper_mats[layer_id],
            lower_mats[layer_id],
            layer_rows[layer_id],
            layer_states[layer_id],
            seq_len,
            seq_index,
        )
    grad_in_low = grad_hidden.astype(jnp.bfloat16)
    grad_in = contract_rows(inputs, grad_in_low)
    grad_in_bias = jnp.sum(grad_in_low, axis=0, dtype=jnp.float32)
    grad_inputs = contract_cols(grad_in_low, in_weight)
    grad_token = jnp.sum(jnp.where(chosen, grad_inputs, 0.0), axis=0)
    grad_upper = jnp.stack([item[0] for item in layer_grads])
    grad_lower = jnp.stack([item[1] for item in layer_grads])
    slot_grads = disassemble(grad_upper, grad_lower)[owners]
    io_grads = jnp.stack([grad_in, grad_head], axis=1)
    vec_grads = jnp.concatenate(
        [
            jnp.stack([item[2] for item in layer_grads]).reshape(-1, D),
            jnp.stack([grad_gain_last, grad_shift_last, grad_in_bias]),
            grad_head_bias.reshape(-1, D),
            grad_token.reshape(-1, D),
        ],
        axis=0,
    )
    slot_sum, io_sum = (
        lax.psum_scatter(slot_grads, ("seq", "opt"), scatter_dimension=0, tiled=True),
        lax.psum_scatter(io_grads, ("seq", "opt"), scatter_dimension=0, tiled=True),
    )
    vec_sum, error_sum = lax.psum((vec_grads, error_local), ("seq", "opt"))
    local_sq = jnp.sum(slot_sum * slot_sum) + jnp.sum(io_sum * io_sum)
    grad_norm = jnp.sqrt(lax.psum(local_sq, ("seq", "opt")) + jnp.sum(vec_sum * vec_sum))
    factor = jnp.minimum(1.0, clip_limit / grad_norm)
    block_grads = slot_sum * factor
    left_new = beta_stat * stat_left + (1.0 - beta_stat) * jnp.einsum(
        "kij,klj->kil", block_grads, block_grads, precision=highest
    )
    right_new = beta_stat * stat_right + (1.0 - beta_stat) * jnp.einsum(
        "kji,kjl->kil", block_grads, block_grads, precision=highest
    )
    direction = jnp.einsum("kij,kjl->kil", inverse_root(left_new), block_grads, precision=highest)
    direction = jnp.einsum("kij,kjl->kil", direction, inverse_root(right_new), precision=highest)
    blocks_new = layer_blocks - rate_shampoo * direction
    io_first_new, io_second_new, io_new = adam_update(
        io_weights, io_first, io_second, io_sum * factor, rate_adam, weight_decay
    )
    vec_first_new, vec_second_new, vec_new = adam_update(
        vectors, vec_first, vec_second, vec_sum * factor, rate_vector, 0.0
    )
    return (
        grad_norm,
        error_sum,
        tile_count,
        block_grads,
        left_new,
        right_new,
        blocks_new,
        io_first_new,
        io_second_new,
        io_new,
        vec_first_new,
        vec_second_new,
        vec_new,
    )


BF=jnp.bfloat16; LANE=128; IO=48
def swap(value, axis, mask):
    return lax.ppermute(value, axis, [(s, s ^ mask) for s in range(lax.axis_size(axis))])
def gate(*values):
    return lax.optimization_barrier(values)

COUNT_AT=3*3*BLOCK+6*IO
SHARD_HALF=COUNT_AT+16
def pack_kernel(blocks_ref, in_ref, head_ref, mask_ref, first_ref, second_ref, whole_ref):
    count=jnp.sum(mask_ref[...].astype(jnp.float32),keepdims=True)
    lane=lax.broadcasted_iota(jnp.int32,(BLOCK,LANE),1)
    pad=lambda x: jnp.concatenate([x,jnp.zeros((BLOCK,LANE-BLOCK),x.dtype)],axis=1)
    for h,(io,out_ref) in enumerate(zip((in_ref,head_ref),(first_ref,second_ref))):
        for g in range(3):
            b=[pad(blocks_ref[(h*3+g)*4+t]) for t in range(4)]
            for v in range(3):
                tile=jnp.where(lane<BLOCK,b[v],pltpu.roll(b[3],BLOCK-32*v,1))
                at=(g*3+v)*BLOCK
                out_ref[at:at+BLOCK,:]=tile.astype(BF)
        for v in range(6):
            at=9*BLOCK+v*IO
            out_ref[at:at+IO,:]=io[:,v*LANE:(v+1)*LANE].astype(BF)
        out_ref[COUNT_AT:,:]=jnp.broadcast_to(count,(16,LANE)).astype(BF)
        whole_ref[h*SHARD_HALF:(h+1)*SHARD_HALF,:]=out_ref[...]
def vmem(): return pl.BlockSpec(memory_space=pltpu.VMEM)
def smem(): return pl.BlockSpec(memory_space=pltpu.SMEM)
def hbm(): return pl.BlockSpec(memory_space=pltpu.HBM)
def from_hbm(body, name, outs, ins, scratch, smem_args=(), late=(), vmem_mib=48, micros=10):
    n_s,n_i,n_o=len(smem_args),len(ins),len(outs)
    def kernel(*refs):
        scalars,args,results=refs[:n_s],refs[n_s:n_s+n_i],refs[n_s+n_i:n_s+n_i+n_o]
        rest=refs[n_s+n_i+n_o:]
        held,made,more=rest[:n_i],rest[n_i:n_i+n_o],rest[n_i+n_o:-2]
        in_sem,out_sem=rest[-2:]
        loads=[pltpu.make_async_copy(a,h,in_sem.at[i]) for i,(a,h) in enumerate(zip(args,held))]
        for c in loads: c.start()
        for i,c in enumerate(loads):
            if i not in late: c.wait()
        body(*([loads[i].wait for i in late]),*scalars,*held,*made,*more)
        stores=[pltpu.make_async_copy(m,r,out_sem.at[i]) for i,(m,r) in enumerate(zip(made,results))]
        for c in stores: c.start()
        for c in stores: c.wait()
    ins=[pltpu.with_memory_space_constraint(a,pltpu.HBM) for a in ins]
    return pl.pallas_call(kernel,out_shape=[pltpu.HBM(s,t) for s,t in outs],
        in_specs=[smem()]*n_s+[hbm()]*n_i,out_specs=[hbm()]*n_o,
        scratch_shapes=[pltpu.VMEM(a.shape,a.dtype) for a in ins]+[pltpu.VMEM(s,t) for s,t in outs]+list(scratch)
            +[pltpu.SemaphoreType.DMA((n_i,)),pltpu.SemaphoreType.DMA((n_o,))],
        compiler_params=pltpu.CompilerParams(vmem_limit_bytes=vmem_mib<<20),
        cost_estimate=pl.CostEstimate(flops=0,transcendentals=0,bytes_accessed=int(micros*3.3e6)),name=name)(*smem_args,*ins)
def pack_shard(blocks, io, mask):
    return pl.pallas_call(pack_kernel,out_shape=[jax.ShapeDtypeStruct((n*SHARD_HALF,LANE),BF) for n in (1,1,2)],in_specs=[vmem()]*4,out_specs=[vmem()]*3,name="pack_shard")(blocks,io[:,0],io[:,1],mask)

HOPS=(("opt",1),("seq",1),("seq",2),("seq",4),("seq",8))
def hop(value, k):
    return value+swap(value,*HOPS[k])

def gather_tree(first, second, own):
    half=first.shape[0]
    near=[None]*4; cross=[None]*4
    def first_step(k,a,b):
        near[k]=(swap(a,"seq",1),swap(b,"seq",2))
    def second_step(k,a,b):
        cross[k]=(swap(jnp.concatenate([a,near[k][0]]),"seq",2),swap(jnp.concatenate([b,near[k][1]]),"seq",1))
    far1=swap(own,"seq",4)
    far2=swap(own,"seq",8)
    first_step(0,first,second)
    second_step(0,first,second)
    first_step(1,far1[:half],far1[half:])
    first_step(2,far2[:half],far2[half:])
    far3=swap(far2,"seq",4)
    near[1],near[2],far3=gate(near[1],near[2],far3)
    second_step(1,far1[:half],far1[half:])
    first_step(3,far3[:half],far3[half:])
    second_step(2,far2[:half],far2[half:])
    second_step(3,far3[:half],far3[half:])
    out=[jnp.concatenate([piece,*near[k],*cross[k]]) for k,piece in enumerate((own,far1,far2,far3))]
    return out+[swap(piece,"opt",1) for piece in out]

HELD=64*SHARD_HALF
N_BLOCK=768
def load_shards(bufs, held, sem, fourths):
    rows=bufs[0].shape[0]
    loads=[pltpu.make_async_copy(b,held.at[pl.ds(k*rows,rows)],sem.at[k]) for k,b in enumerate(bufs)]
    for c in loads: c.start()
    fourths()
    for k,c in enumerate(loads):
        c.wait()
        def unpack(u,carry,k=k):
            at=(k*8+u)*SHARD_HALF
            for g in range(3):
                parts=[held[pl.ds(pl.multiple_of(at+(g*3+v)*BLOCK,16),BLOCK),BLOCK:] for v in range(3)]
                to=HELD+((k*8+u)*3+g)*BLOCK
                held[pl.ds(pl.multiple_of(to,16),BLOCK),:BLOCK]=jnp.concatenate(parts,axis=1)
            return carry
        lax.fori_loop(0,8,unpack,0,unroll=8)

def join_kernel(plan, io_out, owners_ref, row_ref, io_ref, *refs):
    bufs=refs[:8]; n_out=len(plan); outs=refs[8:8+n_out]; io_ref_out,count_ref=refs[8+n_out:8+n_out+2]
    held,stage,where,in_sem,out_sem,io_sem=refs[8+n_out+2:]
    def invert():
        def one(i,carry):
            for j in range(8):
                where[owners_ref[i*8+j]]=row_ref[i*8+j]
            return carry
        lax.fori_loop(0,N_BLOCK//8,one,0)
    load_shards(bufs,held,in_sem,invert)
    def io_copy(d,total):
        at=io_ref[io_out,d]
        for v in range(6):
            pltpu.make_async_copy(held.at[pl.ds(pl.multiple_of(at+v*IO,16),IO)],
                io_ref_out.at[pl.ds(pl.multiple_of(d*IO,IO),IO),pl.ds(v*LANE,LANE)],io_sem).start()
        return total+held[pl.ds(pl.multiple_of(at+6*IO,16),16),:].astype(jnp.float32)
    count_ref[...]=lax.fori_loop(0,io_ref.shape[1],io_copy,jnp.zeros((16,LANE),jnp.float32))
    def block(n):
        return held[pl.ds(pl.multiple_of(where[n],16),BLOCK),:BLOCK]
    pending=[]; index=0
    for (first,stride,rows,stripes),out in zip(plan,outs):
        per=8//stripes if stripes<8 else 1
        for i0 in range(0,rows,per):
            slot=index%2
            if index>=2:
                for c in pending[index-2]: c.wait()
            for b in range(per):
                def one(c,carry,b=b,i0=i0):
                    n=first+(i0+b)*stride+4*c
                    stage[slot,:,pl.ds(pl.multiple_of((b*stripes+c)*4*BLOCK,128),4*BLOCK)]=jnp.concatenate([block(n+t) for t in range(4)],axis=1)
                    return carry
                lax.fori_loop(0,stripes,one,0,unroll=2 if stripes%4 else 4)
            w=stripes*4*BLOCK
            cs=[pltpu.make_async_copy(stage.at[slot,:,pl.ds(b*w,w)],out.at[pl.ds((i0+b)*BLOCK,BLOCK)],out_sem.at[slot,b]) for b in range(per)]
            for c in cs: c.start()
            pending.append(cs); index+=1
    for cs in pending[-2:]:
        for c in cs: c.wait()
    pltpu.make_async_copy(io_ref_out,io_ref_out,io_sem).wait()

COLS=(4*D+FF)//BLOCK
FIRST_PLAN=((0,COLS,8,6),(24,COLS,8,2))
SECOND_PLAN=((32,COLS,8,8),(8*COLS,8,32,2))
def join_weights(plan, io_out, bufs, owners, rows, io_rows):
    shapes=[(r*BLOCK,s*4*BLOCK) for _,_,r,s in plan]+[(FEAT,D)]
    return pl.pallas_call(partial(join_kernel,plan,io_out),
        out_shape=[pltpu.HBM(s,BF) for s in shapes]+[jax.ShapeDtypeStruct((16,LANE),jnp.float32)],
        in_specs=[smem()]*3+[hbm()]*8, out_specs=[hbm()]*len(shapes)+[vmem()],
        scratch_shapes=[pltpu.VMEM((HELD+N_BLOCK//4*BLOCK,LANE),BF),pltpu.VMEM((2,BLOCK,FF),BF),pltpu.SMEM((N_BLOCK,),jnp.int32),
            pltpu.SemaphoreType.DMA((8,)),pltpu.SemaphoreType.DMA((2,4)),pltpu.SemaphoreType.DMA],
        compiler_params=pltpu.CompilerParams(vmem_limit_bytes=40<<20), cost_estimate=pl.CostEstimate(flops=0,transcendentals=0,bytes_accessed=int((13 if io_out==0 else 17)*3.3e6)), name="join_weights")(owners,rows,io_rows,*[pltpu.with_memory_space_constraint(b,pltpu.HBM) for b in bufs])

def shard_rows(seq_index, core):
    def unit(dev,h):
        rel=(dev//2)^seq_index; xy=rel%4
        u=jnp.where(xy==0,h,jnp.where(h==0,jnp.where(xy==1,2,xy+2),jnp.where(xy==2,3,jnp.where(xy==1,6,7))))
        return (rel//4+4*((dev%2)^core))*8+u
    slot=jnp.arange(N_BLOCK,dtype=jnp.int32); s=slot%24
    u=unit(slot//24,s//12); g=s%12//4; t=s%4
    rows=jnp.where(t<3,u*SHARD_HALF+(g*3+t)*BLOCK,HELD+(u*3+g)*BLOCK)
    dev=jnp.arange(32,dtype=jnp.int32)
    io=jnp.stack([unit(dev,h)*SHARD_HALF+9*BLOCK for h in (0,1)])
    return rows.astype(jnp.int32),io.astype(jnp.int32)
def gather_shards(layer_blocks, io_weights, mask):
    return gather_tree(*pack_shard(layer_blocks,io_weights,mask))

HD=48; HEADS=16; SLIDES=4; SEG=1024; N=2048; H=512; TQ=256; TK=128
C2=HD**-0.5*math.log2(math.e)
def place_facts(index, head, lengths_ref, core):
    parity=lax.rem(head+(index//H)%2,2)
    pos=(index//SEG)*SEG+2*(index%H)+parity
    slide=jnp.zeros_like(index); end=jnp.int32(0)
    for i in range(SLIDES-1):
        end=end+lengths_ref[core,i]
        slide=slide+jnp.where(pos>=end,1,0)
    d=(pos-head)&15
    level=sum(jnp.where((d&(2**i-1))==0,1,0) for i in range(1,5))
    return slide.astype(jnp.float32), level.astype(jnp.float32)

def arrange(src, dst, odd):
    for pair in range(8):
        first, second = src[2*pair], src[2*pair+1]
        turn=lambda t: jnp.concatenate([t[:,64:],t[:,:64]],axis=1)
        ft, st = turn(first), turn(second)
        low=lax.broadcasted_iota(jnp.int32,first.shape,1)<64
        evens=jnp.where(low,first,st); odds=jnp.where(low,ft,second)
        near=jnp.where(odd,odds,evens); far=jnp.where(odd,evens,odds)
        at=(pair//4)*SEG+(pair%4)*128
        dst[:,at:at+128]=near.astype(dst.dtype); dst[:,at+H:at+H+128]=far.astype(dst.dtype)

def restore(get, put, odd):
    for pair in range(8):
        at=(pair//4)*SEG+(pair%4)*128
        near, far = get(at), get(at+H)
        evens=jnp.where(odd,far,near); odds=jnp.where(odd,near,far)
        turn=lambda t: jnp.concatenate([t[:,64:],t[:,:64]],axis=1)
        low=lax.broadcasted_iota(jnp.int32,evens.shape,1)<64
        put(2*pair, jnp.where(low,evens,turn(odds)))
        put(2*pair+1, jnp.where(low,turn(evens),odds))

def setup(lengths_ref, ids_ref, slide_k, level_k, row_facts):
    head, core = ids_ref[0], ids_ref[1]
    def fill(i, c):
        idx=lax.broadcasted_iota(jnp.int32,(TK,128),0)+i*TK
        s,l=place_facts(idx,head,lengths_ref,core)
        slide_k[pl.ds(pl.multiple_of(i*TK,TK),TK),:]=s
        level_k[pl.ds(pl.multiple_of(i*TK,TK),TK),:]=l
        return c
    lax.fori_loop(0,N//TK,fill,0)
    idx=lax.broadcasted_iota(jnp.int32,(8,N),1)
    s,l=place_facts(idx,head,lengths_ref,core)
    row_facts[0:8,:]=s; row_facts[8:16,:]=l

def key_rows(seg, near):
    own=[(seg*SEG+i*TK,True) for i in range(SEG//TK)]
    other=[((1-seg)*SEG+i*TK,False) for i in range(H//TK)] if near else []
    return own+other

def wide(x): return jnp.concatenate([x]*(TQ//128),axis=1)

def forward_kernel(lengths_ref, ids_ref, qkv_ref, o_ref, out_ref, lse_ref, qkvT, krow, slide_k, level_k, row_facts, s_ref, p_ref):
    odd=lax.rem(ids_ref[0],2)==1
    arrange(qkv_ref, qkvT, odd)
    setup(lengths_ref, ids_ref, slide_k, level_k, row_facts)
    for i in range(N//128):
        krow[i*128:(i+1)*128,:]=qkvT[HD:2*HD,i*128:(i+1)*128].astype(jnp.float32).T.astype(jnp.bfloat16)
    for seg in range(2):
        for near in (True,False):
            tiles=key_rows(seg,near)
            def part(c, carry, seg=seg, near=near, tiles=tiles):
                at=pl.multiple_of(seg*SEG+(0 if near else H)+c*TQ,TQ)
                qT=qkvT[0:HD,pl.ds(at,TQ)]
                sq=row_facts[0:1,pl.ds(at,TQ)]; lq=row_facts[8:9,pl.ds(at,TQ)]
                top=jnp.full((8,TQ),-jnp.inf,jnp.float32)
                for t,(r,own) in enumerate(tiles):
                    s=jnp.dot(krow[r:r+TK,:],qT,preferred_element_type=jnp.float32)
                    s=jnp.where(wide(slide_k[r:r+TK,:])==sq,s,-1e30)
                    s_ref[t*TK:(t+1)*TK,:]=s
                    top=jnp.maximum(top,jnp.max(s.reshape(TK//8,8,TQ),axis=0))
                m=jnp.max(top,axis=0,keepdims=True)
                total=jnp.zeros((8,TQ),jnp.float32)
                for t,(r,own) in enumerate(tiles):
                    e=jnp.exp2((s_ref[t*TK:(t+1)*TK,:]-m)*C2)
                    if near:
                        lk=wide(level_k[r:r+TK,:])
                        e=e*(jnp.minimum(lk,lq)+1.0 if own else jnp.minimum(lk,lq))
                    total=total+jnp.sum(e.reshape(TK//8,8,TQ),axis=0)
                    p_ref[t*TK:(t+1)*TK,:]=e.astype(jnp.bfloat16)
                l=jnp.sum(total,axis=0,keepdims=True)
                acc=jnp.zeros((HD,TQ),jnp.float32)
                acc=jnp.dot(qkvT[2*HD:3*HD,seg*SEG:(seg+1)*SEG],p_ref[0:SEG,:],preferred_element_type=jnp.float32)
                if near:
                    acc=acc+jnp.dot(qkvT[2*HD:3*HD,(1-seg)*SEG:(1-seg)*SEG+H],p_ref[SEG:SEG+H,:],preferred_element_type=jnp.float32)
                o_ref[:,pl.ds(at,TQ)]=acc/l
                lse_ref[:,pl.ds(at,TQ)]=jnp.broadcast_to(m*C2+jnp.log2(l),(8,TQ))
                return carry
            lax.fori_loop(0,H//TQ,part,0)
    def put(c,v): out_ref[c]=v.astype(jnp.bfloat16)
    restore(lambda at: o_ref[:,at:at+128], put, odd)

def backward_kernel(lengths_ref, ids_ref, qkv_ref, do_ref, o_ref, lse_ref, out_ref, qkvT, doT, rows, slide_k, level_k, row_facts, dqT, dkv, p_ref, ds_ref):
    odd=lax.rem(ids_ref[0],2)==1
    arrange(qkv_ref, qkvT, odd)
    arrange(do_ref, doT, odd)
    setup(lengths_ref, ids_ref, slide_k, level_k, row_facts)
    for i in range(N//128):
        l=slice(i*128,(i+1)*128)
        for j in range(3):
            rows[j,l,:]=qkvT[j*HD:(j+1)*HD,l].astype(jnp.float32).T.astype(jnp.bfloat16)
        rows[3,l,:]=doT[:,l].astype(jnp.float32).T.astype(jnp.bfloat16)
    dkv[...]=jnp.zeros_like(dkv)
    for seg in range(2):
        for near in (True,False):
            tiles=key_rows(seg,near)
            def part(c, carry, seg=seg, near=near, tiles=tiles):
                at=pl.multiple_of(seg*SEG+(0 if near else H)+c*TQ,TQ)
                qT=qkvT[0:HD,pl.ds(at,TQ)]; gT=doT[:,pl.ds(at,TQ)]
                q=rows[0,pl.ds(at,TQ),:]; g=rows[3,pl.ds(at,TQ),:]
                sq=row_facts[0:1,pl.ds(at,TQ)]; lq=row_facts[8:9,pl.ds(at,TQ)]
                lse=lse_ref[0:1,pl.ds(at,TQ)]
                inner=jnp.sum(gT.astype(jnp.float32)*o_ref[:,pl.ds(at,TQ)],axis=0,keepdims=True)
                for t,(r,own) in enumerate(tiles):
                    s=jnp.dot(rows[1,r:r+TK,:],qT,preferred_element_type=jnp.float32)
                    dp=jnp.dot(rows[2,r:r+TK,:],gT,preferred_element_type=jnp.float32)
                    e=jnp.exp2(s*C2-lse)
                    if near:
                        lk=wide(level_k[r:r+TK,:])
                        e=e*(jnp.minimum(lk,lq)+1.0 if own else jnp.minimum(lk,lq))
                    e=jnp.where(wide(slide_k[r:r+TK,:])==sq,e,0.0)
                    p_ref[t*TK:(t+1)*TK,:]=e.astype(jnp.bfloat16)
                    ds_ref[t*TK:(t+1)*TK,:]=(e*(dp-inner)).astype(jnp.bfloat16)
                dq=jnp.dot(qkvT[HD:2*HD,seg*SEG:(seg+1)*SEG],ds_ref[0:SEG,:],preferred_element_type=jnp.float32)
                if near:
                    dq=dq+jnp.dot(qkvT[HD:2*HD,(1-seg)*SEG:(1-seg)*SEG+H],ds_ref[SEG:SEG+H,:],preferred_element_type=jnp.float32)
                dqT[:,pl.ds(at,TQ)]=dq*HD**-0.5
                own=slice(seg*SEG,(seg+1)*SEG)
                dkv[0,own,:]+=jnp.dot(ds_ref[0:SEG,:],q,preferred_element_type=jnp.float32)
                dkv[1,own,:]+=jnp.dot(p_ref[0:SEG,:],g,preferred_element_type=jnp.float32)
                if near:
                    oth=slice((1-seg)*SEG,(1-seg)*SEG+H)
                    dkv[0,oth,:]+=jnp.dot(ds_ref[SEG:SEG+H,:],q,preferred_element_type=jnp.float32)
                    dkv[1,oth,:]+=jnp.dot(p_ref[SEG:SEG+H,:],g,preferred_element_type=jnp.float32)
                return carry
            lax.fori_loop(0,H//TQ,part,0)
    def putter(j):
        def put(c,v): out_ref[c,j*HD:(j+1)*HD,:]=v.astype(jnp.bfloat16)
        return put
    restore(lambda at: dqT[:,at:at+128], putter(0), odd)
    restore(lambda at: dkv[0,at:at+128,:].T*HD**-0.5, putter(1), odd)
    restore(lambda at: dkv[1,at:at+128,:].T, putter(2), odd)

def attend(lengths, ids, qkv):
    return from_hbm(forward_kernel,"attend_forward",[((HD,N),F32),((16,HD,128),BF),((8,N),F32)],[qkv],
        [pltpu.VMEM((3*HD,N),BF),pltpu.VMEM((N,HD),BF),pltpu.VMEM((N,128),F32),pltpu.VMEM((N,128),F32),pltpu.VMEM((16,N),F32),
            pltpu.VMEM((SEG+H,TQ),F32),pltpu.VMEM((SEG+H,TQ),BF)],(lengths,ids))
def attend_back(lengths, ids, qkv, do, o, lse):
    return from_hbm(backward_kernel,"attend_backward",[((16,3*HD,128),BF)],[qkv,do,o,lse],
        [pltpu.VMEM((3*HD,N),BF),pltpu.VMEM((HD,N),BF),pltpu.VMEM((4,N,HD),BF),pltpu.VMEM((N,128),F32),pltpu.VMEM((N,128),F32),pltpu.VMEM((16,N),F32),
            pltpu.VMEM((HD,N),F32),pltpu.VMEM((2,N,HD),F32),pltpu.VMEM((SEG+H,TQ),BF),pltpu.VMEM((SEG+H,TQ),BF)],(lengths,ids),micros=13)[0]

F32=jnp.float32
EPS=1e-05
def norm_parts(x):
    centred=x-jnp.mean(x,axis=-1,keepdims=True)
    spread=lax.rsqrt(jnp.mean(centred*centred,axis=-1,keepdims=True)+EPS)
    return centred*spread,spread
def norm_back(grad,unit,spread,gain):
    inner=grad*gain
    back=spread*(inner-jnp.mean(inner,axis=-1,keepdims=True)-unit*jnp.mean(inner*unit,axis=-1,keepdims=True))
    return back,jnp.sum(grad*unit,axis=0,keepdims=True),jnp.sum(grad,axis=0,keepdims=True)
def put_turned(ref,at,x):
    for c in range(x.shape[1]//LANE):
        ref[at+c*LANE:at+(c+1)*LANE,:]=x[:,c*LANE:(c+1)*LANE].astype(F32).T.astype(BF)
def turned(ref,rows):
    return jnp.concatenate([ref[c*LANE:(c+1)*LANE,:].astype(F32).T for c in range(rows//LANE)],axis=1)
def mm(a,b): return jnp.dot(a,b,preferred_element_type=F32)
def mm_t(a,b): return lax.dot_general(a,b,(((1,),(1,)),((),())),preferred_element_type=F32)
LATE_ROWS=4*D+2*FF+FEAT
GELU_A=math.sqrt(2.0/math.pi); GELU_B=0.044715
def mlp_kernel(up_here, down_here, head_here, count_ref, hidden_ref, mixed_ref, targets_ref, chosen_ref, vec_ref, wo_ref, up_ref, down_ref, head_ref,
               middle_grad_ref, mixed_grad_ref, late_ref, rows_ref, kept):
    row=lambda i: vec_ref[i:i+1,:]
    mixed=turned(mixed_ref,D).astype(BF)
    middle=hidden_ref[...]+mm(mixed,wo_ref[...])+row(4)
    unit2,spread2=norm_parts(middle)
    second=(unit2*row(5)+row(6)).astype(BF)
    put_turned(late_ref,0,second)
    result=middle+row(7)
    up_here(); down_here()
    for c in range(FF//D):
        s=slice(c*D,(c+1)*D)
        before=mm(second,up_ref[:,s])+row(8+c)
        kept[:,s]=before
        active=(before*(0.5*(1.0+jnp.tanh(GELU_A*(before+GELU_B*(before*before*before)))))).astype(BF)
        put_turned(late_ref,D+c*D,active)
        result=result+mm(active,down_ref[s,:])
    unit,spread=norm_parts(result)
    final=(unit*row(12)+row(13)).astype(BF)
    put_turned(late_ref,3*D+2*FF+FEAT,final)
    head_here()
    chosen=chosen_ref[...]>0.0
    error=jnp.zeros((1,1),F32); grad_final=jnp.zeros_like(middle)
    for c in range(FEAT//D):
        s=slice(c*D,(c+1)*D)
        difference=mm_t(final,head_ref[s,:])+row(15+c)-targets_ref[:,s].astype(F32)
        error=error+jnp.sum(jnp.where(chosen,difference*difference,0.0),keepdims=True)
        pred=jnp.where(chosen,2.0*difference/count_ref[0],0.0).astype(BF)
        put_turned(late_ref,3*D+2*FF+c*D,pred)
        rows_ref[10+c:11+c,:]=jnp.sum(pred.astype(F32),axis=0,keepdims=True)
        grad_final=grad_final+mm(pred,head_ref[s,:])
    rows_ref[12:13,:]=jnp.broadcast_to(error,(1,D))
    grad_result,rows_ref[8:9,:],rows_ref[9:10,:]=norm_back(grad_final,unit,spread,row(12))
    grad_out=grad_result.astype(BF)
    put_turned(late_ref,2*D+2*FF,grad_out)
    rows_ref[3:4,:]=jnp.sum(grad_out.astype(F32),axis=0,keepdims=True)
    grad_second=jnp.zeros_like(middle)
    for c in range(FF//D):
        s=slice(c*D,(c+1)*D)
        grad_active=mm_t(grad_out,down_ref[s,:])
        x=kept[:,s]
        t=jnp.tanh(GELU_A*(x+GELU_B*(x*x*x)))
        slope=0.5*(1.0+t)+x*(0.5*(1.0-t*t)*(GELU_A*(1.0+3.0*GELU_B*(x*x))))
        grad_before=(grad_active*slope).astype(BF)
        put_turned(late_ref,2*D+FF+c*D,grad_before)
        rows_ref[4+c:5+c,:]=jnp.sum(grad_before.astype(F32),axis=0,keepdims=True)
        grad_second=grad_second+mm_t(grad_before,up_ref[:,s])
    back,rows_ref[1:2,:],rows_ref[2:3,:]=norm_back(grad_second,unit2,spread2,row(5))
    grad_middle=back+grad_result
    middle_grad_ref[...]=grad_middle
    grad_branch=grad_middle.astype(BF)
    put_turned(late_ref,D+FF,grad_branch)
    rows_ref[0:1,:]=jnp.sum(grad_branch.astype(F32),axis=0,keepdims=True)
    mixed_grad_ref[...]=mm_t(wo_ref[...],grad_branch).astype(BF)
    rows_ref[13:16,:]=jnp.zeros((3,D),F32)
def mlp_step(count, hidden, mixed, targets, chosen, vectors, wo, up, down, head):
    t=hidden.shape[0]
    low=lambda rows: ((rows,t),BF)
    return from_hbm(mlp_kernel,"mlp_step",[((t,D),F32),low(D),low(LATE_ROWS),((16,D),F32)],
        [hidden,mixed,targets,chosen,vectors,wo,up,down,head],[pltpu.VMEM((t,FF),F32)],(count.reshape(1),),late=(6,7,8),micros=13)

def input_kernel(in_here, parts_ref, hidden_ref, middle_grad_ref, chosen_ref, vec_ref, rows_ref, qkv_ref, in_ref, last_ref, sums_ref):
    heads,wide,t=parts_ref.shape; hd=wide//3
    for j in range(3):
        for h in range(heads):
            last_ref[j*D+h*hd:j*D+(h+1)*hd,:]=parts_ref[h,j*hd:(j+1)*hd,:]
    packed=last_ref[:3*D,:]
    grad_t=mm(qkv_ref[...],packed)
    grad=jnp.concatenate([grad_t[c*LANE:(c+1)*LANE,:].T for c in range(D//LANE)],axis=1)
    unit,spread=norm_parts(hidden_ref[...])
    back,gain,shift=norm_back(grad,unit,spread,vec_ref[0:1,:])
    grad_hidden=back+middle_grad_ref[...]
    low=grad_hidden.astype(BF)
    put_turned(last_ref,3*D,low)
    sums_ref[0:1,:]=gain; sums_ref[1:2,:]=shift
    ones=jnp.ones((8,t),BF)
    sums_ref[2:3,:]=mm_t(ones,packed[:D])[0:1]
    sums_ref[3:4,:]=mm_t(ones,packed[2*D:])[0:1]
    sums_ref[4:14,:]=rows_ref[0:10,:]
    sums_ref[14:15,:]=jnp.sum(low.astype(F32),axis=0,keepdims=True)
    sums_ref[15:17,:]=rows_ref[10:12,:]
    in_here()
    masked=jnp.where(chosen_ref[...]>0.0,low.astype(F32),0.0).astype(BF)
    for c in range(FEAT//D):
        sums_ref[17+c:18+c,:]=jnp.sum(mm_t(masked,in_ref[c*D:(c+1)*D,:]),axis=0,keepdims=True)
    sums_ref[19:20,:]=rows_ref[12:13,:]
    sums_ref[20:24,:]=jnp.zeros((4,D),F32)
def input_step(parts, hidden, middle_grad, chosen, vectors, rows, qkv, w_in):
    t=hidden.shape[0]
    return from_hbm(input_kernel,"input_step",[((4*D,t),BF),((24,D),F32)],[parts,hidden,middle_grad,chosen,vectors,rows,qkv,w_in],[],late=(7,),micros=5)

def front_kernel(qkv_here, features_ref, chosen_ref, places_ref, vec_ref, in_ref, qkv_ref, hidden_ref, early_ref, heads_ref, turned_ref):
    row=lambda i: vec_ref[i:i+1,:]
    chosen=chosen_ref[...]>0.0
    hidden=places_ref[...]+row(14)
    for c in range(FEAT//D):
        s=slice(c*D,(c+1)*D)
        part=jnp.where(chosen,row(17+c),features_ref[:,s].astype(F32)).astype(BF)
        put_turned(early_ref,D+c*D,part)
        hidden=hidden+mm(part,in_ref[s,:])
    hidden_ref[...]=hidden
    unit,spread=norm_parts(hidden)
    normed=(unit*row(0)+row(1)).astype(BF)
    put_turned(early_ref,0,normed)
    qkv_here()
    heads,wide,t=heads_ref.shape; hd=wide//3
    for j in range(3):
        out=mm(normed,qkv_ref[:,j*D:(j+1)*D])
        if j!=1: out=out+row(2 if j==0 else 3)
        put_turned(turned_ref,j*D,out.astype(BF))
        for h in range(heads):
            heads_ref[h,j*hd:(j+1)*hd,:]=turned_ref[j*D+h*hd:j*D+(h+1)*hd,:]
def front_step(features, chosen, places, vectors, w_in, qkv, heads):
    t=features.shape[0]
    return from_hbm(front_kernel,"front_step",[((t,D),F32),((D+FEAT,t),BF),((heads,3*D//heads,t),BF)],[features,chosen,places,vectors,w_in,qkv],
        [pltpu.VMEM((3*D,t),BF)],late=(5,),micros=5)

I16=jnp.int16; F32=jnp.float32; BF=jnp.bfloat16
GROUP=48; LANE=128; IO=48
STEP_Q=32000.0
UNITS=24; CODE_ROWS=32; PART=UNITS*GROUP+CODE_ROWS
A_ROWS=3*D+FF; X_ROWS=3*D+D+FF+D
ROUND=12582912.0

def encode(x):
    top=jnp.max(jnp.abs(x),axis=0,keepdims=True)
    code=jnp.ceil(jnp.log2(jnp.maximum(top,1e-30))*256.0)
    v=x*(STEP_Q*jnp.exp2(code*(-1.0/256.0)))
    return ((v+ROUND)-ROUND).astype(jnp.int32).astype(I16), code
def scale_of(code16):
    return jnp.exp2(code16.astype(jnp.int32).astype(F32)*(1.0/256.0))*(1.0/STEP_Q)
def pack_codes(codes):
    codes=codes+[jnp.zeros((CODE_ROWS-len(codes),LANE),F32)]
    return jnp.concatenate(codes,axis=0).astype(jnp.int32).astype(I16)

EARLY,MIXED,LATE,LAST=range(4)
PARTS=(((EARLY,0,D),("a",0)),((MIXED,0,D),("a",D)),((LATE,0,D),("a",2*D)),((LATE,D,FF),("a",3*D)),
    ((LAST,0,3*D),("x",0)),((LATE,D+FF,D),("x",3*D)),((LATE,2*D+FF,FF),("x",4*D)),((LATE,2*D+2*FF,D),("x",4*D+FF)),
    ((EARLY,D,FEAT),("a_in",0)),((LAST,3*D,D),("x_in",0)),((LATE,3*D+2*FF,FEAT),("a_head",0)),((LATE,3*D+2*FF+FEAT,D),("x_head",0)))
def grads_kernel(zone, ids_ref, owners_ref, *refs):
    operands=refs[:8]; outs=refs[8:12]
    a_all,x_all,a_in,x_in,a_head,x_head,sem=refs[12:]
    buf_of=dict(a=a_all,x=x_all,a_in=a_in,x_in=x_in,a_head=a_head,x_head=x_head)
    seq,core=ids_ref[0],ids_ref[1]
    copies=[]
    for (source,first,count),(buf,at) in PARTS:
        for side in range(2):
            c=pltpu.make_async_copy(operands[2*source+side].at[pl.ds(first,count)],buf_of[buf].at[pl.ds(at,count),pl.ds(side*LANE,LANE)],sem.at[len(copies)])
            c.start(); copies.append(c)
    for c in copies: c.wait()
    lane=lax.broadcasted_iota(jnp.int32,(BLOCK,LANE),1)
    cols=(4*D+FF)//BLOCK; wide_count=D//BLOCK*cols
    def block(slot):
        n=owners_ref[slot]
        i=n//cols; j=n%cols
        m=n-wide_count
        group=jnp.where(j>=3*D//BLOCK,1,0)+jnp.where(j>=4*D//BLOCK,1,0)
        a_at=jnp.where(m<0,i*BLOCK+group*D,3*D+m//(D//BLOCK)*BLOCK)
        x_at=jnp.where(m<0,j*BLOCK,4*D+FF+m%(D//BLOCK)*BLOCK)
        a=a_all[pl.ds(pl.multiple_of(a_at,32),BLOCK),:]
        x=x_all[pl.ds(pl.multiple_of(x_at,32),BLOCK),:]
        w=lax.dot_general(a,x,(((1,),(1,)),((),())),preferred_element_type=F32)
        return jnp.concatenate([w,jnp.zeros((BLOCK,LANE-BLOCK),F32)],axis=1)
    for out,h,first,step in ((outs[0],0,2,1),(outs[2],1,1,2),(outs[1],0,0,1),(outs[3],1,0,2)):
        def one(j,carry,out=out,h=h,first=first,step=step):
            device=2*jnp.bitwise_xor(seq,zone*4+first+step*j)+core
            codes=[]
            for g in range(3):
                w=[block(device*24+(h*3+g)*4+t) for t in range(4)]
                for v in range(3):
                    tile=jnp.where(lane<BLOCK,w[v],pltpu.roll(w[3],BLOCK-32*v,1))
                    for half in range(2):
                        q,code=encode(tile[half*GROUP:(half+1)*GROUP])
                        at=((g*3+v)*2+half)*GROUP
                        out[j,at:at+GROUP,:]=q; codes.append(code)
            a_ref,x_ref=((a_in,x_in),(a_head,x_head))[h]
            w=lax.dot_general(a_ref[pl.ds(pl.multiple_of(device*IO,16),IO),:],x_ref[...],(((1,),(1,)),((),())),preferred_element_type=F32)
            for v in range(6):
                q,code=encode(w[:,v*LANE:(v+1)*LANE])
                at=(18+v)*GROUP
                out[j,at:at+GROUP,:]=q; codes.append(code)
            out[j,UNITS*GROUP:,:]=pack_codes(codes)
            return carry
        lax.fori_loop(0,2,one,0)

def weight_grads(zone, ids, owners, operands):
    n=len(operands)
    return pl.pallas_call(partial(grads_kernel,zone),
        out_shape=[jax.ShapeDtypeStruct((2,PART,LANE),I16)]*4,
        in_specs=[pl.BlockSpec(memory_space=pltpu.SMEM)]*2+[pl.BlockSpec(memory_space=pl.ANY)]*n,
        out_specs=[pl.BlockSpec(memory_space=pltpu.VMEM)]*4,
        scratch_shapes=[pltpu.VMEM((A_ROWS,2*LANE),BF),pltpu.VMEM((X_ROWS,2*LANE),BF),pltpu.VMEM((FEAT,2*LANE),BF),pltpu.VMEM((D,2*LANE),BF),
            pltpu.VMEM((FEAT,2*LANE),BF),pltpu.VMEM((D,2*LANE),BF),pltpu.SemaphoreType.DMA((2*len(PARTS),))],
        compiler_params=pltpu.CompilerParams(vmem_limit_bytes=40<<20), cost_estimate=takes(0.8), name="weight_grads")(ids,owners,*operands)

class At:
    def __init__(s,ref,*i): s.ref,s.i=ref,i
    def __getitem__(s,k): return s.ref[(*s.i,k,slice(None))]
    def __setitem__(s,k,v): s.ref[(*s.i,k,slice(None))]=v
def summed(views):
    scales=[scale_of(v[UNITS*GROUP:PART]) for v in views]
    for k in range(UNITS):
        total=None
        for v,s in zip(views,scales):
            x=v[k*GROUP:(k+1)*GROUP].astype(jnp.int32).astype(F32)*s[k:k+1,:]
            total=x if total is None else total+x
        yield k,total
def add_codes(views, out):
    codes=[]
    for k,total in summed(views):
        q,code=encode(total)
        out[k*GROUP:(k+1)*GROUP]=q
        codes.append(code)
    out[UNITS*GROUP:PART]=pack_codes(codes)
def takes(micros):
    return pl.CostEstimate(flops=0,transcendentals=0,bytes_accessed=int(micros*3.3e6))
def code_call(kernel, name, outs, *args):
    return pl.pallas_call(kernel, out_shape=[jax.ShapeDtypeStruct(s,t) for s,t in outs],
        in_specs=[pl.BlockSpec(memory_space=pltpu.VMEM)]*len(args), out_specs=[pl.BlockSpec(memory_space=pltpu.VMEM)]*len(outs),
        compiler_params=pltpu.CompilerParams(vmem_limit_bytes=32<<20), cost_estimate=takes(0.15), name=name)(*args)
def plane_kernel(*refs):
    n=len(refs)//2
    for i in range(0,n,2):
        (keep,got),(send,stay)=refs[i:i+2],refs[n+i:n+i+2]
        add_codes([At(keep,1),At(got,1)],At(send))
        add_codes([At(keep,0),At(got,0)],At(stay))
def line_kernel(*refs):
    stay_a,got_a,stay_b,got_b=refs[:4]; more=refs[4:-1]; out=refs[-1]
    for h,(stay,got) in enumerate(((stay_a,got_a),(stay_b,got_b))):
        add_codes([At(stay),At(got)]+[At(m,h) for m in more],At(out,h))
def final_kernel(*refs):
    stay_a,got_a,stay_b,got_b=refs[:4]; more=refs[4:-4]; vec,blocks,io,sums=refs[-4:]
    square=jnp.zeros((1,LANE),F32)
    for h,(stay,got) in enumerate(((stay_a,got_a),(stay_b,got_b))):
        for k,total in summed([At(stay),At(got)]+[At(m,h) for m in more]):
            square=square+jnp.sum(total*total,axis=0,keepdims=True)
            if k<18:
                g,v,half=k//6,k//2%3,k%2
                rows=slice(half*GROUP,(half+1)*GROUP)
                blocks[(h*3+g)*4+v,rows,:]=total[:,:BLOCK]
                blocks[(h*3+g)*4+3,rows,32*v:32*(v+1)]=total[:,BLOCK:]
            else:
                io[:,h,(k-18)*LANE:(k-17)*LANE]=total
    sums[0:23,:]=vec[0:23,:]
    sums[23:24,:]=jnp.broadcast_to(jnp.sum(square,keepdims=True),(1,D))
HALF=(PART,LANE)
def reduce_tree(ids, owners, operands, vec):
    send={}; keep={}; got={}; stay={}; far={}
    def make(k):
        send_a,keep_a,send_b,keep_b=weight_grads(k,ids,owners,operands)
        send[k]=(send_a,send_b); keep[k]=(keep_a,keep_b)
    def leave(k,*masks):
        got[k]=tuple(swap(part,"seq",mask) for part,mask in zip(send[k],masks))
    def plane(*pieces):
        outs=code_call(plane_kernel,"add_plane",[(HALF,I16)]*4*len(pieces),*[ref for k in pieces for ref in (keep[k][0],got[k][0],keep[k][1],got[k][1])])
        for i,k in enumerate(pieces):
            send_a,stay_a,send_b,stay_b=outs[4*i:4*i+4]
            stay[k]=(stay_a,stay_b); send[k]=(send_a,send_b)
            leave(k,1,2)
    def line(k,mask,*more):
        far[k]=swap(code_call(line_kernel,"add_line",[((2,)+HALF,I16)],stay[k][0],got[k][0],stay[k][1],got[k][1],*more)[0],"seq",mask)
    make(3); leave(3,2,1)
    make(2); leave(2,2,1)
    make(1)
    (got[3],got[2]),keep[1]=gate((got[3],got[2]),keep[1])
    plane(3,2)
    (send[1],ids),got[3],got[2]=gate((send[1],ids),got[3],got[2])
    line(3,4)
    leave(1,2,1)
    make(0)
    got[1],far[3],keep[0]=gate(got[1],far[3],keep[0])
    line(2,8,far[3])
    plane(1)
    line(1,4)
    send[0],got[1]=gate(send[0],got[1])
    leave(0,2,1)
    plane(0)
    return code_call(final_kernel,"add_final",[((24,BLOCK,BLOCK),F32),((IO,2,D),F32),((24,D),F32)],stay[0][0],got[0][0],stay[0][1],got[0][1],far[1],far[2],vec)

BLOCK=96; NEWTON=6; F32=jnp.float32; BF=jnp.bfloat16; LANE=128
def halves(x):
    hi=x.astype(BF); return hi,(x-hi.astype(F32)).astype(BF)
def left_of(x):
    hi,lo=halves(x)
    return jnp.concatenate([hi,lo],axis=1)
def right_of(x):
    hi,lo=halves(x)
    zero=jnp.zeros_like(lo)
    return jnp.concatenate([jnp.concatenate([hi,lo],axis=1),jnp.concatenate([hi,zero],axis=1)],axis=0)
def times(a,b):
    w=jnp.dot(a,b,preferred_element_type=F32)
    n=w.shape[1]//2
    return w[:,:n]+w[:,n:]
def shampoo_kernel(sums_ref, grad_ref, left_ref, right_ref, block_ref, io_grad_ref, io_ref, io_first_ref, io_second_ref, vec_ref, vec_first_ref, vec_second_ref,
                   grad_out, left_out, right_out, block_out, io_first_out, io_second_out, io_out, vec_first_out, vec_second_out, vec_out, norm_out, *, beta, rate, eps, n_side):
    n_vec=vec_ref.shape[0]
    vec_grad=sums_ref[0:n_vec,:]
    norm=jnp.sqrt(sums_ref[23:24,0:1]+jnp.sum(vec_grad*vec_grad,keepdims=True))
    norm_out[...]=jnp.broadcast_to(norm,norm_out.shape)
    factor=jnp.minimum(1.0,clip_limit/norm)
    vec_first_out[...],vec_second_out[...],vec_out[...]=adam_update(vec_ref[...],vec_first_ref[...],vec_second_ref[...],vec_grad*factor,rate_vector,0.0)
    for m in range(2):
        parts=[ref[:,m,:] for ref in (io_ref,io_first_ref,io_second_ref,io_grad_ref)]
        io_first_out[:,m,:],io_second_out[:,m,:],io_out[:,m,:]=adam_update(*parts[:3],parts[3]*factor,rate_adam,weight_decay)
    side=LANE
    row=lax.broadcasted_iota(jnp.int32,(side,side),0); col=lax.broadcasted_iota(jnp.int32,(side,side),1)
    eye=jnp.where((row==col)&(row<BLOCK),1.0,0.0)
    def full(x):
        x=jnp.concatenate([x,jnp.zeros((BLOCK,side-BLOCK),F32)],axis=1)
        return jnp.concatenate([x,jnp.zeros((side-BLOCK,side),F32)],axis=0)
    def one(i,carry):
        grads=[full(grad_ref[i*n_side+j]*factor) for j in range(n_side)]
        flipped=[g.T for g in grads]
        stats=[]
        for j in range(n_side):
            s=i*n_side+j
            gl,gr=left_of(grads[j]),right_of(grads[j]); tl,tr=left_of(flipped[j]),right_of(flipped[j])
            l=beta*full(left_ref[s])+(1.0-beta)*times(gl,tr)
            r=beta*full(right_ref[s])+(1.0-beta)*times(tl,gr)
            grad_out[s]=grads[j][:BLOCK,:BLOCK]; left_out[s]=l[:BLOCK,:BLOCK]; right_out[s]=r[:BLOCK,:BLOCK]
            stats+=[l,r]
        n=len(stats)
        regular=[m+eps*eye for m in stats]
        scaled=[2.5*lax.rsqrt(jnp.sum(m*m,keepdims=True)) for m in regular]
        moving=[m*s for m,s in zip(regular,scaled)]
        root=[None]*n
        for sweep in range(NEWTON):
            factors=[(5.0*eye-m)*0.25 for m in moving]
            fl=[left_of(f) for f in factors]; fr=[right_of(f) for f in factors]
            if sweep==0: root=[f*jnp.sqrt(jnp.sqrt(s)) for f,s in zip(factors,scaled)]
            else: root=[times(left_of(x),f) for x,f in zip(root,fr)]
            if sweep<NEWTON-1:
                square=[times(a,b) for a,b in zip(fl,fr)]
                fourth=[times(left_of(q),right_of(q)) for q in square]
                moving=[times(left_of(q),right_of(m)) for q,m in zip(fourth,moving)]
        for j in range(n_side):
            s=i*n_side+j
            d=times(left_of(root[2*j]),right_of(grads[j]))
            d=times(left_of(d),right_of(root[2*j+1]))
            block_out[s]=block_ref[s]-rate*d[:BLOCK,:BLOCK]
        return carry
    lax.fori_loop(0,grad_ref.shape[0]//n_side,one,0)
def update_step(sums, grads, left, right, blocks, io_grad, io_set, vec_set, n_side=8):
    like=lambda *xs: [jax.ShapeDtypeStruct(x.shape,F32) for x in xs]
    args=(sums,grads,left,right,blocks,io_grad,*io_set,*vec_set)
    return pl.pallas_call(partial(shampoo_kernel,beta=beta_stat,rate=rate_shampoo,eps=root_eps,n_side=n_side),
        out_shape=like(grads,grads,grads,grads,*io_set,*vec_set)+[jax.ShapeDtypeStruct((8,LANE),F32)],
        in_specs=[vmem()]*len(args),out_specs=[vmem()]*11,
        compiler_params=pltpu.CompilerParams(vmem_limit_bytes=48<<20),name="update_step")(*args)


def fits(mesh):
    return mesh.shape["seq"] == 16 and mesh.shape["opt"] == 2


def sum_everywhere(value):
    value = value + swap(value, "opt", 1)
    for bit in range((lax.axis_size("seq") - 1).bit_length()):
        value = value + swap(value, "seq", 2**bit)
    return value


def to_heads(parts):
    return lax.all_to_all(parts, "seq", 0, 0, tiled=True)


def evens_first(rows):
    return rows.reshape((rows.shape[0] // 2, 2) + rows.shape[1:]).swapaxes(0, 1).reshape(rows.shape)


def fast_device(
    features,
    tile_mask,
    lengths,
    owners,
    layer_blocks,
    stat_left,
    stat_right,
    io_weights,
    io_first,
    io_second,
    vectors,
    vec_first,
    vec_second,
):
    tok_dev = features.shape[1]
    seq_index = lax.axis_index("seq")
    core_index = lax.axis_index("opt")
    ids = jnp.stack([seq_index, core_index]).astype(jnp.int32)
    low_targets = evens_first(features[0])
    chosen_rows = evens_first(tile_mask[0]).astype(jnp.float32)[:, None]
    lengths_row = lax.dynamic_index_in_dim(lengths, core_index, 0, keepdims=False)
    places = seq_index * tok_dev + evens_first(jnp.arange(tok_dev, dtype=jnp.int32))
    shards = gather_shards(layer_blocks, io_weights, tile_mask)
    block_rows, io_rows = shard_rows(seq_index, core_index)
    qkv_weight, out_weight, in_weight, tile_counts = join_weights(
        FIRST_PLAN, 0, shards, owners, block_rows, io_rows
    )
    tile_count = tile_counts[0, 0]
    hidden, early_low, by_head = front_step(
        low_targets,
        chosen_rows,
        sine_places(slide_offsets(lengths_row, places)),
        vectors,
        in_weight,
        qkv_weight,
        HEADS,
    )
    late_owners, by_head = gate(owners, by_head)
    up_weight, down_weight, head_weight, late_counts = join_weights(
        SECOND_PLAN, 1, shards, late_owners, block_rows, io_rows
    )
    own_head, head_weight = gate(to_heads(by_head), head_weight)
    head_out, mixed_parts, head_totals = attend(lengths, ids, own_head)
    mixed_low = to_heads(mixed_parts).reshape(D, tok_dev)
    grad_middle, grad_mixed, late_low, late_rows = mlp_step(
        tile_count,
        hidden,
        mixed_low,
        low_targets,
        chosen_rows,
        vectors,
        out_weight,
        up_weight,
        down_weight,
        head_weight,
    )
    grad_head_out = to_heads(grad_mixed.reshape(HEADS, HEAD_DIM, tok_dev))
    grad_parts = attend_back(lengths, ids, own_head, grad_head_out, head_out, head_totals)
    others = [swap(operand, "opt", 1) for operand in (early_low, mixed_low, late_low)]
    own_parts, others[0], others[1] = gate(to_heads(grad_parts), others[0], others[1])
    last_low, vec_grads = input_step(
        own_parts,
        hidden,
        grad_middle,
        chosen_rows,
        vectors,
        late_rows,
        qkv_weight,
        in_weight,
    )
    others.append(swap(last_low, "opt", 1))
    operands = []
    for pair in zip((early_low, mixed_low, late_low, last_low), others):
        operands += pair
    slot_sum, io_sum, own_sums = reduce_tree(ids, owners, operands, vec_grads)
    all_sums = sum_everywhere(own_sums)
    (
        block_grads,
        left_new,
        right_new,
        blocks_new,
        io_first_new,
        io_second_new,
        io_new,
        vec_first_new,
        vec_second_new,
        vec_new,
        norms,
    ) = update_step(
        all_sums,
        slot_sum,
        stat_left,
        stat_right,
        layer_blocks,
        io_sum,
        (io_weights, io_first, io_second),
        (vectors, vec_first, vec_second),
    )
    grad_norm = norms[0, 0]
    error_sum = all_sums[vectors.shape[0], 0]
    return (
        grad_norm,
        error_sum,
        tile_count,
        block_grads,
        left_new,
        right_new,
        blocks_new,
        io_first_new,
        io_second_new,
        io_new,
        vec_first_new,
        vec_second_new,
        vec_new,
    )


def solution(mesh):
    return jax.shard_map(
        fast_device if fits(mesh) else per_device,
        mesh=mesh,
        in_specs=(
            P("opt", "seq", None),
            P("opt", "seq"),
            P(),
            P(),
            P(("seq", "opt"), None, None),
            P(("seq", "opt"), None, None),
            P(("seq", "opt"), None, None),
            P(("seq", "opt"), None, None),
            P(("seq", "opt"), None, None),
            P(("seq", "opt"), None, None),
            P(),
            P(),
            P(),
        ),
        out_specs=(
            P(),
            P(),
            P(),
            P(("seq", "opt"), None, None),
            P(("seq", "opt"), None, None),
            P(("seq", "opt"), None, None),
            P(("seq", "opt"), None, None),
            P(("seq", "opt"), None, None),
            P(("seq", "opt"), None, None),
            P(("seq", "opt"), None, None),
            P(),
            P(),
            P(),
        ),
        check_vma=False,
    )
```

profile of v0, /device:TPU:0, one launch (start us, length us, event | category | flops | bytes accessed | tf_op | source)
XLA Modules:
  0.0 410.0 jit_solution(11544878268079832129)
XLA Ops:
  2.7 2.6 pack_shard.1
  5.2 4.0 collective-permute-start.7
  9.3 1.6 collective-permute-start.4
  10.9 1.5 collective-permute-start
  12.3 1.5 collective-permute-start.1
  13.9 1.9 constant_dynamic-update-slice_fusion.4
  15.8 4.7 %collective-permute-done.1 = bf16[1168,128]{1,0:T(8,128)(2,1)S(1)} collective-permute-done((bf16[1168,128]{1,0:T(8,128)(2,1)}, bf16[1168,128]{1,0:T(8,128)(2,1)S(1)}, u32[]{:S(2)}, u32[]{:S(2)}) %collective-permute-start.1) | collective-permute-done | bytes 299040 | tf_op jit(solution)/shard_map/ppermute | solution.py:564
  22.2 1.6 collective-permute-start.2
  25.3 10.6 %collective-permute-done.7 = bf16[2336,128]{1,0:T(8,128)(2,1)S(1)} collective-permute-done((bf16[2336,128]{1,0:T(8,128)(2,1)}, bf16[2336,128]{1,0:T(8,128)(2,1)S(1)}, u32[]{:S(2)}, u32[]{:S(2)}) %collective-permute-start.7) | collective-permute-done | bytes 598048 | tf_op jit(solution)/shard_map/ppermute | solution.py:564
  36.0 1.6 collective-permute-start.9
  37.6 1.5 collective-permute-start.8
  43.6 2.4 collective-permute-done.9
  46.7 4.0 collective-permute-done.6
  51.6 2.5 collective-permute-done.10
  54.4 1.6 collective-permute-start.16
  56.6 1.5 collective-permute-start.14
  61.0 3.5 collective-permute-done.16
  68.2 9.1 %collective-permute-done.13 = bf16[2336,128]{1,0:T(8,128)(2,1)S(1)} collective-permute-done((bf16[2336,128]{1,0:T(8,128)(2,1)S(1)}, bf16[2336,128]{1,0:T(8,128)(2,1)S(1)}, u32[]{:S(2)}, u32[]{:S(2)}) %collective-permute-start.13) | collective-permute-done | bytes 598048 | tf_op jit(solution)/shard_map/ppermute | solution.py:564
  77.3 1.5 collective-permute-start.17
  79.7 10.5 %collective-permute-done.11 = bf16[2336,128]{1,0:T(8,128)(2,1)S(1)} collective-permute-done((bf16[2336,128]{1,0:T(8,128)(2,1)S(1)}, bf16[2336,128]{1,0:T(8,128)(2,1)S(1)}, u32[]{:S(2)}, u32[]{:S(2)}) %collective-permute-start.11) | collective-permute-done | bytes 598048 | tf_op jit(solution)/shard_map/ppermute | solution.py:564
  92.5 6.9 %collective-permute-done.17 = bf16[2336,128]{1,0:T(8,128)(2,1)S(1)} collective-permute-done((bf16[2336,128]{1,0:T(8,128)(2,1)S(1)}, bf16[2336,128]{1,0:T(8,128)(2,1)S(1)}, u32[]{:S(2)}, u32[]{:S(2)}) %collective-permute-start.17) | collective-permute-done | bytes 598048 | tf_op jit(solution)/shard_map/ppermute | solution.py:564
  106.5 14.2 %join_weights.2 = (bf16[768,2304]{1,0:T(8,128)(2,1)}, bf16[768,768]{1,0:T(8,128)(2,1)}, bf16[1536,768]{1,0:T(8,128)(2,1)}, f32[16,128]{1,0:T(8,128)S(1)}) custom-call(s32[768]{0:T(1024)S(1)} %copy-done.16, s32[768]{0:T(1024)S(1)} %add_select_fusion.10.row_ref, s32[2,32]{1,0:T(2,128)S(1)} %pad_add_fusion.io_ref, ...), custom_call_target="tpu_custom_call" | custom-call | bytes 42900000 | tf_op jit(solution)/shard_map/join_weights/pallas_call | solution.py:703
  120.7 4.8 %front_step.1 = (f32[128,768]{1,0:T(8,128)}, bf16[2304,128]{1,0:T(8,128)(2,1)}, bf16[16,144,128]{2,1,0:T(8,128)(2,1)}) custom-call(bf16[128,1536]{1,0:T(8,128)(2,1)} %bitcast.32, f32[128,1]{1,0:T(8,128)} %convert_element_type.35.refs_1_.refs_4_.refs_3_, f32[128,768]{1,0:T(8,128)} %pad_maximum_fusion.8.refs_2_, f32[19,768]{1,0:T(8,128)} %vec_ref.1, ...), custom_call_target="tpu_custom_call" | custom-call | bytes 16500000 | tf_op jit(solution)/shard_map/front_step/pallas_call | solution.py:605
  125.5 7.7 %all-to-all-start = ((bf16[16,144,128]{2,1,0:T(8,128)(2,1)}), bf16[16,144,128]{2,1,0:T(8,128)(2,1)S(1)}, u32[]{:S(2)}, u32[]{:S(2)}) async-start(bf16[16,144,128]{2,1,0:T(8,128)(2,1)} %get-tuple-element.125), calls=%async_computation | async-start | bytes 1179648 | tf_op jit(solution)/shard_map/all_to_all | solution.py:1260
  133.3 18.1 %join_weights.3 = (bf16[768,3072]{1,0:T(8,128)(2,1)}, bf16[3072,768]{1,0:T(8,128)(2,1)}, bf16[1536,768]{1,0:T(8,128)(2,1)}, f32[16,128]{1,0:T(8,128)}) custom-call(s32[768]{0:T(1024)S(1)} %copy-done.16, s32[768]{0:T(1024)S(1)} %add_select_fusion.10.row_ref, s32[2,32]{1,0:T(2,128)S(1)} %pad_add_fusion.io_ref, ...), custom_call_target="tpu_custom_call" | custom-call | bytes 56100000 | tf_op jit(solution)/shard_map/join_weights/pallas_call | solution.py:703
  152.3 12.6 %attend_forward.1 = (f32[48,2048]{1,0:T(8,128)}, bf16[16,48,128]{2,1,0:T(8,128)(2,1)}, f32[8,2048]{1,0:T(8,128)}) custom-call(s32[2,4]{1,0:T(2,128)S(1)} %copy-done.20, s32[2]{0:T(128)S(1)} %pad_add_fusion.1.refs_1_.ids_ref, bf16[16,144,128]{2,1,0:T(8,128)(2,1)} %copy-done.22), custom_call_target="tpu_custom_call" | custom-call | bytes 33000000 | tf_op jit(solution)/shard_map/attend_forward/pallas_call | solution.py:605
  164.9 7.2 %all-to-all-start.1 = ((bf16[16,48,128]{2,1,0:T(8,128)(2,1)}), bf16[16,48,128]{2,1,0:T(8,128)(2,1)S(1)}, u32[]{:S(2)}, u32[]{:S(2)}) async-start(bf16[16,48,128]{2,1,0:T(8,128)(2,1)} %get-tuple-element.131), calls=%async_computation.1 | async-start | bytes 393216 | tf_op jit(solution)/shard_map/all_to_all | solution.py:1260
  172.6 7.9 %all-to-all-done.1 = bf16[16,48,128]{2,1,0:T(8,128)(2,1)S(1)} async-done(((bf16[16,48,128]{2,1,0:T(8,128)(2,1)}), bf16[16,48,128]{2,1,0:T(8,128)(2,1)S(1)}, u32[]{:S(2)}, u32[]{:S(2)}) %all-to-all-start.1) | async-done | bytes 196640 | tf_op jit(solution)/shard_map/all_to_all | solution.py:1260
  181.2 14.4 %mlp_step.1 = (f32[128,768]{1,0:T(8,128)}, bf16[768,128]{1,0:T(8,128)(2,1)}, bf16[10752,128]{1,0:T(8,128)(2,1)}, f32[16,768]{1,0:T(8,128)}) custom-call(f32[1]{0:T(128)} %bitcast.11.refs_0_, f32[128,768]{1,0:T(8,128)} %get-tuple-element.130.refs_1_, bf16[768,128]{1,0:T(8,128)(2,1)} %bitcast.26, bf16[128,1536]{1,0:T(8,128)(2,1)} %bitcast.33, ...), custom_call_target="tpu_custom_call" | custom-call | bytes 42900000 | tf_op jit(solution)/shard_map/mlp_step/pallas_call | solution.py:605
  195.8 13.3 %all_to_all.20.refs_3_ = bf16[16,48,128]{2,1,0:T(8,128)(2,1)} all-to-all(bf16[16,48,128]{2,1,0:T(8,128)(2,1)} %bitcast.34), channel_id=1, replica_groups=mesh['seq'=16,'opt'=2] {'seq'}, dimensions={0} | all-to-all | bytes 393216 | tf_op jit(solution)/shard_map/all_to_all | solution.py:1260
  209.1 15.8 %attend_backward.1 = bf16[16,144,128]{2,1,0:T(8,128)(2,1)} custom-call(s32[2,4]{1,0:T(2,128)S(1)} %copy-done.20, s32[2]{0:T(128)S(1)} %pad_add_fusion.1.refs_1_.ids_ref, bf16[16,144,128]{2,1,0:T(8,128)(2,1)} %copy-done.22, bf16[16,48,128]{2,1,0:T(8,128)(2,1)} %all_to_all.20.refs_3_, f32[48,2048]{1,0:T(8,128)} %get-tuple-element.137.refs_4_, ...), custom_call_target="tpu_custom_call" | custom-call | bytes 42900000 | tf_op jit(solution)/shard_map/attend_backward/pallas_call | solution.py:605
  224.9 4.5 %all-to-all-start.3 = ((bf16[16,144,128]{2,1,0:T(8,128)(2,1)}), bf16[16,144,128]{2,1,0:T(8,128)(2,1)}, u32[]{:S(2)}, u32[]{:S(2)}) async-start(bf16[16,144,128]{2,1,0:T(8,128)(2,1)} %attend_backward.1), calls=%async_computation.3 | async-start | bytes 1179648 | tf_op jit(solution)/shard_map/all_to_all | solution.py:1260
  230.0 1.5 collective-permute-done.23.refs_1_
  233.0 12.4 %all-to-all-done.3.refs_0_ = bf16[16,144,128]{2,1,0:T(8,128)(2,1)} async-done(((bf16[16,144,128]{2,1,0:T(8,128)(2,1)}), bf16[16,144,128]{2,1,0:T(8,128)(2,1)}, u32[]{:S(2)}, u32[]{:S(2)}) %all-to-all-start.3) | async-done | bytes 589856 | tf_op jit(solution)/shard_map/all_to_all | solution.py:1260
  245.4 6.9 %input_step.1 = (bf16[3072,128]{1,0:T(8,128)(2,1)}, f32[24,768]{1,0:T(8,128)}) custom-call(bf16[16,144,128]{2,1,0:T(8,128)(2,1)} %all-to-all-done.3.refs_0_, f32[128,768]{1,0:T(8,128)} %get-tuple-element.130.refs_1_, f32[128,768]{1,0:T(8,128)} %get-tuple-element.143.refs_2_, f32[128,1]{1,0:T(8,128)} %convert_element_type.35.refs_1_.refs_4_.refs_3_, ...), custom_call_target="tpu_custom_call" | custom-call | bytes 16500000 | tf_op jit(solution)/shard_map/input_step/pallas_call | solution.py:605
  252.4 2.5 collective-permute-done.26.refs_7_
  256.0 6.9 %weight_grads.6 = (s16[2,1184,128]{2,1,0:T(8,128)(2,1)S(1)}, s16[2,1184,128]{2,1,0:T(8,128)(2,1)S(1)}, s16[2,1184,128]{2,1,0:T(8,128)(2,1)S(1)}, s16[2,1184,128]{2,1,0:T(8,128)(2,1)S(1)}) custom-call(s32[2]{0:T(128)S(1)} %pad_add_fusion.1.refs_1_.ids_ref, s32[768]{0:T(1024)S(1)} %copy-done.16, bf16[2304,128]{1,0:T(8,128)(2,1)S(1)} %copy-done.2, ...), custom_call_target="tpu_custom_call" | custom-call | bytes 2640000 | tf_op jit(solution)/shard_map/weight_grads/pallas_call | solution.py:1084
  264.7 7.3 %weight_grads.5 = (s16[2,1184,128]{2,1,0:T(8,128)(2,1)S(1)}, s16[2,1184,128]{2,1,0:T(8,128)(2,1)S(1)}, s16[2,1184,128]{2,1,0:T(8,128)(2,1)S(1)}, s16[2,1184,128]{2,1,0:T(8,128)(2,1)S(1)}) custom-call(s32[2]{0:T(128)S(1)} %pad_add_fusion.1.refs_1_.ids_ref, s32[768]{0:T(1024)S(1)} %copy-done.16, bf16[2304,128]{1,0:T(8,128)(2,1)S(1)} %copy-done.2, ...), custom_call_target="tpu_custom_call" | custom-call | bytes 2640000 | tf_op jit(solution)/shard_map/weight_grads/pallas_call | solution.py:1084
  273.0 1.5 collective-permute-start.28
  274.5 6.9 %weight_grads.4 = (s16[2,1184,128]{2,1,0:T(8,128)(2,1)S(1)}, s16[2,1184,128]{2,1,0:T(8,128)(2,1)S(1)}, s16[2,1184,128]{2,1,0:T(8,128)(2,1)S(1)}, s16[2,1184,128]{2,1,0:T(8,128)(2,1)S(1)}) custom-call(s32[2]{0:T(128)S(1)} %pad_add_fusion.1.refs_1_.ids_ref, s32[768]{0:T(1024)S(1)} %copy-done.16, bf16[2304,128]{1,0:T(8,128)(2,1)S(1)} %copy-done.2, ...), custom_call_target="tpu_custom_call" | custom-call | bytes 2640000 | tf_op jit(solution)/shard_map/weight_grads/pallas_call | solution.py:1084
  281.5 10.3 %collective-permute-done.27.refs_1_ = s16[2,1184,128]{2,1,0:T(8,128)(2,1)S(1)} collective-permute-done((s16[2,1184,128]{2,1,0:T(8,128)(2,1)S(1)}, s16[2,1184,128]{2,1,0:T(8,128)(2,1)S(1)}, u32[]{:S(2)}, u32[]{:S(2)}) %collective-permute-start.27) | collective-permute-done | bytes 606240 | tf_op jit(solution)/shard_map/ppermute | solution.py:564
  292.5 2.6 add_plane.3
  296.7 1.5 collective-permute-start.33
  299.3 6.1 %collective-permute-done.31.refs_1_ = s16[1184,128]{1,0:T(8,128)(2,1)S(1)} collective-permute-done((s16[1184,128]{1,0:T(8,128)(2,1)S(1)}, s16[1184,128]{1,0:T(8,128)(2,1)S(1)}, u32[]{:S(2)}, u32[]{:S(2)}) %collective-permute-start.31) | collective-permute-done | bytes 303136 | tf_op jit(solution)/shard_map/ppermute | solution.py:564
  305.9 3.9 collective-permute-done.33.refs_1_
  311.0 1.5 collective-permute-start.36
  313.2 1.5 collective-permute-start.37
  314.7 7.1 %weight_grads.7 = (s16[2,1184,128]{2,1,0:T(8,128)(2,1)S(1)}, s16[2,1184,128]{2,1,0:T(8,128)(2,1)S(1)}, s16[2,1184,128]{2,1,0:T(8,128)(2,1)S(1)}, s16[2,1184,128]{2,1,0:T(8,128)(2,1)S(1)}) custom-call(s32[2]{0:T(128)S(1)} %pad_add_fusion.1.refs_1_.ids_ref, s32[768]{0:T(1024)S(1)} %copy-done.16, bf16[2304,128]{1,0:T(8,128)(2,1)S(1)} %copy-done.2, ...), custom_call_target="tpu_custom_call" | custom-call | bytes 2640000 | tf_op jit(solution)/shard_map/weight_grads/pallas_call | solution.py:1084
  321.8 1.6 collective-permute-done.35.refs_1_
  324.1 1.9 collective-permute-done.37.refs_4_
  329.0 6.3 %collective-permute-done.38.refs_1_ = s16[1184,128]{1,0:T(8,128)(2,1)S(1)} collective-permute-done((s16[1184,128]{1,0:T(8,128)(2,1)S(1)}, s16[1184,128]{1,0:T(8,128)(2,1)S(1)}, u32[]{:S(2)}, u32[]{:S(2)}) %collective-permute-start.38) | collective-permute-done | bytes 303136 | tf_op jit(solution)/shard_map/ppermute | solution.py:564
  335.3 2.1 collective-permute-done.39.refs_3_
  338.4 1.5 collective-permute-start.41
  342.2 2.1 collective-permute-start.44
  344.3 4.2 %collective-permute-done.40.refs_1_ = s16[2,1184,128]{2,1,0:T(8,128)(2,1)S(1)} collective-permute-done((s16[2,1184,128]{2,1,0:T(8,128)(2,1)S(1)}, s16[2,1184,128]{2,1,0:T(8,128)(2,1)S(1)}, u32[]{:S(2)}, u32[]{:S(2)}) %collective-permute-start.40) | collective-permute-done | bytes 606240 | tf_op jit(solution)/shard_map/ppermute | solution.py:564
  348.5 2.6 collective-permute-done.41.refs_3_
  352.6 1.6 collective-permute-start.42
  354.9 7.1 %collective-permute-done.45.refs_5_ = s16[2,1184,128]{2,1,0:T(8,128)(2,1)S(1)} collective-permute-done((s16[2,1184,128]{2,1,0:T(8,128)(2,1)S(1)}, s16[2,1184,128]{2,1,0:T(8,128)(2,1)S(1)}, u32[]{:S(2)}, u32[]{:S(2)}) %collective-permute-start.45) | collective-permute-done | bytes 606240 | tf_op jit(solution)/shard_map/ppermute | solution.py:564
  365.7 3.1 collective-permute-done.47
  369.8 3.4 collective-permute-done.48
  373.8 3.9 collective-permute-done.49
  377.7 2.2 collective-permute-start.50
  379.9 3.9 collective-permute-done.50
  384.4 24.9 %update_step.1 = (f32[24,96,96]{2,1,0:T(8,128)}, f32[24,96,96]{2,1,0:T(8,128)}, f32[24,96,96]{2,1,0:T(8,128)}, f32[24,96,96]{2,1,0:T(8,128)}, f32[48,2,768]{2,1,...) custom-call(f32[24,768]{1,0:T(8,128)S(1)} %add.264.sums_ref, ...), custom_call_target="tpu_custom_call" | custom-call | tf_op jit(solution)/shard_map/update_step/pallas_call | solution.py:1242
  (180 shorter events, 58.4 us)
Async XLA Ops:
  5.2 30.7 %collective-permute-start.7 = (bf16[2336,128]{1,0:T(8,128)(2,1)}, bf16[2336,128]{1,0:T(8,128)(2,1)S(1)}, u32[]{:S(2)}, u32[]{:S(2)}) collective-permute-start(bf16[2336,128]{1,0:T(8,128)(2,1)} %get-tuple-element.113), channel_id=1, source_target_pairs={{0,16},{2,18},{4,20},{6,22},{8,24},{10,26},{12,28},{14,30},{16,0},... | collective-permute-start | bytes 1794056 | tf_op jit(solution)/shard_map/ppermute | solution.py:564
  9.3 29.8 %collective-permute-start.4 = (bf16[2336,128]{1,0:T(8,128)(2,1)}, bf16[2336,128]{1,0:T(8,128)(2,1)S(1)}, u32[]{:S(2)}, u32[]{:S(2)}) collective-permute-start(bf16[2336,128]{1,0:T(8,128)(2,1)} %get-tuple-element.113), channel_id=1, source_target_pairs={{0,8},{2,10},{4,12},{6,14},{8,0},{10,2},{12,4},{14,6},{16,24},{18,... | collective-permute-start | bytes 1794056 | tf_op jit(solution)/shard_map/ppermute | solution.py:564
  10.9 11.3 %collective-permute-start = (bf16[1168,128]{1,0:T(8,128)(2,1)}, bf16[1168,128]{1,0:T(8,128)(2,1)S(1)}, u32[]{:S(2)}, u32[]{:S(2)}) collective-permute-start(bf16[1168,128]{1,0:T(8,128)(2,1)} %get-tuple-element.114), channel_id=1, source_target_pairs={{0,2},{2,0},{4,6},{6,4},{8,10},{10,8},{12,14},{14,12},{16,18},{18,... | collective-permute-start | bytes 897032 | tf_op jit(solution)/shard_map/ppermute | solution.py:564
  12.3 8.2 %collective-permute-start.1 = (bf16[1168,128]{1,0:T(8,128)(2,1)}, bf16[1168,128]{1,0:T(8,128)(2,1)S(1)}, u32[]{:S(2)}, u32[]{:S(2)}) collective-permute-start(bf16[1168,128]{1,0:T(8,128)(2,1)} %get-tuple-element.115), channel_id=1, source_target_pairs={{0,4},{2,6},{4,0},{6,2},{8,12},{10,14},{12,8},{14,10},{16,20},{18,... | collective-permute-start | bytes 897032 | tf_op jit(solution)/shard_map/ppermute | solution.py:564
  21.6 20.7 %collective-permute-start.3 = (bf16[2336,128]{1,0:T(8,128)(2,1)S(1)}, bf16[2336,128]{1,0:T(8,128)(2,1)S(1)}, u32[]{:S(2)}, u32[]{:S(2)}) collective-permute-start(bf16[2336,128]{1,0:T(8,128)(2,1)S(1)} %pad_maximum_fusion.1), channel_id=1, source_target_pairs={{0,2},{2,0},{4,6},{6,4},{8,10},{10,8},{12,14},{14,12},{16,18},{18,... | collective-permute-start | bytes 1794056 | tf_op jit(solution)/shard_map/ppermute | solution.py:564
  22.2 18.4 %collective-permute-start.2 = (bf16[2336,128]{1,0:T(8,128)(2,1)S(1)}, bf16[2336,128]{1,0:T(8,128)(2,1)S(1)}, u32[]{:S(2)}, u32[]{:S(2)}) collective-permute-start(bf16[2336,128]{1,0:T(8,128)(2,1)S(1)} %pad_maximum_fusion), channel_id=1, source_target_pairs={{0,4},{2,6},{4,0},{6,2},{8,12},{10,14},{12,8},{14,10},{16,20},{18,... | collective-permute-start | bytes 1794056 | tf_op jit(solution)/shard_map/ppermute | solution.py:564
  36.0 10.1 %collective-permute-start.9 = (bf16[1168,128]{1,0:T(8,128)(2,1)S(1)}, bf16[1168,128]{1,0:T(8,128)(2,1)S(1)}, u32[]{:S(2)}, u32[]{:S(2)}) collective-permute-start(bf16[1168,128]{1,0:T(8,128)(2,1)S(1)} %get-tuple-element.215), channel_id=1, source_target_pairs={{0,4},{2,6},{4,0},{6,2},{8,12},{10,14},{12,8},{14,10},{16,20},{18,... | collective-permute-start | bytes 897032 | tf_op jit(solution)/shard_map/ppermute | solution.py:564
  37.6 9.1 %collective-permute-start.8 = (bf16[1168,128]{1,0:T(8,128)(2,1)S(1)}, bf16[1168,128]{1,0:T(8,128)(2,1)S(1)}, u32[]{:S(2)}, u32[]{:S(2)}) collective-permute-start(bf16[1168,128]{1,0:T(8,128)(2,1)S(1)} %get-tuple-element.216), channel_id=1, source_target_pairs={{0,2},{2,0},{4,6},{6,4},{8,10},{10,8},{12,14},{14,12},{16,18},{18,... | collective-permute-start | bytes 897032 | tf_op jit(solution)/shard_map/ppermute | solution.py:564
  39.1 11.5 %collective-permute-start.6 = (bf16[1168,128]{1,0:T(8,128)(2,1)S(1)}, bf16[1168,128]{1,0:T(8,128)(2,1)S(1)}, u32[]{:S(2)}, u32[]{:S(2)}) collective-permute-start(bf16[1168,128]{1,0:T(8,128)(2,1)S(1)} %get-tuple-element.217), channel_id=1, source_target_pairs={{0,4},{2,6},{4,0},{6,2},{8,12},{10,14},{12,8},{14,10},{16,20},{18,... | collective-permute-start | bytes 897032 | tf_op jit(solution)/shard_map/ppermute | solution.py:564
  40.6 13.6 %collective-permute-start.10 = (bf16[2336,128]{1,0:T(8,128)(2,1)S(1)}, bf16[2336,128]{1,0:T(8,128)(2,1)S(1)}, u32[]{:S(2)}, u32[]{:S(2)}) collective-permute-start(bf16[2336,128]{1,0:T(8,128)(2,1)S(1)} %collective-permute-done.7), channel_id=1, source_target_pairs={{0,8},{2,10},{4,12},{6,14},{8,0},{10,2},{12,4},{14,6},{16,24},{18,... | collective-permute-start | bytes 1794056 | tf_op jit(solution)/shard_map/ppermute | solution.py:564
  42.2 9.4 %collective-permute-start.5 = (bf16[1168,128]{1,0:T(8,128)(2,1)S(1)}, bf16[1168,128]{1,0:T(8,128)(2,1)S(1)}, u32[]{:S(2)}, u32[]{:S(2)}) collective-permute-start(bf16[1168,128]{1,0:T(8,128)(2,1)S(1)} %get-tuple-element.218), channel_id=1, source_target_pairs={{0,2},{2,0},{4,6},{6,4},{8,10},{10,8},{12,14},{14,12},{16,18},{18,... | collective-permute-start | bytes 897032 | tf_op jit(solution)/shard_map/ppermute | solution.py:564
  46.1 59.6 %collective-permute-start.19 = (bf16[9344,128]{1,0:T(8,128)(2,1)}, bf16[9344,128]{1,0:T(8,128)(2,1)}, u32[]{:S(2)}, u32[]{:S(2)}) collective-permute-start(bf16[9344,128]{1,0:T(8,128)(2,1)} %constant_dynamic-update-slice_fusion.refs_0_), channel_id=1, source_target_pairs={{0,1},{1,0},{2,3},{3,2},{4,5},{5,4},{6,7},{7,6},{8,9},{9,8},{10,11... | collective-permute-start | bytes 7176200 | tf_op jit(solution)/shard_map/ppermute | solution.py:564
  54.4 10.1 %collective-permute-start.16 = (bf16[1168,128]{1,0:T(8,128)(2,1)S(1)}, bf16[1168,128]{1,0:T(8,128)(2,1)S(1)}, u32[]{:S(2)}, u32[]{:S(2)}) collective-permute-start(bf16[1168,128]{1,0:T(8,128)(2,1)S(1)} %get-tuple-element.213), channel_id=1, source_target_pairs={{0,4},{2,6},{4,0},{6,2},{8,12},{10,14},{12,8},{14,10},{16,20},{18,... | collective-permute-start | bytes 897032 | tf_op jit(solution)/shard_map/ppermute | solution.py:564
  56.0 10.0 %collective-permute-start.15 = (bf16[1168,128]{1,0:T(8,128)(2,1)S(1)}, bf16[1168,128]{1,0:T(8,128)(2,1)S(1)}, u32[]{:S(2)}, u32[]{:S(2)}) collective-permute-start(bf16[1168,128]{1,0:T(8,128)(2,1)S(1)} %get-tuple-element.214), channel_id=1, source_target_pairs={{0,2},{2,0},{4,6},{6,4},{8,10},{10,8},{12,14},{14,12},{16,18},{18,... | collective-permute-start | bytes 897032 | tf_op jit(solution)/shard_map/ppermute | solution.py:564
  56.6 22.4 %collective-permute-start.14 = (bf16[2336,128]{1,0:T(8,128)(2,1)S(1)}, bf16[2336,128]{1,0:T(8,128)(2,1)S(1)}, u32[]{:S(2)}, u32[]{:S(2)}) collective-permute-start(bf16[2336,128]{1,0:T(8,128)(2,1)S(1)} %pad_maximum_fusion.5), channel_id=1, source_target_pairs={{0,2},{2,0},{4,6},{6,4},{8,10},{10,8},{12,14},{14,12},{16,18},{18,... | collective-permute-start | bytes 1794056 | tf_op jit(solution)/shard_map/ppermute | solution.py:564
  58.0 19.3 %collective-permute-start.13 = (bf16[2336,128]{1,0:T(8,128)(2,1)S(1)}, bf16[2336,128]{1,0:T(8,128)(2,1)S(1)}, u32[]{:S(2)}, u32[]{:S(2)}) collective-permute-start(bf16[2336,128]{1,0:T(8,128)(2,1)S(1)} %pad_maximum_fusion.4), channel_id=1, source_target_pairs={{0,4},{2,6},{4,0},{6,2},{8,12},{10,14},{12,8},{14,10},{16,20},{18,... | collective-permute-start | bytes 1794056 | tf_op jit(solution)/shard_map/ppermute | solution.py:564
  64.5 27.1 %collective-permute-start.12 = (bf16[2336,128]{1,0:T(8,128)(2,1)S(1)}, bf16[2336,128]{1,0:T(8,128)(2,1)S(1)}, u32[]{:S(2)}, u32[]{:S(2)}) collective-permute-start(bf16[2336,128]{1,0:T(8,128)(2,1)S(1)} %pad_maximum_fusion.3), channel_id=1, source_target_pairs={{0,2},{2,0},{4,6},{6,4},{8,10},{10,8},{12,14},{14,12},{16,18},{18,... | collective-permute-start | bytes 1794056 | tf_op jit(solution)/shard_map/ppermute | solution.py:564
  66.0 24.1 %collective-permute-start.11 = (bf16[2336,128]{1,0:T(8,128)(2,1)S(1)}, bf16[2336,128]{1,0:T(8,128)(2,1)S(1)}, u32[]{:S(2)}, u32[]{:S(2)}) collective-permute-start(bf16[2336,128]{1,0:T(8,128)(2,1)S(1)} %pad_maximum_fusion.2), channel_id=1, source_target_pairs={{0,4},{2,6},{4,0},{6,2},{8,12},{10,14},{12,8},{14,10},{16,20},{18,... | collective-permute-start | bytes 1794056 | tf_op jit(solution)/shard_map/ppermute | solution.py:564
  77.3 22.1 %collective-permute-start.17 = (bf16[2336,128]{1,0:T(8,128)(2,1)S(1)}, bf16[2336,128]{1,0:T(8,128)(2,1)S(1)}, u32[]{:S(2)}, u32[]{:S(2)}) collective-permute-start(bf16[2336,128]{1,0:T(8,128)(2,1)S(1)} %pad_maximum_fusion.6), channel_id=1, source_target_pairs={{0,4},{2,6},{4,0},{6,2},{8,12},{10,14},{12,8},{14,10},{16,20},{18,... | collective-permute-start | bytes 1794056 | tf_op jit(solution)/shard_map/ppermute | solution.py:564
  79.0 21.7 %collective-permute-start.18 = (bf16[2336,128]{1,0:T(8,128)(2,1)S(1)}, bf16[2336,128]{1,0:T(8,128)(2,1)S(1)}, u32[]{:S(2)}, u32[]{:S(2)}) collective-permute-start(bf16[2336,128]{1,0:T(8,128)(2,1)S(1)} %pad_maximum_fusion.7), channel_id=1, source_target_pairs={{0,2},{2,0},{4,6},{6,4},{8,10},{10,8},{12,14},{14,12},{16,18},{18,... | collective-permute-start | bytes 1794056 | tf_op jit(solution)/shard_map/ppermute | solution.py:564
  90.2 15.5 %collective-permute-start.21 = (bf16[9344,128]{1,0:T(8,128)(2,1)S(1)}, bf16[9344,128]{1,0:T(8,128)(2,1)}, u32[]{:S(2)}, u32[]{:S(2)}) collective-permute-start(bf16[9344,128]{1,0:T(8,128)(2,1)S(1)} %constant_dynamic-update-slice_fusion.10.refs_2_), channel_id=1, source_target_pairs={{0,1},{1,0},{2,3},{3,2},{4,5},{5,4},{6,7},{7,6},{8,9},{9,8},{10,11... | collective-permute-start | bytes 7176200 | tf_op jit(solution)/shard_map/ppermute | solution.py:564
  92.5 13.2 %collective-permute-start.20 = (bf16[9344,128]{1,0:T(8,128)(2,1)}, bf16[9344,128]{1,0:T(8,128)(2,1)}, u32[]{:S(2)}, u32[]{:S(2)}) collective-permute-start(bf16[9344,128]{1,0:T(8,128)(2,1)} %constant_dynamic-update-slice_fusion.5.refs_1_), channel_id=1, source_target_pairs={{0,1},{1,0},{2,3},{3,2},{4,5},{5,4},{6,7},{7,6},{8,9},{9,8},{10,11... | collective-permute-start | bytes 7176200 | tf_op jit(solution)/shard_map/ppermute | solution.py:564
  101.6 4.9 %collective-permute-start.22 = (bf16[9344,128]{1,0:T(8,128)(2,1)}, bf16[9344,128]{1,0:T(8,128)(2,1)}, u32[]{:S(2)}, u32[]{:S(2)}) collective-permute-start(bf16[9344,128]{1,0:T(8,128)(2,1)} %constant_dynamic-update-slice_fusion.15.refs_3_), channel_id=1, source_target_pairs={{0,1},{1,0},{2,3},{3,2},{4,5},{5,4},{6,7},{7,6},{8,9},{9,8},{10,11... | collective-permute-start | bytes 7176200 | tf_op jit(solution)/shard_map/ppermute | solution.py:564
  125.5 25.9 %all-to-all-start = ((bf16[16,144,128]{2,1,0:T(8,128)(2,1)}), bf16[16,144,128]{2,1,0:T(8,128)(2,1)S(1)}, u32[]{:S(2)}, u32[]{:S(2)}) async-start(bf16[16,144,128]{2,1,0:T(8,128)(2,1)} %get-tuple-element.125), calls=%async_computation | async-start | bytes 1179648 | tf_op jit(solution)/shard_map/all_to_all | solution.py:1260
  164.9 15.7 %all-to-all-start.1 = ((bf16[16,48,128]{2,1,0:T(8,128)(2,1)}), bf16[16,48,128]{2,1,0:T(8,128)(2,1)S(1)}, u32[]{:S(2)}, u32[]{:S(2)}) async-start(bf16[16,48,128]{2,1,0:T(8,128)(2,1)} %get-tuple-element.131), calls=%async_computation.1 | async-start | bytes 393216 | tf_op jit(solution)/shard_map/all_to_all | solution.py:1260
  195.7 33.7 %copy-start.2 = (bf16[2304,128]{1,0:T(8,128)(2,1)S(1)}, bf16[2304,128]{1,0:T(8,128)(2,1)}, u32[]{:S(2)}) copy-start(bf16[2304,128]{1,0:T(8,128)(2,1)} %get-tuple-element.123.refs_0_) | copy-start | bytes 1769476
  195.7 33.8 %copy-start.6 = (bf16[16,48,128]{2,1,0:T(8,128)(2,1)S(1)}, bf16[16,48,128]{2,1,0:T(8,128)(2,1)}, u32[]{:S(2)}) copy-start(bf16[16,48,128]{2,1,0:T(8,128)(2,1)} %copy-done.5) | copy-start | bytes 589828
  195.7 59.2 %collective-permute-start.25 = (bf16[10752,128]{1,0:T(8,128)(2,1)}, bf16[10752,128]{1,0:T(8,128)(2,1)S(1)}, u32[]{:S(2)}, u32[]{:S(2)}) collective-permute-start(bf16[10752,128]{1,0:T(8,128)(2,1)} %get-tuple-element.141.refs_4_), channel_id=1, source_target_pairs={{0,1},{1,0},{2,3},{3,2},{4,5},{5,4},{6,7},{7,6},{8,9},{9,8},{10,11... | collective-permute-start | bytes 8257544 | tf_op jit(solution)/shard_map/ppermute | solution.py:564
  224.9 20.5 %all-to-all-start.3 = ((bf16[16,144,128]{2,1,0:T(8,128)(2,1)}), bf16[16,144,128]{2,1,0:T(8,128)(2,1)}, u32[]{:S(2)}, u32[]{:S(2)}) async-start(bf16[16,144,128]{2,1,0:T(8,128)(2,1)} %attend_backward.1), calls=%async_computation.3 | async-start | bytes 1179648 | tf_op jit(solution)/shard_map/all_to_all | solution.py:1260
  229.4 2.1 collective-permute-start.23
  229.5 2.8 collective-permute-start.24
  252.3 2.6 collective-permute-start.26
  263.0 18.5 %collective-permute-start.29 = (s16[2,1184,128]{2,1,0:T(8,128)(2,1)S(1)}, s16[2,1184,128]{2,1,0:T(8,128)(2,1)S(1)}, u32[]{:S(2)}, u32[]{:S(2)}) collective-permute-start(s16[2,1184,128]{2,1,0:T(8,128)(2,1)S(1)} %get-tuple-element.151), channel_id=1, source_target_pairs={{0,4},{2,6},{4,0},{6,2},{8,12},{10,14},{12,8},{14,10},{16,20},{18,... | collective-permute-start | bytes 1818632 | tf_op jit(solution)/shard_map/ppermute | solution.py:564
  264.1 17.3 %collective-permute-start.30 = (s16[2,1184,128]{2,1,0:T(8,128)(2,1)S(1)}, s16[2,1184,128]{2,1,0:T(8,128)(2,1)S(1)}, u32[]{:S(2)}, u32[]{:S(2)}) collective-permute-start(s16[2,1184,128]{2,1,0:T(8,128)(2,1)S(1)} %get-tuple-element.152), channel_id=1, source_target_pairs={{0,2},{2,0},{4,6},{6,4},{8,10},{10,8},{12,14},{14,12},{16,18},{18,... | collective-permute-start | bytes 1818632 | tf_op jit(solution)/shard_map/ppermute | solution.py:564
  272.0 19.7 %collective-permute-start.27 = (s16[2,1184,128]{2,1,0:T(8,128)(2,1)S(1)}, s16[2,1184,128]{2,1,0:T(8,128)(2,1)S(1)}, u32[]{:S(2)}, u32[]{:S(2)}) collective-permute-start(s16[2,1184,128]{2,1,0:T(8,128)(2,1)S(1)} %get-tuple-element.149), channel_id=1, source_target_pairs={{0,4},{2,6},{4,0},{6,2},{8,12},{10,14},{12,8},{14,10},{16,20},{18,... | collective-permute-start | bytes 1818632 | tf_op jit(solution)/shard_map/ppermute | solution.py:564
  273.0 19.5 %collective-permute-start.28 = (s16[2,1184,128]{2,1,0:T(8,128)(2,1)S(1)}, s16[2,1184,128]{2,1,0:T(8,128)(2,1)S(1)}, u32[]{:S(2)}, u32[]{:S(2)}) collective-permute-start(s16[2,1184,128]{2,1,0:T(8,128)(2,1)S(1)} %get-tuple-element.150), channel_id=1, source_target_pairs={{0,2},{2,0},{4,6},{6,4},{8,10},{10,8},{12,14},{14,12},{16,18},{18,... | collective-permute-start | bytes 1818632 | tf_op jit(solution)/shard_map/ppermute | solution.py:564
  295.2 10.2 %collective-permute-start.31 = (s16[1184,128]{1,0:T(8,128)(2,1)S(1)}, s16[1184,128]{1,0:T(8,128)(2,1)S(1)}, u32[]{:S(2)}, u32[]{:S(2)}) collective-permute-start(s16[1184,128]{1,0:T(8,128)(2,1)S(1)} %get-tuple-element.162), channel_id=1, source_target_pairs={{0,2},{2,0},{4,6},{6,4},{8,10},{10,8},{12,14},{14,12},{16,18},{18,... | collective-permute-start | bytes 909320 | tf_op jit(solution)/shard_map/ppermute | solution.py:564
  295.8 10.1 %collective-permute-start.32 = (s16[1184,128]{1,0:T(8,128)(2,1)S(1)}, s16[1184,128]{1,0:T(8,128)(2,1)S(1)}, u32[]{:S(2)}, u32[]{:S(2)}) collective-permute-start(s16[1184,128]{1,0:T(8,128)(2,1)S(1)} %get-tuple-element.163), channel_id=1, source_target_pairs={{0,4},{2,6},{4,0},{6,2},{8,12},{10,14},{12,8},{14,10},{16,20},{18,... | collective-permute-start | bytes 909320 | tf_op jit(solution)/shard_map/ppermute | solution.py:564
  296.7 13.0 %collective-permute-start.33 = (s16[1184,128]{1,0:T(8,128)(2,1)S(1)}, s16[1184,128]{1,0:T(8,128)(2,1)S(1)}, u32[]{:S(2)}, u32[]{:S(2)}) collective-permute-start(s16[1184,128]{1,0:T(8,128)(2,1)S(1)} %get-tuple-element.164), channel_id=1, source_target_pairs={{0,2},{2,0},{4,6},{6,4},{8,10},{10,8},{12,14},{14,12},{16,18},{18,... | collective-permute-start | bytes 909320 | tf_op jit(solution)/shard_map/ppermute | solution.py:564
  298.2 11.9 %collective-permute-start.34 = (s16[1184,128]{1,0:T(8,128)(2,1)S(1)}, s16[1184,128]{1,0:T(8,128)(2,1)S(1)}, u32[]{:S(2)}, u32[]{:S(2)}) collective-permute-start(s16[1184,128]{1,0:T(8,128)(2,1)S(1)} %get-tuple-element.165), channel_id=1, source_target_pairs={{0,4},{2,6},{4,0},{6,2},{8,12},{10,14},{12,8},{14,10},{16,20},{18,... | collective-permute-start | bytes 909320 | tf_op jit(solution)/shard_map/ppermute | solution.py:564
  310.1 13.4 %collective-permute-start.35 = (s16[2,1184,128]{2,1,0:T(8,128)(2,1)S(1)}, s16[2,1184,128]{2,1,0:T(8,128)(2,1)S(1)}, u32[]{:S(2)}, u32[]{:S(2)}) collective-permute-start(s16[2,1184,128]{2,1,0:T(8,128)(2,1)S(1)} %get-tuple-element.166), channel_id=1, source_target_pairs={{0,4},{2,6},{4,0},{6,2},{8,12},{10,14},{12,8},{14,10},{16,20},{18,... | collective-permute-start | bytes 1818632 | tf_op jit(solution)/shard_map/ppermute | solution.py:564
  311.0 13.1 %collective-permute-start.36 = (s16[2,1184,128]{2,1,0:T(8,128)(2,1)S(1)}, s16[2,1184,128]{2,1,0:T(8,128)(2,1)S(1)}, u32[]{:S(2)}, u32[]{:S(2)}) collective-permute-start(s16[2,1184,128]{2,1,0:T(8,128)(2,1)S(1)} %get-tuple-element.167), channel_id=1, source_target_pairs={{0,2},{2,0},{4,6},{6,4},{8,10},{10,8},{12,14},{14,12},{16,18},{18,... | collective-permute-start | bytes 1818632 | tf_op jit(solution)/shard_map/ppermute | solution.py:564
  313.2 12.9 %collective-permute-start.37 = (s16[2,1184,128]{2,1,0:T(8,128)(2,1)S(1)}, s16[2,1184,128]{2,1,0:T(8,128)(2,1)S(1)}, u32[]{:S(2)}, u32[]{:S(2)}) collective-permute-start(s16[2,1184,128]{2,1,0:T(8,128)(2,1)S(1)} %add_line.3), channel_id=1, source_target_pairs={{0,8},{2,10},{4,12},{6,14},{8,0},{10,2},{12,4},{14,6},{16,24},{18,... | collective-permute-start | bytes 1818632 | tf_op jit(solution)/shard_map/ppermute | solution.py:564
  327.3 8.0 %collective-permute-start.38 = (s16[1184,128]{1,0:T(8,128)(2,1)S(1)}, s16[1184,128]{1,0:T(8,128)(2,1)S(1)}, u32[]{:S(2)}, u32[]{:S(2)}) collective-permute-start(s16[1184,128]{1,0:T(8,128)(2,1)S(1)} %get-tuple-element.182), channel_id=1, source_target_pairs={{0,2},{2,0},{4,6},{6,4},{8,10},{10,8},{12,14},{14,12},{16,18},{18,... | collective-permute-start | bytes 909320 | tf_op jit(solution)/shard_map/ppermute | solution.py:564
  328.0 9.4 %collective-permute-start.39 = (s16[1184,128]{1,0:T(8,128)(2,1)S(1)}, s16[1184,128]{1,0:T(8,128)(2,1)S(1)}, u32[]{:S(2)}, u32[]{:S(2)}) collective-permute-start(s16[1184,128]{1,0:T(8,128)(2,1)S(1)} %get-tuple-element.183), channel_id=1, source_target_pairs={{0,4},{2,6},{4,0},{6,2},{8,12},{10,14},{12,8},{14,10},{16,20},{18,... | collective-permute-start | bytes 909320 | tf_op jit(solution)/shard_map/ppermute | solution.py:564
  337.4 11.2 %collective-permute-start.40 = (s16[2,1184,128]{2,1,0:T(8,128)(2,1)S(1)}, s16[2,1184,128]{2,1,0:T(8,128)(2,1)S(1)}, u32[]{:S(2)}, u32[]{:S(2)}) collective-permute-start(s16[2,1184,128]{2,1,0:T(8,128)(2,1)S(1)} %get-tuple-element.184), channel_id=1, source_target_pairs={{0,4},{2,6},{4,0},{6,2},{8,12},{10,14},{12,8},{14,10},{16,20},{18,... | collective-permute-start | bytes 1818632 | tf_op jit(solution)/shard_map/ppermute | solution.py:564
  338.4 12.7 %collective-permute-start.41 = (s16[2,1184,128]{2,1,0:T(8,128)(2,1)S(1)}, s16[2,1184,128]{2,1,0:T(8,128)(2,1)S(1)}, u32[]{:S(2)}, u32[]{:S(2)}) collective-permute-start(s16[2,1184,128]{2,1,0:T(8,128)(2,1)S(1)} %get-tuple-element.186), channel_id=1, source_target_pairs={{0,2},{2,0},{4,6},{6,4},{8,10},{10,8},{12,14},{14,12},{16,18},{18,... | collective-permute-start | bytes 1818632 | tf_op jit(solution)/shard_map/ppermute | solution.py:564
  340.8 21.3 %collective-permute-start.45 = (s16[2,1184,128]{2,1,0:T(8,128)(2,1)S(1)}, s16[2,1184,128]{2,1,0:T(8,128)(2,1)S(1)}, u32[]{:S(2)}, u32[]{:S(2)}) collective-permute-start(s16[2,1184,128]{2,1,0:T(8,128)(2,1)S(1)} %add_line.5), channel_id=1, source_target_pairs={{0,16},{2,18},{4,20},{6,22},{8,24},{10,26},{12,28},{14,30},{16,0},... | collective-permute-start | bytes 1818632 | tf_op jit(solution)/shard_map/ppermute | solution.py:564
  342.2 19.8 %collective-permute-start.44 = (s16[2,1184,128]{2,1,0:T(8,128)(2,1)S(1)}, s16[2,1184,128]{2,1,0:T(8,128)(2,1)S(1)}, u32[]{:S(2)}, u32[]{:S(2)}) collective-permute-start(s16[2,1184,128]{2,1,0:T(8,128)(2,1)S(1)} %add_line.4), channel_id=1, source_target_pairs={{0,8},{2,10},{4,12},{6,14},{8,0},{10,2},{12,4},{14,6},{16,24},{18,... | collective-permute-start | bytes 1818632 | tf_op jit(solution)/shard_map/ppermute | solution.py:564
  351.1 33.2 %copy-start.12 = (f32[24,96,96]{2,1,0:T(8,128)S(1)}, f32[24,96,96]{2,1,0:T(8,128)}, u32[]{:S(2)}) copy-start(f32[24,96,96]{2,1,0:T(8,128)} %right_ref.1) | copy-start | bytes 2654212
  352.5 31.9 %copy-start.7 = (f32[24,96,96]{2,1,0:T(8,128)S(1)}, f32[24,96,96]{2,1,0:T(8,128)}, u32[]{:S(2)}) copy-start(f32[24,96,96]{2,1,0:T(8,128)} %block_ref.1) | copy-start | bytes 2654212
  352.5 31.9 %copy-start.10 = (f32[48,2,768]{2,1,0:T(2,128)S(1)}, f32[48,2,768]{2,1,0:T(2,128)}, u32[]{:S(2)}) copy-start(f32[48,2,768]{2,1,0:T(2,128)} %io_ref.1) | copy-start | bytes 884740
  352.5 31.9 %copy-start.11 = (f32[24,96,96]{2,1,0:T(8,128)S(1)}, f32[24,96,96]{2,1,0:T(8,128)}, u32[]{:S(2)}) copy-start(f32[24,96,96]{2,1,0:T(8,128)} %left_ref.1) | copy-start | bytes 2654212
  352.5 31.9 %copy-start.13 = (f32[19,768]{1,0:T(8,128)S(1)}, f32[19,768]{1,0:T(8,128)}, u32[]{:S(2)}) copy-start(f32[19,768]{1,0:T(8,128)} %vec_ref.1) | copy-start | bytes 175108
  352.5 31.8 %copy-start.14 = (f32[48,2,768]{2,1,0:T(2,128)S(1)}, f32[48,2,768]{2,1,0:T(2,128)}, u32[]{:S(2)}) copy-start(f32[48,2,768]{2,1,0:T(2,128)} %io_first_ref.1) | copy-start | bytes 884740
  352.5 31.8 %copy-start.15 = (f32[48,2,768]{2,1,0:T(2,128)S(1)}, f32[48,2,768]{2,1,0:T(2,128)}, u32[]{:S(2)}) copy-start(f32[48,2,768]{2,1,0:T(2,128)} %io_second_ref.1) | copy-start | bytes 884740
  352.5 31.8 %copy-start.18 = (f32[19,768]{1,0:T(8,128)S(1)}, f32[19,768]{1,0:T(8,128)}, u32[]{:S(2)}) copy-start(f32[19,768]{1,0:T(8,128)} %vec_first_ref.1) | copy-start | bytes 175108
  352.6 9.5 %collective-permute-start.42 = (s16[1184,128]{1,0:T(8,128)(2,1)S(1)}, s16[1184,128]{1,0:T(8,128)(2,1)S(1)}, u32[]{:S(2)}, u32[]{:S(2)}) collective-permute-start(s16[1184,128]{1,0:T(8,128)(2,1)S(1)} %get-tuple-element.188), channel_id=1, source_target_pairs={{0,2},{2,0},{4,6},{6,4},{8,10},{10,8},{12,14},{14,12},{16,18},{18,... | collective-permute-start | bytes 909320 | tf_op jit(solution)/shard_map/ppermute | solution.py:564
  354.1 7.9 %collective-permute-start.43 = (s16[1184,128]{1,0:T(8,128)(2,1)S(1)}, s16[1184,128]{1,0:T(8,128)(2,1)S(1)}, u32[]{:S(2)}, u32[]{:S(2)}) collective-permute-start(s16[1184,128]{1,0:T(8,128)(2,1)S(1)} %get-tuple-element.190), channel_id=1, source_target_pairs={{0,4},{2,6},{4,0},{6,2},{8,12},{10,14},{12,8},{14,10},{16,20},{18,... | collective-permute-start | bytes 909320 | tf_op jit(solution)/shard_map/ppermute | solution.py:564
  363.1 1.3 collective-permute-start.46
  364.4 4.4 %collective-permute-start.47 = (f32[24,768]{1,0:T(8,128)S(1)}, f32[24,768]{1,0:T(8,128)S(1)}, u32[]{:S(2)}, u32[]{:S(2)}) collective-permute-start(f32[24,768]{1,0:T(8,128)S(1)} %add.260), channel_id=1, source_target_pairs={{0,2},{2,0},{4,6},{6,4},{8,10},{10,8},{12,14},{14,12},{16,18},{18,... | collective-permute-start | bytes 221192 | tf_op jit(solution)/shard_map/ppermute | solution.py:564
  368.8 4.4 %collective-permute-start.48 = (f32[24,768]{1,0:T(8,128)S(1)}, f32[24,768]{1,0:T(8,128)S(1)}, u32[]{:S(2)}, u32[]{:S(2)}) collective-permute-start(f32[24,768]{1,0:T(8,128)S(1)} %add.261), channel_id=1, source_target_pairs={{0,4},{2,6},{4,0},{6,2},{8,12},{10,14},{12,8},{14,10},{16,20},{18,... | collective-permute-start | bytes 221192 | tf_op jit(solution)/shard_map/ppermute | solution.py:564
  373.3 4.4 %collective-permute-start.49 = (f32[24,768]{1,0:T(8,128)S(1)}, f32[24,768]{1,0:T(8,128)S(1)}, u32[]{:S(2)}, u32[]{:S(2)}) collective-permute-start(f32[24,768]{1,0:T(8,128)S(1)} %add.262), channel_id=1, source_target_pairs={{0,8},{2,10},{4,12},{6,14},{8,0},{10,2},{12,4},{14,6},{16,24},{18,... | collective-permute-start | bytes 221192 | tf_op jit(solution)/shard_map/ppermute | solution.py:564
  377.7 6.1 %collective-permute-start.50 = (f32[24,768]{1,0:T(8,128)S(1)}, f32[24,768]{1,0:T(8,128)S(1)}, u32[]{:S(2)}, u32[]{:S(2)}) collective-permute-start(f32[24,768]{1,0:T(8,128)S(1)} %add.263), channel_id=1, source_target_pairs={{0,16},{2,18},{4,20},{6,22},{8,24},{10,26},{12,28},{14,30},{16,0},... | collective-permute-start | bytes 221192 | tf_op jit(solution)/shard_map/ppermute | solution.py:564
  (16 other events, 206.0 us)
where the time goes:
time: 418 us; the launch traced here: 410 us
  Pallas kernels  151 us (36%)
  waiting for transfers between devices  147 us (35%)
  starting transfers between devices  70.4 us (17%)
  local copies, waits for them, and re-layouts  23.5 us (6%)
  blocking collectives  13.3 us (3%)
    ppermute x51, waiting for transfers between devices, swap(): lax.ppermute(value, axis, [(s, s ^ mask) for s in range(lax.axis_size(axi...  126 us
    pallas_call x5, Pallas kernels, from_hbm(): pl.pallas_call(kernel, out_shape=[pltpu.HBM(s, t) for s, t in outs], in_s...  54.6 us
    ppermute x51, starting transfers between devices, swap(): lax.ppermute(value, axis, [(s, s ^ mask) for s in range(lax.axis_size(axi...  51 us
    pallas_call x2, Pallas kernels, join_weights(): pl.pallas_call(partial(join_kernel, plan, io_out), out_shape=[pltpu.HBM(s...  32.3 us
    pallas_call x4, Pallas kernels, weight_grads(): pl.pallas_call(partial(grads_kernel, zone), out_shape=[jax.ShapeDtypeStru...  28.3 us
    pallas_call x1, Pallas kernels, update_step(): pl.pallas_call(partial(shampoo_kernel, beta=beta_stat, rate=rate_shampoo,...  24.9 us
    all_to_all x3, waiting for transfers between devices, to_heads(): return lax.all_to_all(parts, 'seq', 0, 0, tiled=True)  20.3 us
    all_to_all x3, starting transfers between devices, to_heads(): return lax.all_to_all(parts, 'seq', 0, 0, tiled=True)  19.3 us
  transfers between devices with their start and end apart: 54, of which 38 were waited for; matrix products, arithmetic and copies ran while one was open for 5% of the time, Pallas kernels for 16%

commit v1 on v0

--- a/solution.py
+++ b/solution.py
@@ -565,24 +565,26 @@
 def gate(*values):
     return lax.optimization_barrier(values)
 
-COUNT_AT=3*3*BLOCK+6*IO
-SHARD_HALF=COUNT_AT+16
-def pack_kernel(blocks_ref, in_ref, head_ref, mask_ref, first_ref, second_ref, whole_ref):
+GROUP_ROWS=3*BLOCK
+IO_AT=2*GROUP_ROWS; COUNT_AT=IO_AT+6*IO; THIRD_AT=COUNT_AT+16
+SHARD_HALF=THIRD_AT+GROUP_ROWS
+PIECE=8*SHARD_HALF; THIRDS=8*THIRD_AT
+def pack_kernel(blocks_ref, io_ref, mask_ref, first_ref, second_ref, both_ref):
     count=jnp.sum(mask_ref[...].astype(jnp.float32),keepdims=True)
     lane=lax.broadcasted_iota(jnp.int32,(BLOCK,LANE),1)
     pad=lambda x: jnp.concatenate([x,jnp.zeros((BLOCK,LANE-BLOCK),x.dtype)],axis=1)
-    for h,(io,out_ref) in enumerate(zip((in_ref,head_ref),(first_ref,second_ref))):
+    for h,out_ref in enumerate((first_ref,second_ref)):
         for g in range(3):
             b=[pad(blocks_ref[(h*3+g)*4+t]) for t in range(4)]
             for v in range(3):
                 tile=jnp.where(lane<BLOCK,b[v],pltpu.roll(b[3],BLOCK-32*v,1))
-                at=(g*3+v)*BLOCK
+                at=(g*GROUP_ROWS if g<2 else THIRD_AT)+v*BLOCK
                 out_ref[at:at+BLOCK,:]=tile.astype(BF)
         for v in range(6):
-            at=9*BLOCK+v*IO
-            out_ref[at:at+IO,:]=io[:,v*LANE:(v+1)*LANE].astype(BF)
-        out_ref[COUNT_AT:,:]=jnp.broadcast_to(count,(16,LANE)).astype(BF)
-        whole_ref[h*SHARD_HALF:(h+1)*SHARD_HALF,:]=out_ref[...]
+            at=IO_AT+v*IO
+            out_ref[at:at+IO,:]=io_ref[:,h,v*LANE:(v+1)*LANE].astype(BF)
+        out_ref[COUNT_AT:THIRD_AT,:]=jnp.broadcast_to(count,(16,LANE)).astype(BF)
+        both_ref[h*THIRD_AT:(h+1)*THIRD_AT,:]=out_ref[:THIRD_AT,:]
 def vmem(): return pl.BlockSpec(memory_space=pltpu.VMEM)
 def smem(): return pl.BlockSpec(memory_space=pltpu.SMEM)
 def hbm(): return pl.BlockSpec(memory_space=pltpu.HBM)
@@ -609,32 +611,67 @@
         compiler_params=pltpu.CompilerParams(vmem_limit_bytes=vmem_mib<<20),
         cost_estimate=pl.CostEstimate(flops=0,transcendentals=0,bytes_accessed=int(micros*3.3e6)),name=name)(*smem_args,*ins)
 def pack_shard(blocks, io, mask):
-    return pl.pallas_call(pack_kernel,out_shape=[jax.ShapeDtypeStruct((n*SHARD_HALF,LANE),BF) for n in (1,1,2)],in_specs=[vmem()]*4,out_specs=[vmem()]*3,name="pack_shard")(blocks,io[:,0],io[:,1],mask)
+    return pl.pallas_call(pack_kernel,out_shape=[jax.ShapeDtypeStruct((n,LANE),BF) for n in (SHARD_HALF,SHARD_HALF,2*THIRD_AT)],in_specs=[vmem()]*3,out_specs=[vmem()]*3,name="pack_shard")(blocks,io,mask)
 
 HOPS=(("opt",1),("seq",1),("seq",2),("seq",4),("seq",8))
 def hop(value, k):
     return value+swap(value,*HOPS[k])
 
-def gather_tree(first, second, own):
-    half=first.shape[0]
-    near=[None]*4; cross=[None]*4
+def stack_rows(arrays, *plans):
+    n=len(arrays); total=sum(len(p) for p in plans)
+    shapes=[(sum(c for _,_,c in p),LANE) for p in plans]
+    def kernel(*refs):
+        ins,outs,held,(in_sem,out_sem)=refs[:n],refs[n:n+len(plans)],refs[n+len(plans):-2],refs[-2:]
+        copies=[]; stores=[]
+        for i,plan in enumerate(plans):
+            at=0
+            for k,first,count in plan:
+                copies.append((i,pltpu.make_async_copy(ins[k].at[pl.ds(first,count)],held[i].at[pl.ds(at,count)],in_sem.at[len(copies)])))
+                copies[-1][1].start()
+                at+=count
+        for i,out in enumerate(outs):
+            for k,c in copies:
+                if k==i: c.wait()
+            stores.append(pltpu.make_async_copy(held[i],out,out_sem.at[i]))
+            stores[-1].start()
+        for c in stores: c.wait()
+    return pl.pallas_call(kernel,out_shape=[jax.ShapeDtypeStruct(s,BF) for s in shapes],
+        in_specs=[pl.BlockSpec(memory_space=pl.ANY)]*n,out_specs=[pl.BlockSpec(memory_space=pl.ANY)]*len(plans),
+        scratch_shapes=[pltpu.VMEM(s,BF) for s in shapes]+[pltpu.SemaphoreType.DMA((total,)),pltpu.SemaphoreType.DMA((len(plans),))],
+        compiler_params=pltpu.CompilerParams(vmem_limit_bytes=16<<20),name="stack_rows")(*arrays)
+
+def gather_tree(first, second, both):
+    near=[None]*4; cross=[None]*4; third=[None]*4
     def first_step(k,a,b):
         near[k]=(swap(a,"seq",1),swap(b,"seq",2))
-    def second_step(k,a,b):
-        cross[k]=(swap(jnp.concatenate([a,near[k][0]]),"seq",2),swap(jnp.concatenate([b,near[k][1]]),"seq",1))
-    far1=swap(own,"seq",4)
-    far2=swap(own,"seq",8)
+    def second_step(k,a,b,rows):
+        sent=stack_rows([a[0],near[k][0],b[0],near[k][1]],[(0,a[1],rows),(1,0,rows)],[(2,b[1],rows),(3,0,rows)])
+        cross[k]=(swap(sent[0],"seq",2),swap(sent[1],"seq",1))
+    def halves_of(far): return (far,0),(far,THIRD_AT)
+    far1=swap(both,"seq",4)
+    far2=swap(both,"seq",8)
     first_step(0,first,second)
-    second_step(0,first,second)
-    first_step(1,far1[:half],far1[half:])
-    first_step(2,far2[:half],far2[half:])
+    second_step(0,(first,0),(second,0),SHARD_HALF)
+    arrays=[first,second,*near[0],*cross[0]]
+    units=[(0,0),(1,0),(2,0),(3,0),(4,0),(4,SHARD_HALF),(5,0),(5,SHARD_HALF)]
+    third[0]=stack_rows(arrays,[(k,at+THIRD_AT,GROUP_ROWS) for k,at in units])[0]
+    third[2]=swap(third[0],"seq",8)
+    third[1]=swap(third[0],"seq",4)
+    first_step(1,far1[:THIRD_AT],far1[THIRD_AT:])
+    first_step(2,far2[:THIRD_AT],far2[THIRD_AT:])
     far3=swap(far2,"seq",4)
     near[1],near[2],far3=gate(near[1],near[2],far3)
-    second_step(1,far1[:half],far1[half:])
-    first_step(3,far3[:half],far3[half:])
-    second_step(2,far2[:half],far2[half:])
-    second_step(3,far3[:half],far3[half:])
-    out=[jnp.concatenate([piece,*near[k],*cross[k]]) for k,piece in enumerate((own,far1,far2,far3))]
+    second_step(1,*halves_of(far1),THIRD_AT)
+    first_step(3,far3[:THIRD_AT],far3[THIRD_AT:])
+    near[2],near[3]=gate(near[2],near[3])
+    second_step(2,*halves_of(far2),THIRD_AT)
+    near[3],third[2]=gate(near[3],third[2])
+    second_step(3,*halves_of(far3),THIRD_AT)
+    third[3]=swap(third[2],"seq",4)
+    out=list(stack_rows(arrays+[third[0]],[(k,at,THIRD_AT) for k,at in units]+[(len(arrays),0,third[0].shape[0])]))
+    for k,far in ((1,far1),(2,far2),(3,far3)):
+        arrays=[far,*near[k],*cross[k],third[k]]
+        out+=stack_rows(arrays,[(i,0,part.shape[0]) for i,part in enumerate(arrays)])
     return out+[swap(piece,"opt",1) for piece in out]
 
 HELD=64*SHARD_HALF
@@ -647,9 +684,9 @@
     for k,c in enumerate(loads):
         c.wait()
         def unpack(u,carry,k=k):
-            at=(k*8+u)*SHARD_HALF
             for g in range(3):
-                parts=[held[pl.ds(pl.multiple_of(at+(g*3+v)*BLOCK,16),BLOCK),BLOCK:] for v in range(3)]
+                at=k*PIECE+(u*THIRD_AT+g*GROUP_ROWS if g<2 else THIRDS+u*GROUP_ROWS)
+                parts=[held[pl.ds(pl.multiple_of(at+v*BLOCK,16),BLOCK),BLOCK:] for v in range(3)]
                 to=HELD+((k*8+u)*3+g)*BLOCK
                 held[pl.ds(pl.multiple_of(to,16),BLOCK),:BLOCK]=jnp.concatenate(parts,axis=1)
             return carry
@@ -714,9 +751,10 @@
         return (rel//4+4*((dev%2)^core))*8+u
     slot=jnp.arange(N_BLOCK,dtype=jnp.int32); s=slot%24
     u=unit(slot//24,s//12); g=s%12//4; t=s%4
-    rows=jnp.where(t<3,u*SHARD_HALF+(g*3+t)*BLOCK,HELD+(u*3+g)*BLOCK)
+    start=u//8*PIECE+jnp.where(g<2,u%8*THIRD_AT+g*GROUP_ROWS,THIRDS+u%8*GROUP_ROWS)
+    rows=jnp.where(t<3,start+t*BLOCK,HELD+(u*3+g)*BLOCK)
     dev=jnp.arange(32,dtype=jnp.int32)
-    io=jnp.stack([unit(dev,h)*SHARD_HALF+9*BLOCK for h in (0,1)])
+    io=jnp.stack([unit(dev,h)//8*PIECE+unit(dev,h)%8*THIRD_AT+IO_AT for h in (0,1)])
     return rows.astype(jnp.int32),io.astype(jnp.int32)
 def gather_shards(layer_blocks, io_weights, mask):
     return gather_tree(*pack_shard(layer_blocks,io_weights,mask))
@@ -1176,17 +1214,17 @@
 BLOCK=96; NEWTON=6; F32=jnp.float32; BF=jnp.bfloat16; LANE=128
 def halves(x):
     hi=x.astype(BF); return hi,(x-hi.astype(F32)).astype(BF)
-def left_of(x):
-    hi,lo=halves(x)
-    return jnp.concatenate([hi,lo],axis=1)
-def right_of(x):
-    hi,lo=halves(x)
-    zero=jnp.zeros_like(lo)
-    return jnp.concatenate([jnp.concatenate([hi,lo],axis=1),jnp.concatenate([hi,zero],axis=1)],axis=0)
+def left_of(parts):
+    return jnp.concatenate(parts,axis=1)
+def right_of(parts):
+    hi,lo=parts
+    rest=jnp.zeros((LANE-BLOCK,LANE),BF)
+    top=jnp.concatenate([hi,lo],axis=1); low=jnp.concatenate([hi,jnp.zeros_like(lo)],axis=1)
+    both=jnp.zeros((LANE-BLOCK,2*LANE),BF)
+    return jnp.concatenate([top,both,low,both],axis=0)
 def times(a,b):
-    w=jnp.dot(a,b,preferred_element_type=F32)
-    n=w.shape[1]//2
-    return w[:,:n]+w[:,n:]
+    w=jnp.dot(left_of(a),right_of(b),preferred_element_type=F32)
+    return w[:,:LANE]+w[:,LANE:]
 def shampoo_kernel(sums_ref, grad_ref, left_ref, right_ref, block_ref, io_grad_ref, io_ref, io_first_ref, io_second_ref, vec_ref, vec_first_ref, vec_second_ref,
                    grad_out, left_out, right_out, block_out, io_first_out, io_second_out, io_out, vec_first_out, vec_second_out, vec_out, norm_out, *, beta, rate, eps, n_side):
     n_vec=vec_ref.shape[0]
@@ -1198,45 +1236,42 @@
     for m in range(2):
         parts=[ref[:,m,:] for ref in (io_ref,io_first_ref,io_second_ref,io_grad_ref)]
         io_first_out[:,m,:],io_second_out[:,m,:],io_out[:,m,:]=adam_update(*parts[:3],parts[3]*factor,rate_adam,weight_decay)
-    side=LANE
-    row=lax.broadcasted_iota(jnp.int32,(side,side),0); col=lax.broadcasted_iota(jnp.int32,(side,side),1)
-    eye=jnp.where((row==col)&(row<BLOCK),1.0,0.0)
-    def full(x):
-        x=jnp.concatenate([x,jnp.zeros((BLOCK,side-BLOCK),F32)],axis=1)
-        return jnp.concatenate([x,jnp.zeros((side-BLOCK,side),F32)],axis=0)
+    row=lax.broadcasted_iota(jnp.int32,(BLOCK,LANE),0); col=lax.broadcasted_iota(jnp.int32,(BLOCK,LANE),1)
+    eye=jnp.where(row==col,1.0,0.0)
+    none=jnp.zeros((BLOCK,LANE-BLOCK),F32)
+    def full(x): return jnp.concatenate([x,none],axis=1)
     def one(i,carry):
-        grads=[full(grad_ref[i*n_side+j]*factor) for j in range(n_side)]
-        flipped=[g.T for g in grads]
-        stats=[]
+        stats=[]; grads=[]
         for j in range(n_side):
             s=i*n_side+j
-            gl,gr=left_of(grads[j]),right_of(grads[j]); tl,tr=left_of(flipped[j]),right_of(flipped[j])
-            l=beta*full(left_ref[s])+(1.0-beta)*times(gl,tr)
-            r=beta*full(right_ref[s])+(1.0-beta)*times(tl,gr)
-            grad_out[s]=grads[j][:BLOCK,:BLOCK]; left_out[s]=l[:BLOCK,:BLOCK]; right_out[s]=r[:BLOCK,:BLOCK]
+            g=full(grad_ref[s]*factor)
+            grad_out[s]=g[:,:BLOCK]
+            g=halves(g); t=halves(full((grad_ref[s]*factor).T)); grads.append(g)
+            l=beta*full(left_ref[s])+(1.0-beta)*times(g,t)
+            r=beta*full(right_ref[s])+(1.0-beta)*times(t,g)
+            left_out[s]=l[:,:BLOCK]; right_out[s]=r[:,:BLOCK]
             stats+=[l,r]
-        n=len(stats)
         regular=[m+eps*eye for m in stats]
         scaled=[2.5*lax.rsqrt(jnp.sum(m*m,keepdims=True)) for m in regular]
         moving=[m*s for m,s in zip(regular,scaled)]
-        root=[None]*n
+        root=None
         for sweep in range(NEWTON):
-            factors=[(5.0*eye-m)*0.25 for m in moving]
-            fl=[left_of(f) for f in factors]; fr=[right_of(f) for f in factors]
+            factors=[1.25*eye-0.25*m for m in moving]
+            split=[halves(f) for f in factors]
             if sweep==0: root=[f*jnp.sqrt(jnp.sqrt(s)) for f,s in zip(factors,scaled)]
-            else: root=[times(left_of(x),f) for x,f in zip(root,fr)]
+            else: root=[times(halves(x),f) for x,f in zip(root,split)]
             if sweep<NEWTON-1:
-                square=[times(a,b) for a,b in zip(fl,fr)]
-                fourth=[times(left_of(q),right_of(q)) for q in square]
-                moving=[times(left_of(q),right_of(m)) for q,m in zip(fourth,moving)]
+                square=[halves(times(f,f)) for f in split]
+                fourth=[halves(times(q,q)) for q in square]
+                moving=[times(q,halves(m)) for q,m in zip(fourth,moving)]
         for j in range(n_side):
             s=i*n_side+j
-            d=times(left_of(root[2*j]),right_of(grads[j]))
-            d=times(left_of(d),right_of(root[2*j+1]))
-            block_out[s]=block_ref[s]-rate*d[:BLOCK,:BLOCK]
+            d=times(halves(root[2*j]),grads[j])
+            d=times(halves(d),halves(root[2*j+1]))
+            block_out[s]=block_ref[s]-rate*d[:,:BLOCK]
         return carry
     lax.fori_loop(0,grad_ref.shape[0]//n_side,one,0)
-def update_step(sums, grads, left, right, blocks, io_grad, io_set, vec_set, n_side=8):
+def update_step(sums, grads, left, right, blocks, io_grad, io_set, vec_set, n_side=12):
     like=lambda *xs: [jax.ShapeDtypeStruct(x.shape,F32) for x in xs]
     args=(sums,grads,left,right,blocks,io_grad,*io_set,*vec_set)
     return pl.pallas_call(partial(shampoo_kernel,beta=beta_stat,rate=rate_shampoo,eps=root_eps,n_side=n_side),

time: 418 us -> 403 us (0.964)
  Pallas kernels: 151 us -> 165 us
  waiting for transfers between devices: 147 us -> 133 us
  local copies, waits for them, and re-layouts: 23.5 us -> 9.8 us
    pallas_call x1 -> x10, Pallas kernels: 2.55 us -> 21.1 us  [the longest x9 18.3 us: stack_rows(): pl.pallas_call(kernel, out_shape=[jax.ShapeDtypeStruct(s, BF) for s in sh...]
    ppermute x51 -> x54, waiting for transfers between devices: 126 us -> 113 us  [swap(): lax.ppermute(value, axis, [(s, s ^ mask) for s in range(lax.axis_size(axi...]
    unnamed x68 -> x56, local copies, waits for them, and re-layouts: 15.1 us -> 6.15 us
    pallas_call x1, Pallas kernels: 24.9 us -> 20.4 us  [update_step(): pl.pallas_call(partial(shampoo_kernel, beta=beta_stat, rate=rate_shampoo,...]
    ppermute x51 -> x54, starting transfers between devices: 51 us -> 52.3 us  [swap(): lax.ppermute(value, axis, [(s, s ^ mask) for s in range(lax.axis_size(axi...]
  transfers between devices with their start and end apart: 54 -> 57, of which waited for: 38 -> 39; matrix products, arithmetic and copies ran while one was open for 5% -> 1% of each run, Pallas kernels for 16% -> 21%
where the time goes in v1:
time: 403 us; the launch traced here: 395 us
  Pallas kernels  165 us (41%)
  waiting for transfers between devices  133 us (33%)
  starting transfers between devices  69.9 us (17%)
  blocking collectives  13.3 us (3%)
  local copies, waits for them, and re-layouts  9.8 us (2%)
    ppermute x54, waiting for transfers between devices, swap(): lax.ppermute(value, axis, [(s, s ^ mask) for s in range(lax.axis_size(axi...  113 us
    pallas_call x5, Pallas kernels, from_hbm(): pl.pallas_call(kernel, out_shape=[pltpu.HBM(s, t) for s, t in outs], in_s...  54.6 us
    ppermute x54, starting transfers between devices, swap(): lax.ppermute(value, axis, [(s, s ^ mask) for s in range(lax.axis_size(axi...  52.3 us
    pallas_call x2, Pallas kernels, join_weights(): pl.pallas_call(partial(join_kernel, plan, io_out), out_shape=[pltpu.HBM(s...  32.3 us
    pallas_call x4, Pallas kernels, weight_grads(): pl.pallas_call(partial(grads_kernel, zone), out_shape=[jax.ShapeDtypeStru...  28.3 us
    all_to_all x3, waiting for transfers between devices, to_heads(): return lax.all_to_all(parts, 'seq', 0, 0, tiled=True)  20.4 us
    pallas_call x1, Pallas kernels, update_step(): pl.pallas_call(partial(shampoo_kernel, beta=beta_stat, rate=rate_shampoo,...  20.4 us
    pallas_call x9, Pallas kernels, stack_rows(): pl.pallas_call(kernel, out_shape=[jax.ShapeDtypeStruct(s, BF) for s in sh...  18.3 us
  transfers between devices with their start and end apart: 57, of which 39 were waited for; matrix products, arithmetic and copies ran while one was open for 1% of the time, Pallas kernels for 21%

profile of v1, /device:TPU:0, one launch (start us, length us, event | category | flops | bytes accessed | tf_op | source)
XLA Modules:
  0.0 394.8 jit_solution(14703221186966875376)
XLA Ops:
  0.6 2.8 pack_shard.1
  3.4 4.0 %collective-permute-start.7 = (bf16[1760,128]{1,0:T(8,128)(2,1)}, bf16[1760,128]{1,0:T(8,128)(2,1)S(1)}, u32[]{:S(2)}, u32[]{:S(2)}) collective-permute-start(bf16[1760,128]{1,0:T(8,128)(2,1)} %get-tuple-element.132), channel_id=1, source_target_pairs={{0,16},{2,18},{4,20},{6,22},{8,24},{10,26},{12,28},{14,30},{16,0},... | collective-permute-start | bytes 1351688 | tf_op jit(solution)/shard_map/ppermute | solution.py:564
  8.9 1.5 collective-permute-start.1
  10.5 1.6 collective-permute-start.4
  12.0 4.2 %collective-permute-done.refs_1_.refs_2_ = bf16[1168,128]{1,0:T(8,128)(2,1)S(1)} collective-permute-done((bf16[1168,128]{1,0:T(8,128)(2,1)}, bf16[1168,128]{1,0:T(8,128)(2,1)S(1)}, u32[]{:S(2)}, u32[]{:S(2)}) %collective-permute-start) | collective-permute-done | bytes 299040 | tf_op jit(solution)/shard_map/ppermute | solution.py:564
  19.9 1.6 collective-permute-start.2
  22.1 5.7 %collective-permute-done.7.refs_0_.refs_2_ = bf16[1760,128]{1,0:T(8,128)(2,1)S(1)} collective-permute-done((bf16[1760,128]{1,0:T(8,128)(2,1)}, bf16[1760,128]{1,0:T(8,128)(2,1)S(1)}, u32[]{:S(2)}, u32[]{:S(2)}) %collective-permute-start.7) | collective-permute-done | bytes 450592 | tf_op jit(solution)/shard_map/ppermute | solution.py:564
  27.8 1.6 collective-permute-start.9
  31.6 4.8 %collective-permute-done.2.refs_4_ = bf16[2336,128]{1,0:T(8,128)(2,1)S(1)} collective-permute-done((bf16[2336,128]{1,0:T(8,128)(2,1)S(1)}, bf16[2336,128]{1,0:T(8,128)(2,1)S(1)}, u32[]{:S(2)}, u32[]{:S(2)}) %collective-permute-start.2) | collective-permute-done | bytes 598048 | tf_op jit(solution)/shard_map/ppermute | solution.py:564
  36.4 1.5 collective-permute-start.6
  39.5 1.5 collective-permute-done.9.refs_3_.refs_2_
  44.7 2.8 collective-permute-done.10.refs_0_.refs_2_
  47.6 1.7 stack_rows.12
  49.4 2.0 collective-permute-start.11
  51.8 3.3 collective-permute-done.15.refs_3_.refs_2_
  55.7 7.8 %collective-permute-done.14.refs_1_ = bf16[880,128]{1,0:T(8,128)(2,1)S(1)} collective-permute-done((bf16[880,128]{1,0:T(8,128)(2,1)S(1)}, bf16[880,128]{1,0:T(8,128)(2,1)S(1)}, u32[]{:S(2)}, u32[]{:S(2)}) %collective-permute-start.14) | collective-permute-done | bytes 225312 | tf_op jit(solution)/shard_map/ppermute | solution.py:564
  65.0 1.7 stack_rows.14
  66.7 1.5 collective-permute-start.16
  68.3 1.7 stack_rows.16
  72.6 3.9 stack_rows.11.refs_0_
  76.5 1.8 stack_rows.13.refs_1_
  78.3 1.7 collective-permute-done.16.refs_3_
  80.1 3.3 collective-permute-done.17.refs_4_
  83.3 3.0 stack_rows.15.refs_2_
  86.9 2.7 collective-permute-done.20.refs_4_
  89.6 3.0 stack_rows.17.refs_3_
  97.7 14.2 %join_weights.2 = (bf16[768,2304]{1,0:T(8,128)(2,1)}, bf16[768,768]{1,0:T(8,128)(2,1)}, bf16[1536,768]{1,0:T(8,128)(2,1)}, f32[16,128]{1,0:T(8,128)S(1)}) custom-call(s32[768]{0:T(1024)S(1)} %copy-done.20, s32[768]{0:T(1024)S(1)} %fusion.11.row_ref, s32[2,32]{1,0:T(2,128)S(1)} %pad_add_fusion.io_ref, bf16[9344,128]{1,0:T(8,128)(2,1)} %stack_rows.11.refs_0_, ...), custom_call_target="tpu_custom_call" | custom-call | bytes 42900000 | tf_op jit(solution)/shard_map/join_weights/pallas_call | solution.py:740
  111.9 4.8 %front_step.1 = (f32[128,768]{1,0:T(8,128)}, bf16[2304,128]{1,0:T(8,128)(2,1)}, bf16[16,144,128]{2,1,0:T(8,128)(2,1)}) custom-call(bf16[128,1536]{1,0:T(8,128)(2,1)} %bitcast.28, f32[128,1]{1,0:T(8,128)} %convert_element_type.35.refs_1_.refs_4_.refs_3_, f32[128,768]{1,0:T(8,128)} %pad_maximum_fusion.refs_2_, f32[19,768]{1,0:T(8,128)} %vec_ref.1, ...), custom_call_target="tpu_custom_call" | custom-call | bytes 16500000 | tf_op jit(solution)/shard_map/front_step/pallas_call | solution.py:607
  116.7 5.9 %all-to-all-start = ((bf16[16,144,128]{2,1,0:T(8,128)(2,1)}), bf16[16,144,128]{2,1,0:T(8,128)(2,1)S(1)}, u32[]{:S(2)}, u32[]{:S(2)}) async-start(bf16[16,144,128]{2,1,0:T(8,128)(2,1)} %get-tuple-element.155), calls=%async_computation | async-start | bytes 1179648 | tf_op jit(solution)/shard_map/all_to_all | solution.py:1295
  122.7 18.1 %join_weights.3 = (bf16[768,3072]{1,0:T(8,128)(2,1)}, bf16[3072,768]{1,0:T(8,128)(2,1)}, bf16[1536,768]{1,0:T(8,128)(2,1)}, f32[16,128]{1,0:T(8,128)}) custom-call(s32[768]{0:T(1024)S(1)} %copy-done.20, s32[768]{0:T(1024)S(1)} %fusion.11.row_ref, s32[2,32]{1,0:T(2,128)S(1)} %pad_add_fusion.io_ref, bf16[9344,128]{1,0:T(8,128)(2,1)} %stack_rows.11.refs_0_, ...), custom_call_target="tpu_custom_call" | custom-call | bytes 56100000 | tf_op jit(solution)/shard_map/join_weights/pallas_call | solution.py:740
  141.6 12.6 %attend_forward.1 = (f32[48,2048]{1,0:T(8,128)}, bf16[16,48,128]{2,1,0:T(8,128)(2,1)}, f32[8,2048]{1,0:T(8,128)}) custom-call(s32[2,4]{1,0:T(2,128)S(1)} %copy-done.24, s32[2]{0:T(128)S(1)} %pad_add_fusion.1.refs_1_.ids_ref, bf16[16,144,128]{2,1,0:T(8,128)(2,1)} %copy-done.25), custom_call_target="tpu_custom_call" | custom-call | bytes 33000000 | tf_op jit(solution)/shard_map/attend_forward/pallas_call | solution.py:607
  154.2 7.2 %all-to-all-start.1 = ((bf16[16,48,128]{2,1,0:T(8,128)(2,1)}), bf16[16,48,128]{2,1,0:T(8,128)(2,1)S(1)}, u32[]{:S(2)}, u32[]{:S(2)}) async-start(bf16[16,48,128]{2,1,0:T(8,128)(2,1)} %get-tuple-element.161), calls=%async_computation.1 | async-start | bytes 393216 | tf_op jit(solution)/shard_map/all_to_all | solution.py:1295
  161.9 8.0 %all-to-all-done.1 = bf16[16,48,128]{2,1,0:T(8,128)(2,1)S(1)} async-done(((bf16[16,48,128]{2,1,0:T(8,128)(2,1)}), bf16[16,48,128]{2,1,0:T(8,128)(2,1)S(1)}, u32[]{:S(2)}, u32[]{:S(2)}) %all-to-all-start.1) | async-done | bytes 196640 | tf_op jit(solution)/shard_map/all_to_all | solution.py:1295
  170.6 14.4 %mlp_step.1 = (f32[128,768]{1,0:T(8,128)}, bf16[768,128]{1,0:T(8,128)(2,1)}, bf16[10752,128]{1,0:T(8,128)(2,1)}, f32[16,768]{1,0:T(8,128)}) custom-call(f32[1]{0:T(128)} %bitcast.9.refs_0_, f32[128,768]{1,0:T(8,128)} %get-tuple-element.160.refs_1_, bf16[768,128]{1,0:T(8,128)(2,1)} %bitcast.22, bf16[128,1536]{1,0:T(8,128)(2,1)} %bitcast.29, ...), custom_call_target="tpu_custom_call" | custom-call | bytes 42900000 | tf_op jit(solution)/shard_map/mlp_step/pallas_call | solution.py:607
  185.1 13.3 %all_to_all.20.refs_3_ = bf16[16,48,128]{2,1,0:T(8,128)(2,1)} all-to-all(bf16[16,48,128]{2,1,0:T(8,128)(2,1)} %bitcast.30), channel_id=1, replica_groups=mesh['seq'=16,'opt'=2] {'seq'}, dimensions={0} | all-to-all | bytes 393216 | tf_op jit(solution)/shard_map/all_to_all | solution.py:1295
  198.5 15.8 %attend_backward.1 = bf16[16,144,128]{2,1,0:T(8,128)(2,1)} custom-call(s32[2,4]{1,0:T(2,128)S(1)} %copy-done.24, s32[2]{0:T(128)S(1)} %pad_add_fusion.1.refs_1_.ids_ref, bf16[16,144,128]{2,1,0:T(8,128)(2,1)} %copy-done.25, bf16[16,48,128]{2,1,0:T(8,128)(2,1)} %all_to_all.20.refs_3_, f32[48,2048]{1,0:T(8,128)} %get-tuple-element.167.refs_4_, ...), custom_call_target="tpu_custom_call" | custom-call | bytes 42900000 | tf_op jit(solution)/shard_map/attend_backward/pallas_call | solution.py:607
  214.2 4.5 %all-to-all-start.3 = ((bf16[16,144,128]{2,1,0:T(8,128)(2,1)}), bf16[16,144,128]{2,1,0:T(8,128)(2,1)}, u32[]{:S(2)}, u32[]{:S(2)}) async-start(bf16[16,144,128]{2,1,0:T(8,128)(2,1)} %attend_backward.1), calls=%async_computation.3 | async-start | bytes 1179648 | tf_op jit(solution)/shard_map/all_to_all | solution.py:1295
  222.3 12.4 %all-to-all-done.3.refs_0_ = bf16[16,144,128]{2,1,0:T(8,128)(2,1)} async-done(((bf16[16,144,128]{2,1,0:T(8,128)(2,1)}), bf16[16,144,128]{2,1,0:T(8,128)(2,1)}, u32[]{:S(2)}, u32[]{:S(2)}) %all-to-all-start.3) | async-done | bytes 589856 | tf_op jit(solution)/shard_map/all_to_all | solution.py:1295
  234.7 6.9 %input_step.1 = (bf16[3072,128]{1,0:T(8,128)(2,1)}, f32[24,768]{1,0:T(8,128)}) custom-call(bf16[16,144,128]{2,1,0:T(8,128)(2,1)} %all-to-all-done.3.refs_0_, f32[128,768]{1,0:T(8,128)} %get-tuple-element.160.refs_1_, f32[128,768]{1,0:T(8,128)} %get-tuple-element.173.refs_2_, f32[128,1]{1,0:T(8,128)} %convert_element_type.35.refs_1_.refs_4_.refs_3_, ...), custom_call_target="tpu_custom_call" | custom-call | bytes 16500000 | tf_op jit(solution)/shard_map/input_step/pallas_call | solution.py:607
  241.7 2.5 collective-permute-done.29.refs_7_
  245.4 6.9 %weight_grads.6 = (s16[2,1184,128]{2,1,0:T(8,128)(2,1)S(1)}, s16[2,1184,128]{2,1,0:T(8,128)(2,1)S(1)}, s16[2,1184,128]{2,1,0:T(8,128)(2,1)S(1)}, s16[2,1184,128]{2,1,0:T(8,128)(2,1)S(1)}) custom-call(s32[2]{0:T(128)S(1)} %pad_add_fusion.1.refs_1_.ids_ref, s32[768]{0:T(1024)S(1)} %copy-done.20, bf16[2304,128]{1,0:T(8,128)(2,1)S(1)} %copy-done.3, ...), custom_call_target="tpu_custom_call" | custom-call | bytes 2640000 | tf_op jit(solution)/shard_map/weight_grads/pallas_call | solution.py:1122
  254.0 7.3 %weight_grads.5 = (s16[2,1184,128]{2,1,0:T(8,128)(2,1)S(1)}, s16[2,1184,128]{2,1,0:T(8,128)(2,1)S(1)}, s16[2,1184,128]{2,1,0:T(8,128)(2,1)S(1)}, s16[2,1184,128]{2,1,0:T(8,128)(2,1)S(1)}) custom-call(s32[2]{0:T(128)S(1)} %pad_add_fusion.1.refs_1_.ids_ref, s32[768]{0:T(1024)S(1)} %copy-done.20, bf16[2304,128]{1,0:T(8,128)(2,1)S(1)} %copy-done.3, ...), custom_call_target="tpu_custom_call" | custom-call | bytes 2640000 | tf_op jit(solution)/shard_map/weight_grads/pallas_call | solution.py:1122
  263.8 6.9 %weight_grads.4 = (s16[2,1184,128]{2,1,0:T(8,128)(2,1)S(1)}, s16[2,1184,128]{2,1,0:T(8,128)(2,1)S(1)}, s16[2,1184,128]{2,1,0:T(8,128)(2,1)S(1)}, s16[2,1184,128]{2,1,0:T(8,128)(2,1)S(1)}) custom-call(s32[2]{0:T(128)S(1)} %pad_add_fusion.1.refs_1_.ids_ref, s32[768]{0:T(1024)S(1)} %copy-done.20, bf16[2304,128]{1,0:T(8,128)(2,1)S(1)} %copy-done.3, ...), custom_call_target="tpu_custom_call" | custom-call | bytes 2640000 | tf_op jit(solution)/shard_map/weight_grads/pallas_call | solution.py:1122
  270.8 10.3 %collective-permute-done.30.refs_1_ = s16[2,1184,128]{2,1,0:T(8,128)(2,1)S(1)} collective-permute-done((s16[2,1184,128]{2,1,0:T(8,128)(2,1)S(1)}, s16[2,1184,128]{2,1,0:T(8,128)(2,1)S(1)}, u32[]{:S(2)}, u32[]{:S(2)}) %collective-permute-start.30) | collective-permute-done | bytes 606240 | tf_op jit(solution)/shard_map/ppermute | solution.py:564
  281.9 2.6 add_plane.3
  288.6 6.1 %collective-permute-done.34.refs_1_ = s16[1184,128]{1,0:T(8,128)(2,1)S(1)} collective-permute-done((s16[1184,128]{1,0:T(8,128)(2,1)S(1)}, s16[1184,128]{1,0:T(8,128)(2,1)S(1)}, u32[]{:S(2)}, u32[]{:S(2)}) %collective-permute-start.34) | collective-permute-done | bytes 303136 | tf_op jit(solution)/shard_map/ppermute | solution.py:564
  295.2 3.9 collective-permute-done.36.refs_1_
  302.5 1.5 collective-permute-start.40
  304.0 7.1 %weight_grads.7 = (s16[2,1184,128]{2,1,0:T(8,128)(2,1)S(1)}, s16[2,1184,128]{2,1,0:T(8,128)(2,1)S(1)}, s16[2,1184,128]{2,1,0:T(8,128)(2,1)S(1)}, s16[2,1184,128]{2,1,0:T(8,128)(2,1)S(1)}) custom-call(s32[2]{0:T(128)S(1)} %pad_add_fusion.1.refs_1_.ids_ref, s32[768]{0:T(1024)S(1)} %copy-done.20, bf16[2304,128]{1,0:T(8,128)(2,1)S(1)} %copy-done.3, ...), custom_call_target="tpu_custom_call" | custom-call | bytes 2640000 | tf_op jit(solution)/shard_map/weight_grads/pallas_call | solution.py:1122
  311.1 1.6 collective-permute-done.38.refs_1_
  313.4 1.9 collective-permute-done.40.refs_4_
  318.3 6.3 %collective-permute-done.41.refs_1_ = s16[1184,128]{1,0:T(8,128)(2,1)S(1)} collective-permute-done((s16[1184,128]{1,0:T(8,128)(2,1)S(1)}, s16[1184,128]{1,0:T(8,128)(2,1)S(1)}, u32[]{:S(2)}, u32[]{:S(2)}) %collective-permute-start.41) | collective-permute-done | bytes 303136 | tf_op jit(solution)/shard_map/ppermute | solution.py:564
  324.6 2.0 collective-permute-done.42.refs_3_
  331.5 2.1 collective-permute-start.47
  333.6 4.2 %collective-permute-done.43.refs_1_ = s16[2,1184,128]{2,1,0:T(8,128)(2,1)S(1)} collective-permute-done((s16[2,1184,128]{2,1,0:T(8,128)(2,1)S(1)}, s16[2,1184,128]{2,1,0:T(8,128)(2,1)S(1)}, u32[]{:S(2)}, u32[]{:S(2)}) %collective-permute-start.43) | collective-permute-done | bytes 606240 | tf_op jit(solution)/shard_map/ppermute | solution.py:564
  337.8 2.6 collective-permute-done.44.refs_3_
  341.9 1.5 collective-permute-start.45
  344.3 7.0 %collective-permute-done.48.refs_5_ = s16[2,1184,128]{2,1,0:T(8,128)(2,1)S(1)} collective-permute-done((s16[2,1184,128]{2,1,0:T(8,128)(2,1)S(1)}, s16[2,1184,128]{2,1,0:T(8,128)(2,1)S(1)}, u32[]{:S(2)}, u32[]{:S(2)}) %collective-permute-start.48) | collective-permute-done | bytes 606240 | tf_op jit(solution)/shard_map/ppermute | solution.py:564
  355.0 3.1 collective-permute-done.50
  359.1 3.4 collective-permute-done.51
  363.1 3.9 collective-permute-done.52
  367.0 2.2 collective-permute-start.53
  369.2 3.9 collective-permute-done.53
  373.7 20.4 %update_step.1 = (f32[24,96,96]{2,1,0:T(8,128)}, f32[24,96,96]{2,1,0:T(8,128)}, f32[24,96,96]{2,1,0:T(8,128)}, f32[24,96,96]{2,1,0:T(8,128)}, f32[48,2,768]{2,1,...) custom-call(f32[24,768]{1,0:T(8,128)S(1)} %add.366.sums_ref, ...), custom_call_target="tpu_custom_call" | custom-call | tf_op jit(solution)/shard_map/update_step/pallas_call | solution.py:1277
  (169 shorter events, 61.0 us)
Async XLA Ops:
  3.4 24.4 %collective-permute-start.7 = (bf16[1760,128]{1,0:T(8,128)(2,1)}, bf16[1760,128]{1,0:T(8,128)(2,1)S(1)}, u32[]{:S(2)}, u32[]{:S(2)}) collective-permute-start(bf16[1760,128]{1,0:T(8,128)(2,1)} %get-tuple-element.132), channel_id=1, source_target_pairs={{0,16},{2,18},{4,20},{6,22},{8,24},{10,26},{12,28},{14,30},{16,0},... | collective-permute-start | bytes 1351688 | tf_op jit(solution)/shard_map/ppermute | solution.py:564
  7.4 8.8 %collective-permute-start = (bf16[1168,128]{1,0:T(8,128)(2,1)}, bf16[1168,128]{1,0:T(8,128)(2,1)S(1)}, u32[]{:S(2)}, u32[]{:S(2)}) collective-permute-start(bf16[1168,128]{1,0:T(8,128)(2,1)} %get-tuple-element.128.refs_0_), channel_id=1, source_target_pairs={{0,2},{2,0},{4,6},{6,4},{8,10},{10,8},{12,14},{14,12},{16,18},{18,... | collective-permute-start | bytes 897032 | tf_op jit(solution)/shard_map/ppermute | solution.py:564
  8.9 8.5 %collective-permute-start.1 = (bf16[1168,128]{1,0:T(8,128)(2,1)}, bf16[1168,128]{1,0:T(8,128)(2,1)S(1)}, u32[]{:S(2)}, u32[]{:S(2)}) collective-permute-start(bf16[1168,128]{1,0:T(8,128)(2,1)} %get-tuple-element.129.refs_2_.refs_1_), channel_id=1, source_target_pairs={{0,4},{2,6},{4,0},{6,2},{8,12},{10,14},{12,8},{14,10},{16,20},{18,... | collective-permute-start | bytes 897032 | tf_op jit(solution)/shard_map/ppermute | solution.py:564
  10.5 20.5 %collective-permute-start.4 = (bf16[1760,128]{1,0:T(8,128)(2,1)}, bf16[1760,128]{1,0:T(8,128)(2,1)S(1)}, u32[]{:S(2)}, u32[]{:S(2)}) collective-permute-start(bf16[1760,128]{1,0:T(8,128)(2,1)} %get-tuple-element.132), channel_id=1, source_target_pairs={{0,8},{2,10},{4,12},{6,14},{8,0},{10,2},{12,4},{14,6},{16,24},{18,... | collective-permute-start | bytes 1351688 | tf_op jit(solution)/shard_map/ppermute | solution.py:564
  19.9 16.5 %collective-permute-start.2 = (bf16[2336,128]{1,0:T(8,128)(2,1)S(1)}, bf16[2336,128]{1,0:T(8,128)(2,1)S(1)}, u32[]{:S(2)}, u32[]{:S(2)}) collective-permute-start(bf16[2336,128]{1,0:T(8,128)(2,1)S(1)} %get-tuple-element.130), channel_id=1, source_target_pairs={{0,4},{2,6},{4,0},{6,2},{8,12},{10,14},{12,8},{14,10},{16,20},{18,... | collective-permute-start | bytes 1794056 | tf_op jit(solution)/shard_map/ppermute | solution.py:564
  21.5 16.4 %collective-permute-start.3 = (bf16[2336,128]{1,0:T(8,128)(2,1)S(1)}, bf16[2336,128]{1,0:T(8,128)(2,1)S(1)}, u32[]{:S(2)}, u32[]{:S(2)}) collective-permute-start(bf16[2336,128]{1,0:T(8,128)(2,1)S(1)} %get-tuple-element.131), channel_id=1, source_target_pairs={{0,2},{2,0},{4,6},{6,4},{8,10},{10,8},{12,14},{14,12},{16,18},{18,... | collective-permute-start | bytes 1794056 | tf_op jit(solution)/shard_map/ppermute | solution.py:564
  27.8 13.2 %collective-permute-start.9 = (bf16[880,128]{1,0:T(8,128)(2,1)S(1)}, bf16[880,128]{1,0:T(8,128)(2,1)S(1)}, u32[]{:S(2)}, u32[]{:S(2)}) collective-permute-start(bf16[880,128]{1,0:T(8,128)(2,1)S(1)} %get-tuple-element.245), channel_id=1, source_target_pairs={{0,4},{2,6},{4,0},{6,2},{8,12},{10,14},{12,8},{14,10},{16,20},{18,... | collective-permute-start | bytes 675848 | tf_op jit(solution)/shard_map/ppermute | solution.py:564
  29.4 12.8 %collective-permute-start.8 = (bf16[880,128]{1,0:T(8,128)(2,1)S(1)}, bf16[880,128]{1,0:T(8,128)(2,1)S(1)}, u32[]{:S(2)}, u32[]{:S(2)}) collective-permute-start(bf16[880,128]{1,0:T(8,128)(2,1)S(1)} %get-tuple-element.246), channel_id=1, source_target_pairs={{0,2},{2,0},{4,6},{6,4},{8,10},{10,8},{12,14},{14,12},{16,18},{18,... | collective-permute-start | bytes 675848 | tf_op jit(solution)/shard_map/ppermute | solution.py:564
  30.9 16.5 %collective-permute-start.10 = (bf16[1760,128]{1,0:T(8,128)(2,1)S(1)}, bf16[1760,128]{1,0:T(8,128)(2,1)S(1)}, u32[]{:S(2)}, u32[]{:S(2)}) collective-permute-start(bf16[1760,128]{1,0:T(8,128)(2,1)S(1)} %collective-permute-done.7.refs_0_.refs_2_), channel_id=1, source_target_pairs={{0,8},{2,10},{4,12},{6,14},{8,0},{10,2},{12,4},{14,6},{16,24},{18,... | collective-permute-start | bytes 1351688 | tf_op jit(solution)/shard_map/ppermute | solution.py:564
  36.4 7.0 %collective-permute-start.6 = (bf16[880,128]{1,0:T(8,128)(2,1)S(1)}, bf16[880,128]{1,0:T(8,128)(2,1)S(1)}, u32[]{:S(2)}, u32[]{:S(2)}) collective-permute-start(bf16[880,128]{1,0:T(8,128)(2,1)S(1)} %get-tuple-element.247), channel_id=1, source_target_pairs={{0,4},{2,6},{4,0},{6,2},{8,12},{10,14},{12,8},{14,10},{16,20},{18,... | collective-permute-start | bytes 675848 | tf_op jit(solution)/shard_map/ppermute | solution.py:564
  38.0 6.7 %collective-permute-start.5 = (bf16[880,128]{1,0:T(8,128)(2,1)S(1)}, bf16[880,128]{1,0:T(8,128)(2,1)S(1)}, u32[]{:S(2)}, u32[]{:S(2)}) collective-permute-start(bf16[880,128]{1,0:T(8,128)(2,1)S(1)} %get-tuple-element.248), channel_id=1, source_target_pairs={{0,2},{2,0},{4,6},{6,4},{8,10},{10,8},{12,14},{14,12},{16,18},{18,... | collective-permute-start | bytes 675848 | tf_op jit(solution)/shard_map/ppermute | solution.py:564
  39.4 33.2 %copy-start.13 = (bf16[1168,128]{1,0:T(8,128)(2,1)S(1)}, bf16[1168,128]{1,0:T(8,128)(2,1)}, u32[]{:S(2)}) copy-start(bf16[1168,128]{1,0:T(8,128)(2,1)} %get-tuple-element.129.refs_2_.refs_1_) | copy-start | bytes 897028
  41.0 23.9 %collective-permute-start.18 = (bf16[2304,128]{1,0:T(8,128)(2,1)S(1)}, bf16[2304,128]{1,0:T(8,128)(2,1)S(1)}, u32[]{:S(2)}, u32[]{:S(2)}) collective-permute-start(bf16[2304,128]{1,0:T(8,128)(2,1)S(1)} %stack_rows.10.refs_6_), channel_id=1, source_target_pairs={{0,16},{2,18},{4,20},{6,22},{8,24},{10,26},{12,28},{14,30},{16,0},... | collective-permute-start | bytes 1769480 | tf_op jit(solution)/shard_map/ppermute | solution.py:564
  47.4 7.7 %collective-permute-start.15 = (bf16[880,128]{1,0:T(8,128)(2,1)S(1)}, bf16[880,128]{1,0:T(8,128)(2,1)S(1)}, u32[]{:S(2)}, u32[]{:S(2)}) collective-permute-start(bf16[880,128]{1,0:T(8,128)(2,1)S(1)} %get-tuple-element.243), channel_id=1, source_target_pairs={{0,4},{2,6},{4,0},{6,2},{8,12},{10,14},{12,8},{14,10},{16,20},{18,... | collective-permute-start | bytes 675848 | tf_op jit(solution)/shard_map/ppermute | solution.py:564
  47.5 23.9 %collective-permute-start.13 = (bf16[2304,128]{1,0:T(8,128)(2,1)S(1)}, bf16[2304,128]{1,0:T(8,128)(2,1)S(1)}, u32[]{:S(2)}, u32[]{:S(2)}) collective-permute-start(bf16[2304,128]{1,0:T(8,128)(2,1)S(1)} %stack_rows.10.refs_6_), channel_id=1, source_target_pairs={{0,8},{2,10},{4,12},{6,14},{8,0},{10,2},{12,4},{14,6},{16,24},{18,... | collective-permute-start | bytes 1769480 | tf_op jit(solution)/shard_map/ppermute | solution.py:564
  49.4 20.6 %collective-permute-start.11 = (bf16[1760,128]{1,0:T(8,128)(2,1)S(1)}, bf16[1760,128]{1,0:T(8,128)(2,1)S(1)}, u32[]{:S(2)}, u32[]{:S(2)}) collective-permute-start(bf16[1760,128]{1,0:T(8,128)(2,1)S(1)} %get-tuple-element.135), channel_id=1, source_target_pairs={{0,4},{2,6},{4,0},{6,2},{8,12},{10,14},{12,8},{14,10},{16,20},{18,... | collective-permute-start | bytes 1351688 | tf_op jit(solution)/shard_map/ppermute | solution.py:564
  51.3 19.5 %collective-permute-start.12 = (bf16[1760,128]{1,0:T(8,128)(2,1)S(1)}, bf16[1760,128]{1,0:T(8,128)(2,1)S(1)}, u32[]{:S(2)}, u32[]{:S(2)}) collective-permute-start(bf16[1760,128]{1,0:T(8,128)(2,1)S(1)} %get-tuple-element.136), channel_id=1, source_target_pairs={{0,2},{2,0},{4,6},{6,4},{8,10},{10,8},{12,14},{14,12},{16,18},{18,... | collective-permute-start | bytes 1351688 | tf_op jit(solution)/shard_map/ppermute | solution.py:564
  55.1 8.4 %collective-permute-start.14 = (bf16[880,128]{1,0:T(8,128)(2,1)S(1)}, bf16[880,128]{1,0:T(8,128)(2,1)S(1)}, u32[]{:S(2)}, u32[]{:S(2)}) collective-permute-start(bf16[880,128]{1,0:T(8,128)(2,1)S(1)} %get-tuple-element.244), channel_id=1, source_target_pairs={{0,2},{2,0},{4,6},{6,4},{8,10},{10,8},{12,14},{14,12},{16,18},{18,... | collective-permute-start | bytes 675848 | tf_op jit(solution)/shard_map/ppermute | solution.py:564
  64.9 24.7 %collective-permute-start.21 = (bf16[2304,128]{1,0:T(8,128)(2,1)S(1)}, bf16[2304,128]{1,0:T(8,128)(2,1)S(1)}, u32[]{:S(2)}, u32[]{:S(2)}) collective-permute-start(bf16[2304,128]{1,0:T(8,128)(2,1)S(1)} %collective-permute-done.18.refs_5_), channel_id=1, source_target_pairs={{0,8},{2,10},{4,12},{6,14},{8,0},{10,2},{12,4},{14,6},{16,24},{18,... | collective-permute-start | bytes 1769480 | tf_op jit(solution)/shard_map/ppermute | solution.py:564
  66.7 13.3 %collective-permute-start.16 = (bf16[1760,128]{1,0:T(8,128)(2,1)S(1)}, bf16[1760,128]{1,0:T(8,128)(2,1)S(1)}, u32[]{:S(2)}, u32[]{:S(2)}) collective-permute-start(bf16[1760,128]{1,0:T(8,128)(2,1)S(1)} %get-tuple-element.142), channel_id=1, source_target_pairs={{0,4},{2,6},{4,0},{6,2},{8,12},{10,14},{12,8},{14,10},{16,20},{18,... | collective-permute-start | bytes 1351688 | tf_op jit(solution)/shard_map/ppermute | solution.py:564
  70.0 13.3 %collective-permute-start.17 = (bf16[1760,128]{1,0:T(8,128)(2,1)S(1)}, bf16[1760,128]{1,0:T(8,128)(2,1)S(1)}, u32[]{:S(2)}, u32[]{:S(2)}) collective-permute-start(bf16[1760,128]{1,0:T(8,128)(2,1)S(1)} %get-tuple-element.143), channel_id=1, source_target_pairs={{0,2},{2,0},{4,6},{6,4},{8,10},{10,8},{12,14},{14,12},{16,18},{18,... | collective-permute-start | bytes 1351688 | tf_op jit(solution)/shard_map/ppermute | solution.py:564
  70.9 15.5 %collective-permute-start.19 = (bf16[1760,128]{1,0:T(8,128)(2,1)S(1)}, bf16[1760,128]{1,0:T(8,128)(2,1)S(1)}, u32[]{:S(2)}, u32[]{:S(2)}) collective-permute-start(bf16[1760,128]{1,0:T(8,128)(2,1)S(1)} %get-tuple-element.149), channel_id=1, source_target_pairs={{0,4},{2,6},{4,0},{6,2},{8,12},{10,14},{12,8},{14,10},{16,20},{18,... | collective-permute-start | bytes 1351688 | tf_op jit(solution)/shard_map/ppermute | solution.py:564
  71.5 18.2 %collective-permute-start.20 = (bf16[1760,128]{1,0:T(8,128)(2,1)S(1)}, bf16[1760,128]{1,0:T(8,128)(2,1)S(1)}, u32[]{:S(2)}, u32[]{:S(2)}) collective-permute-start(bf16[1760,128]{1,0:T(8,128)(2,1)S(1)} %get-tuple-element.150), channel_id=1, source_target_pairs={{0,2},{2,0},{4,6},{6,4},{8,10},{10,8},{12,14},{14,12},{16,18},{18,... | collective-permute-start | bytes 1351688 | tf_op jit(solution)/shard_map/ppermute | solution.py:564
  80.1 16.8 %collective-permute-start.22 = (bf16[9344,128]{1,0:T(8,128)(2,1)}, bf16[9344,128]{1,0:T(8,128)(2,1)}, u32[]{:S(2)}, u32[]{:S(2)}) collective-permute-start(bf16[9344,128]{1,0:T(8,128)(2,1)} %stack_rows.11.refs_0_), channel_id=1, source_target_pairs={{0,1},{1,0},{2,3},{3,2},{4,5},{5,4},{6,7},{7,6},{8,9},{9,8},{10,11... | collective-permute-start | bytes 7176200 | tf_op jit(solution)/shard_map/ppermute | solution.py:564
  83.3 13.6 %collective-permute-start.23 = (bf16[9344,128]{1,0:T(8,128)(2,1)S(1)}, bf16[9344,128]{1,0:T(8,128)(2,1)}, u32[]{:S(2)}, u32[]{:S(2)}) collective-permute-start(bf16[9344,128]{1,0:T(8,128)(2,1)S(1)} %stack_rows.13.refs_1_), channel_id=1, source_target_pairs={{0,1},{1,0},{2,3},{3,2},{4,5},{5,4},{6,7},{7,6},{8,9},{9,8},{10,11... | collective-permute-start | bytes 7176200 | tf_op jit(solution)/shard_map/ppermute | solution.py:564
  86.4 10.5 %collective-permute-start.24 = (bf16[9344,128]{1,0:T(8,128)(2,1)}, bf16[9344,128]{1,0:T(8,128)(2,1)}, u32[]{:S(2)}, u32[]{:S(2)}) collective-permute-start(bf16[9344,128]{1,0:T(8,128)(2,1)} %stack_rows.15.refs_2_), channel_id=1, source_target_pairs={{0,1},{1,0},{2,3},{3,2},{4,5},{5,4},{6,7},{7,6},{8,9},{9,8},{10,11... | collective-permute-start | bytes 7176200 | tf_op jit(solution)/shard_map/ppermute | solution.py:564
  92.7 5.0 %collective-permute-start.25 = (bf16[9344,128]{1,0:T(8,128)(2,1)}, bf16[9344,128]{1,0:T(8,128)(2,1)}, u32[]{:S(2)}, u32[]{:S(2)}) collective-permute-start(bf16[9344,128]{1,0:T(8,128)(2,1)} %stack_rows.17.refs_3_), channel_id=1, source_target_pairs={{0,1},{1,0},{2,3},{3,2},{4,5},{5,4},{6,7},{7,6},{8,9},{9,8},{10,11... | collective-permute-start | bytes 7176200 | tf_op jit(solution)/shard_map/ppermute | solution.py:564
  116.7 24.0 %all-to-all-start = ((bf16[16,144,128]{2,1,0:T(8,128)(2,1)}), bf16[16,144,128]{2,1,0:T(8,128)(2,1)S(1)}, u32[]{:S(2)}, u32[]{:S(2)}) async-start(bf16[16,144,128]{2,1,0:T(8,128)(2,1)} %get-tuple-element.155), calls=%async_computation | async-start | bytes 1179648 | tf_op jit(solution)/shard_map/all_to_all | solution.py:1295
  154.2 15.7 %all-to-all-start.1 = ((bf16[16,48,128]{2,1,0:T(8,128)(2,1)}), bf16[16,48,128]{2,1,0:T(8,128)(2,1)S(1)}, u32[]{:S(2)}, u32[]{:S(2)}) async-start(bf16[16,48,128]{2,1,0:T(8,128)(2,1)} %get-tuple-element.161), calls=%async_computation.1 | async-start | bytes 393216 | tf_op jit(solution)/shard_map/all_to_all | solution.py:1295
  185.0 33.7 %copy-start.3 = (bf16[2304,128]{1,0:T(8,128)(2,1)S(1)}, bf16[2304,128]{1,0:T(8,128)(2,1)}, u32[]{:S(2)}) copy-start(bf16[2304,128]{1,0:T(8,128)(2,1)} %get-tuple-element.153.refs_0_) | copy-start | bytes 1769476
  185.0 33.8 %copy-start.7 = (bf16[16,48,128]{2,1,0:T(8,128)(2,1)S(1)}, bf16[16,48,128]{2,1,0:T(8,128)(2,1)}, u32[]{:S(2)}) copy-start(bf16[16,48,128]{2,1,0:T(8,128)(2,1)} %copy-done.6) | copy-start | bytes 589828
  185.0 59.2 %collective-permute-start.28 = (bf16[10752,128]{1,0:T(8,128)(2,1)}, bf16[10752,128]{1,0:T(8,128)(2,1)S(1)}, u32[]{:S(2)}, u32[]{:S(2)}) collective-permute-start(bf16[10752,128]{1,0:T(8,128)(2,1)} %get-tuple-element.171.refs_4_), channel_id=1, source_target_pairs={{0,1},{1,0},{2,3},{3,2},{4,5},{5,4},{6,7},{7,6},{8,9},{9,8},{10,11... | collective-permute-start | bytes 8257544 | tf_op jit(solution)/shard_map/ppermute | solution.py:564
  214.2 20.5 %all-to-all-start.3 = ((bf16[16,144,128]{2,1,0:T(8,128)(2,1)}), bf16[16,144,128]{2,1,0:T(8,128)(2,1)}, u32[]{:S(2)}, u32[]{:S(2)}) async-start(bf16[16,144,128]{2,1,0:T(8,128)(2,1)} %attend_backward.1), calls=%async_computation.3 | async-start | bytes 1179648 | tf_op jit(solution)/shard_map/all_to_all | solution.py:1295
  218.7 2.1 collective-permute-start.26
  218.8 2.8 collective-permute-start.27
  241.6 2.6 collective-permute-start.29
  252.3 18.5 %collective-permute-start.32 = (s16[2,1184,128]{2,1,0:T(8,128)(2,1)S(1)}, s16[2,1184,128]{2,1,0:T(8,128)(2,1)S(1)}, u32[]{:S(2)}, u32[]{:S(2)}) collective-permute-start(s16[2,1184,128]{2,1,0:T(8,128)(2,1)S(1)} %get-tuple-element.181), channel_id=1, source_target_pairs={{0,4},{2,6},{4,0},{6,2},{8,12},{10,14},{12,8},{14,10},{16,20},{18,... | collective-permute-start | bytes 1818632 | tf_op jit(solution)/shard_map/ppermute | solution.py:564
  253.4 17.3 %collective-permute-start.33 = (s16[2,1184,128]{2,1,0:T(8,128)(2,1)S(1)}, s16[2,1184,128]{2,1,0:T(8,128)(2,1)S(1)}, u32[]{:S(2)}, u32[]{:S(2)}) collective-permute-start(s16[2,1184,128]{2,1,0:T(8,128)(2,1)S(1)} %get-tuple-element.182), channel_id=1, source_target_pairs={{0,2},{2,0},{4,6},{6,4},{8,10},{10,8},{12,14},{14,12},{16,18},{18,... | collective-permute-start | bytes 1818632 | tf_op jit(solution)/shard_map/ppermute | solution.py:564
  261.3 19.7 %collective-permute-start.30 = (s16[2,1184,128]{2,1,0:T(8,128)(2,1)S(1)}, s16[2,1184,128]{2,1,0:T(8,128)(2,1)S(1)}, u32[]{:S(2)}, u32[]{:S(2)}) collective-permute-start(s16[2,1184,128]{2,1,0:T(8,128)(2,1)S(1)} %get-tuple-element.179), channel_id=1, source_target_pairs={{0,4},{2,6},{4,0},{6,2},{8,12},{10,14},{12,8},{14,10},{16,20},{18,... | collective-permute-start | bytes 1818632 | tf_op jit(solution)/shard_map/ppermute | solution.py:564
  262.3 19.5 %collective-permute-start.31 = (s16[2,1184,128]{2,1,0:T(8,128)(2,1)S(1)}, s16[2,1184,128]{2,1,0:T(8,128)(2,1)S(1)}, u32[]{:S(2)}, u32[]{:S(2)}) collective-permute-start(s16[2,1184,128]{2,1,0:T(8,128)(2,1)S(1)} %get-tuple-element.180), channel_id=1, source_target_pairs={{0,2},{2,0},{4,6},{6,4},{8,10},{10,8},{12,14},{14,12},{16,18},{18,... | collective-permute-start | bytes 1818632 | tf_op jit(solution)/shard_map/ppermute | solution.py:564
  284.5 10.2 %collective-permute-start.34 = (s16[1184,128]{1,0:T(8,128)(2,1)S(1)}, s16[1184,128]{1,0:T(8,128)(2,1)S(1)}, u32[]{:S(2)}, u32[]{:S(2)}) collective-permute-start(s16[1184,128]{1,0:T(8,128)(2,1)S(1)} %get-tuple-element.192), channel_id=1, source_target_pairs={{0,2},{2,0},{4,6},{6,4},{8,10},{10,8},{12,14},{14,12},{16,18},{18,... | collective-permute-start | bytes 909320 | tf_op jit(solution)/shard_map/ppermute | solution.py:564
  285.1 10.1 %collective-permute-start.35 = (s16[1184,128]{1,0:T(8,128)(2,1)S(1)}, s16[1184,128]{1,0:T(8,128)(2,1)S(1)}, u32[]{:S(2)}, u32[]{:S(2)}) collective-permute-start(s16[1184,128]{1,0:T(8,128)(2,1)S(1)} %get-tuple-element.193), channel_id=1, source_target_pairs={{0,4},{2,6},{4,0},{6,2},{8,12},{10,14},{12,8},{14,10},{16,20},{18,... | collective-permute-start | bytes 909320 | tf_op jit(solution)/shard_map/ppermute | solution.py:564
  286.0 13.0 %collective-permute-start.36 = (s16[1184,128]{1,0:T(8,128)(2,1)S(1)}, s16[1184,128]{1,0:T(8,128)(2,1)S(1)}, u32[]{:S(2)}, u32[]{:S(2)}) collective-permute-start(s16[1184,128]{1,0:T(8,128)(2,1)S(1)} %get-tuple-element.194), channel_id=1, source_target_pairs={{0,2},{2,0},{4,6},{6,4},{8,10},{10,8},{12,14},{14,12},{16,18},{18,... | collective-permute-start | bytes 909320 | tf_op jit(solution)/shard_map/ppermute | solution.py:564
  287.5 11.9 %collective-permute-start.37 = (s16[1184,128]{1,0:T(8,128)(2,1)S(1)}, s16[1184,128]{1,0:T(8,128)(2,1)S(1)}, u32[]{:S(2)}, u32[]{:S(2)}) collective-permute-start(s16[1184,128]{1,0:T(8,128)(2,1)S(1)} %get-tuple-element.195), channel_id=1, source_target_pairs={{0,4},{2,6},{4,0},{6,2},{8,12},{10,14},{12,8},{14,10},{16,20},{18,... | collective-permute-start | bytes 909320 | tf_op jit(solution)/shard_map/ppermute | solution.py:564
  299.4 13.4 %collective-permute-start.38 = (s16[2,1184,128]{2,1,0:T(8,128)(2,1)S(1)}, s16[2,1184,128]{2,1,0:T(8,128)(2,1)S(1)}, u32[]{:S(2)}, u32[]{:S(2)}) collective-permute-start(s16[2,1184,128]{2,1,0:T(8,128)(2,1)S(1)} %get-tuple-element.196), channel_id=1, source_target_pairs={{0,4},{2,6},{4,0},{6,2},{8,12},{10,14},{12,8},{14,10},{16,20},{18,... | collective-permute-start | bytes 1818632 | tf_op jit(solution)/shard_map/ppermute | solution.py:564
  300.3 13.1 %collective-permute-start.39 = (s16[2,1184,128]{2,1,0:T(8,128)(2,1)S(1)}, s16[2,1184,128]{2,1,0:T(8,128)(2,1)S(1)}, u32[]{:S(2)}, u32[]{:S(2)}) collective-permute-start(s16[2,1184,128]{2,1,0:T(8,128)(2,1)S(1)} %get-tuple-element.197), channel_id=1, source_target_pairs={{0,2},{2,0},{4,6},{6,4},{8,10},{10,8},{12,14},{14,12},{16,18},{18,... | collective-permute-start | bytes 1818632 | tf_op jit(solution)/shard_map/ppermute | solution.py:564
  302.5 12.9 %collective-permute-start.40 = (s16[2,1184,128]{2,1,0:T(8,128)(2,1)S(1)}, s16[2,1184,128]{2,1,0:T(8,128)(2,1)S(1)}, u32[]{:S(2)}, u32[]{:S(2)}) collective-permute-start(s16[2,1184,128]{2,1,0:T(8,128)(2,1)S(1)} %add_line.3), channel_id=1, source_target_pairs={{0,8},{2,10},{4,12},{6,14},{8,0},{10,2},{12,4},{14,6},{16,24},{18,... | collective-permute-start | bytes 1818632 | tf_op jit(solution)/shard_map/ppermute | solution.py:564
  316.6 8.0 %collective-permute-start.41 = (s16[1184,128]{1,0:T(8,128)(2,1)S(1)}, s16[1184,128]{1,0:T(8,128)(2,1)S(1)}, u32[]{:S(2)}, u32[]{:S(2)}) collective-permute-start(s16[1184,128]{1,0:T(8,128)(2,1)S(1)} %get-tuple-element.212), channel_id=1, source_target_pairs={{0,2},{2,0},{4,6},{6,4},{8,10},{10,8},{12,14},{14,12},{16,18},{18,... | collective-permute-start | bytes 909320 | tf_op jit(solution)/shard_map/ppermute | solution.py:564
  317.3 9.4 %collective-permute-start.42 = (s16[1184,128]{1,0:T(8,128)(2,1)S(1)}, s16[1184,128]{1,0:T(8,128)(2,1)S(1)}, u32[]{:S(2)}, u32[]{:S(2)}) collective-permute-start(s16[1184,128]{1,0:T(8,128)(2,1)S(1)} %get-tuple-element.213), channel_id=1, source_target_pairs={{0,4},{2,6},{4,0},{6,2},{8,12},{10,14},{12,8},{14,10},{16,20},{18,... | collective-permute-start | bytes 909320 | tf_op jit(solution)/shard_map/ppermute | solution.py:564
  326.7 11.2 %collective-permute-start.43 = (s16[2,1184,128]{2,1,0:T(8,128)(2,1)S(1)}, s16[2,1184,128]{2,1,0:T(8,128)(2,1)S(1)}, u32[]{:S(2)}, u32[]{:S(2)}) collective-permute-start(s16[2,1184,128]{2,1,0:T(8,128)(2,1)S(1)} %get-tuple-element.214), channel_id=1, source_target_pairs={{0,4},{2,6},{4,0},{6,2},{8,12},{10,14},{12,8},{14,10},{16,20},{18,... | collective-permute-start | bytes 1818632 | tf_op jit(solution)/shard_map/ppermute | solution.py:564
  327.7 12.7 %collective-permute-start.44 = (s16[2,1184,128]{2,1,0:T(8,128)(2,1)S(1)}, s16[2,1184,128]{2,1,0:T(8,128)(2,1)S(1)}, u32[]{:S(2)}, u32[]{:S(2)}) collective-permute-start(s16[2,1184,128]{2,1,0:T(8,128)(2,1)S(1)} %get-tuple-element.216), channel_id=1, source_target_pairs={{0,2},{2,0},{4,6},{6,4},{8,10},{10,8},{12,14},{14,12},{16,18},{18,... | collective-permute-start | bytes 1818632 | tf_op jit(solution)/shard_map/ppermute | solution.py:564
  330.0 21.3 %collective-permute-start.48 = (s16[2,1184,128]{2,1,0:T(8,128)(2,1)S(1)}, s16[2,1184,128]{2,1,0:T(8,128)(2,1)S(1)}, u32[]{:S(2)}, u32[]{:S(2)}) collective-permute-start(s16[2,1184,128]{2,1,0:T(8,128)(2,1)S(1)} %add_line.5), channel_id=1, source_target_pairs={{0,16},{2,18},{4,20},{6,22},{8,24},{10,26},{12,28},{14,30},{16,0},... | collective-permute-start | bytes 1818632 | tf_op jit(solution)/shard_map/ppermute | solution.py:564
  331.5 19.8 %collective-permute-start.47 = (s16[2,1184,128]{2,1,0:T(8,128)(2,1)S(1)}, s16[2,1184,128]{2,1,0:T(8,128)(2,1)S(1)}, u32[]{:S(2)}, u32[]{:S(2)}) collective-permute-start(s16[2,1184,128]{2,1,0:T(8,128)(2,1)S(1)} %add_line.4), channel_id=1, source_target_pairs={{0,8},{2,10},{4,12},{6,14},{8,0},{10,2},{12,4},{14,6},{16,24},{18,... | collective-permute-start | bytes 1818632 | tf_op jit(solution)/shard_map/ppermute | solution.py:564
  340.5 33.2 %copy-start.16 = (f32[24,96,96]{2,1,0:T(8,128)S(1)}, f32[24,96,96]{2,1,0:T(8,128)}, u32[]{:S(2)}) copy-start(f32[24,96,96]{2,1,0:T(8,128)} %right_ref.1) | copy-start | bytes 2654212
  341.8 31.9 %copy-start.8 = (f32[24,96,96]{2,1,0:T(8,128)S(1)}, f32[24,96,96]{2,1,0:T(8,128)}, u32[]{:S(2)}) copy-start(f32[24,96,96]{2,1,0:T(8,128)} %block_ref.1) | copy-start | bytes 2654212
  341.8 31.8 %copy-start.14 = (f32[48,2,768]{2,1,0:T(2,128)S(1)}, f32[48,2,768]{2,1,0:T(2,128)}, u32[]{:S(2)}) copy-start(f32[48,2,768]{2,1,0:T(2,128)} %io_ref.3) | copy-start | bytes 884740
  341.8 31.8 %copy-start.15 = (f32[24,96,96]{2,1,0:T(8,128)S(1)}, f32[24,96,96]{2,1,0:T(8,128)}, u32[]{:S(2)}) copy-start(f32[24,96,96]{2,1,0:T(8,128)} %left_ref.1) | copy-start | bytes 2654212
  341.9 9.5 %collective-permute-start.45 = (s16[1184,128]{1,0:T(8,128)(2,1)S(1)}, s16[1184,128]{1,0:T(8,128)(2,1)S(1)}, u32[]{:S(2)}, u32[]{:S(2)}) collective-permute-start(s16[1184,128]{1,0:T(8,128)(2,1)S(1)} %get-tuple-element.218), channel_id=1, source_target_pairs={{0,2},{2,0},{4,6},{6,4},{8,10},{10,8},{12,14},{14,12},{16,18},{18,... | collective-permute-start | bytes 909320 | tf_op jit(solution)/shard_map/ppermute | solution.py:564
  343.4 7.9 %collective-permute-start.46 = (s16[1184,128]{1,0:T(8,128)(2,1)S(1)}, s16[1184,128]{1,0:T(8,128)(2,1)S(1)}, u32[]{:S(2)}, u32[]{:S(2)}) collective-permute-start(s16[1184,128]{1,0:T(8,128)(2,1)S(1)} %get-tuple-element.220), channel_id=1, source_target_pairs={{0,4},{2,6},{4,0},{6,2},{8,12},{10,14},{12,8},{14,10},{16,20},{18,... | collective-permute-start | bytes 909320 | tf_op jit(solution)/shard_map/ppermute | solution.py:564
  352.3 1.3 collective-permute-start.49
  353.7 4.4 %collective-permute-start.50 = (f32[24,768]{1,0:T(8,128)S(1)}, f32[24,768]{1,0:T(8,128)S(1)}, u32[]{:S(2)}, u32[]{:S(2)}) collective-permute-start(f32[24,768]{1,0:T(8,128)S(1)} %add.362), channel_id=1, source_target_pairs={{0,2},{2,0},{4,6},{6,4},{8,10},{10,8},{12,14},{14,12},{16,18},{18,... | collective-permute-start | bytes 221192 | tf_op jit(solution)/shard_map/ppermute | solution.py:564
  358.1 4.4 %collective-permute-start.51 = (f32[24,768]{1,0:T(8,128)S(1)}, f32[24,768]{1,0:T(8,128)S(1)}, u32[]{:S(2)}, u32[]{:S(2)}) collective-permute-start(f32[24,768]{1,0:T(8,128)S(1)} %add.363), channel_id=1, source_target_pairs={{0,4},{2,6},{4,0},{6,2},{8,12},{10,14},{12,8},{14,10},{16,20},{18,... | collective-permute-start | bytes 221192 | tf_op jit(solution)/shard_map/ppermute | solution.py:564
  362.5 4.4 %collective-permute-start.52 = (f32[24,768]{1,0:T(8,128)S(1)}, f32[24,768]{1,0:T(8,128)S(1)}, u32[]{:S(2)}, u32[]{:S(2)}) collective-permute-start(f32[24,768]{1,0:T(8,128)S(1)} %add.364), channel_id=1, source_target_pairs={{0,8},{2,10},{4,12},{6,14},{8,0},{10,2},{12,4},{14,6},{16,24},{18,... | collective-permute-start | bytes 221192 | tf_op jit(solution)/shard_map/ppermute | solution.py:564
  367.0 6.1 %collective-permute-start.53 = (f32[24,768]{1,0:T(8,128)S(1)}, f32[24,768]{1,0:T(8,128)S(1)}, u32[]{:S(2)}, u32[]{:S(2)}) collective-permute-start(f32[24,768]{1,0:T(8,128)S(1)} %add.365), channel_id=1, source_target_pairs={{0,16},{2,18},{4,20},{6,22},{8,24},{10,26},{12,28},{14,30},{16,0},... | collective-permute-start | bytes 221192 | tf_op jit(solution)/shard_map/ppermute | solution.py:564
  (21 other events, 255.3 us)
